TPU v7x, 32 devices: a whole 2x2x4 slice. The times are simulated.
32 devices in a mesh: dp: 8 (over y, x, core), seq: 4 (over z).
Axes of the slice: x: 2, y: 2, z: 4, core: 2. Of those that a mesh axis runs over, the one named last changes fastest.
Arguments:
- text: bfloat16 [64, 128, 768], P('dp', 'seq'), may hold values from -6 to 6
- image: bfloat16 [64, 128, 1024], P('dp', 'seq'), may hold values from -6 to 6
- text_len: int32 [64], P('dp'), may hold values from 72 to 128, as said below
- region_count: int32 [64], P('dp'), may hold values from 10 to 100, as said below
- text_cot: bfloat16 [64, 128, 768], P('dp', 'seq'), may hold values from -8 to 8
- image_cot: bfloat16 [64, 128, 1024], P('dp', 'seq'), may hold values from -8 to 8
- selfproject: bfloat16 [768, 3, 768], P('dp'), may hold values from -0.21875 to 0.21875
- selfbiases: bfloat16 [2, 768], P(None, 'dp'), may hold values from -1.25 to 1.25
- selfoutput: bfloat16 [768, 768], P('dp'), may hold values from -0.875 to 0.875
- textcoproject: bfloat16 [768, 3, 1024], P('dp'), may hold values from -0.21875 to 0.21875
- textcobiases: bfloat16 [2, 1024], P(None, 'dp'), may hold values from -1.25 to 1.25
- imagecoproject: bfloat16 [1024, 3, 1024], P('dp'), may hold values from -0.1875 to 0.1875
- imagecobiases: bfloat16 [2, 1024], P(None, 'dp'), may hold values from -1.25 to 1.25
- textcooutput: bfloat16 [1024, 768], P('dp'), may hold values from -0.5 to 0.5
- imagecooutput: bfloat16 [1024, 1024], P('dp'), may hold values from -0.75 to 0.75
- textffinner: bfloat16 [768, 3072], P('dp'), may hold values from -0.21875 to 0.21875
- textffinbias: bfloat16 [3072], P('dp'), may hold values from -1.25 to 1.25
- textffouter: bfloat16 [3072, 768], P('dp'), may hold values from -0.109375 to 0.109375
- imageffinner: bfloat16 [1024, 1024], P('dp'), may hold values from -0.1875 to 0.1875
- imageffinbias: bfloat16 [1024], P('dp'), may hold values from -1.25 to 1.25
- imageffouter: bfloat16 [1024, 1024], P('dp'), may hold values from -0.1875 to 0.1875
- textgains: bfloat16 [3, 768], P(None, 'dp'), may hold values from 0.5 to 1.5
- textshifts: bfloat16 [3, 768], P(None, 'dp'), may hold values from -1.25 to 1.25
- textbiases: bfloat16 [3, 768], P(None, 'dp'), may hold values from -1.25 to 1.25
- imagegains: bfloat16 [2, 1024], P(None, 'dp'), may hold values from 0.5 to 1.5
- imageshifts: bfloat16 [2, 1024], P(None, 'dp'), may hold values from -1.25 to 1.25
- imagebiases: bfloat16 [2, 1024], P(None, 'dp'), may hold values from -1.25 to 1.25
Outputs:
- text_out: bfloat16 [64, 128, 768], P('dp', 'seq')
- image_out: bfloat16 [64, 128, 1024], P('dp', 'seq')
- text_grad: bfloat16 [64, 128, 768], P('dp', 'seq')
- image_grad: bfloat16 [64, 128, 1024], P('dp', 'seq')
- grad_selfproject: float32 [768, 3, 768], P('dp')
- grad_selfbiases: float32 [2, 768], P(None, 'dp')
- grad_selfoutput: float32 [768, 768], P('dp')
- grad_textcoproject: float32 [768, 3, 1024], P('dp')
- grad_textcobiases: float32 [2, 1024], P(None, 'dp')
- grad_imagecoproject: float32 [1024, 3, 1024], P('dp')
- grad_imagecobiases: float32 [2, 1024], P(None, 'dp')
- grad_textcooutput: float32 [1024, 768], P('dp')
- grad_imagecooutput: float32 [1024, 1024], P('dp')
- grad_textffinner: float32 [768, 3072], P('dp')
- grad_textffinbias: float32 [3072], P('dp')
- grad_textffouter: float32 [3072, 768], P('dp')
- grad_imageffinner: float32 [1024, 1024], P('dp')
- grad_imageffinbias: float32 [1024], P('dp')
- grad_imageffouter: float32 [1024, 1024], P('dp')
- grad_textgains: float32 [3, 768], P(None, 'dp')
- grad_textshifts: float32 [3, 768], P(None, 'dp')
- grad_textbiases: float32 [3, 768], P(None, 'dp')
- grad_imagegains: float32 [2, 1024], P(None, 'dp')
- grad_imageshifts: float32 [2, 1024], P(None, 'dp')
- grad_imagebiases: float32 [2, 1024], P(None, 'dp')
Inputs may be any that keep to these rules, and one draw needn't show every extreme that they name: Each pair's caption fills its first text_len slots of 128; in every aligned block of 8 pairs (those of one index of dp) one caption fills all 128 slots. Each pair's regions fill its first region_count slots of 128; in every aligned block of 8 pairs one image has 100 regions.
All inputs are finite; a program needn't handle non-finite values.
Results may differ from a plain program's by a relative error of at most 0.023.
Values may be sent and summed in bfloat16 or wider, within the bound.
A program may use at most 256 MiB of HBM per device.

v0:
```python
import jax
import jax.numpy as jnp
from jax import lax
from jax.sharding import PartitionSpec as P

HT = 12
HC = 8
MB = 2


EPSILON = 1e-05
NEG_FILL = -1e30


def layer_norm(hidden, factor, offset):
    centre = hidden - jnp.mean(hidden, axis=-1, keepdims=True)
    spread = jnp.mean(centre * centre, axis=-1, keepdims=True)
    return centre * lax.rsqrt(spread + EPSILON) * factor + offset


def norm_back(hidden, factor, offset, upstream):
    outcome, pullback = jax.vjp(layer_norm, hidden, factor, offset)
    return pullback(upstream)


def gelu_exact(hidden):
    return jax.nn.gelu(hidden, approximate=False)


def gelu_back(hidden, upstream):
    outcome, pullback = jax.vjp(gelu_exact, hidden)
    return pullback(upstream)[0]


def linear(inputs, weight):
    return jnp.einsum("pte,ef->ptf", inputs, weight, preferred_element_type=jnp.float32)


def linear_weight(inputs, gradient):
    return jnp.einsum("pte,ptf->ef", inputs, gradient, preferred_element_type=jnp.float32)


def linear_input(gradient, weight):
    return jnp.einsum("ptf,ef->pte", gradient, weight, preferred_element_type=jnp.float32)


def row_total(gradient):
    return jnp.sum(gradient, axis=(0, 1), dtype=jnp.float32)


def project(inputs, weight, biases):
    bias_rows = biases.astype(jnp.float32)
    stacked = jnp.stack([bias_rows[0], jnp.zeros_like(bias_rows[0]), bias_rows[1]])
    triple = jnp.einsum("pte,ekf->ptkf", inputs, weight, preferred_element_type=jnp.float32)
    return (triple + stacked).astype(jnp.bfloat16)


def project_back(inputs, gradient, weight):
    weight_grad = jnp.einsum("pte,ptkf->ekf", inputs, gradient, preferred_element_type=jnp.float32)
    totals = row_total(gradient)
    input_grad = jnp.einsum("ptkf,ekf->pte", gradient, weight, preferred_element_type=jnp.float32)
    return (weight_grad, jnp.stack([totals[0], totals[2]]), input_grad)


def split_heads(values, head_count):
    return values.reshape(
        values.shape[0], values.shape[1], head_count, values.shape[2] // head_count
    )


def score_table(queries, keyvals, keymask, head_count):
    query_heads = split_heads(queries, head_count)
    key_heads = split_heads(keyvals[:, :, 0], head_count)
    shrink = query_heads.shape[-1] ** (-0.5)
    scores = (
        jnp.einsum("pthd,pshd->phts", query_heads, key_heads, preferred_element_type=jnp.float32)
        * shrink
    )
    scores = jnp.where(keymask[:, None, None, :], scores, NEG_FILL)
    return (scores, query_heads, key_heads, shrink)


def attend(queries, keyvals, keymask, head_count):
    scores, query_heads, key_heads, shrink = score_table(queries, keyvals, keymask, head_count)
    highest = jnp.max(scores, axis=-1, keepdims=True)
    powers = jnp.exp(scores - highest)
    totals = jnp.sum(powers, axis=-1, keepdims=True)
    prob_table = (powers / totals).astype(jnp.bfloat16)
    value_heads = split_heads(keyvals[:, :, 1], head_count)
    mixture = jnp.einsum(
        "phts,pshd->pthd", prob_table, value_heads, preferred_element_type=jnp.float32
    )
    return (mixture.reshape(queries.shape).astype(jnp.bfloat16), highest + jnp.log(totals))


def attend_back(upstream, queries, keyvals, keymask, logsum, head_count):
    scores, query_heads, key_heads, shrink = score_table(queries, keyvals, keymask, head_count)
    prob_table = jnp.exp(scores - logsum)
    value_heads = split_heads(keyvals[:, :, 1], head_count)
    upper_heads = split_heads(upstream, head_count)
    value_grad = jnp.einsum(
        "phts,pthd->pshd",
        prob_table.astype(jnp.bfloat16),
        upper_heads,
        preferred_element_type=jnp.float32,
    )
    prob_grad = jnp.einsum(
        "pthd,pshd->phts", upper_heads, value_heads, preferred_element_type=jnp.float32
    )
    score_grad = prob_table * (prob_grad - jnp.sum(prob_grad * prob_table, axis=-1, keepdims=True))
    score_grad = score_grad.astype(jnp.bfloat16)
    query_grad = (
        jnp.einsum("phts,pshd->pthd", score_grad, key_heads, preferred_element_type=jnp.float32)
        * shrink
    )
    key_grad = (
        jnp.einsum("phts,pthd->pshd", score_grad, query_heads, preferred_element_type=jnp.float32)
        * shrink
    )
    keyval_grad = jnp.stack([key_grad, value_grad], axis=2).reshape(keyvals.shape)
    return (query_grad.reshape(queries.shape), keyval_grad)


def feed_forward(inputs, weight_in, bias_in, weight_out, bias_out):
    inner_sum = linear(inputs, weight_in) + bias_in.astype(jnp.float32)
    active = gelu_exact(inner_sum).astype(jnp.bfloat16)
    totals = inputs.astype(jnp.float32) + linear(active, weight_out) + bias_out
    return (inner_sum, active, totals)


def feed_back(upstream, inputs, inner_sum, active, totals, factor, offset, weight_in, weight_out):
    sum_grad, factor_grad, offset_grad = norm_back(totals, factor, offset, upstream)
    branch_grad = sum_grad.astype(jnp.bfloat16)
    outer_grad = linear_weight(active, branch_grad)
    outbias_grad = row_total(branch_grad)
    active_grad = linear_input(branch_grad, weight_out)
    inner_grad = gelu_back(inner_sum, active_grad).astype(jnp.bfloat16)
    weightin_grad = linear_weight(inputs, inner_grad)
    inbias_grad = row_total(inner_grad)
    input_grad = linear_input(inner_grad, weight_in) + sum_grad
    return (
        input_grad,
        weightin_grad,
        inbias_grad,
        outer_grad,
        outbias_grad,
        factor_grad,
        offset_grad,
    )


def micro_step(
    fetched, text, image, text_len, region_count, text_cot, image_cot, caption_slots, region_slots
):
    (
        selfproject,
        selfbiases,
        selfoutput,
        textcoproject,
        textcobiases,
        imagecoproject,
        imagecobiases,
        textcooutput,
        imagecooutput,
        textffinner,
        textffinbias,
        textffouter,
        imageffinner,
        imageffinbias,
        imageffouter,
        textgains,
        textshifts,
        textbiases,
        imagegains,
        imageshifts,
        imagebiases,
    ) = fetched
    text_factor = textgains.astype(jnp.float32)
    text_offset = textshifts.astype(jnp.float32)
    text_bias = textbiases.astype(jnp.float32)
    image_factor = imagegains.astype(jnp.float32)
    image_offset = imageshifts.astype(jnp.float32)
    image_bias = imagebiases.astype(jnp.float32)
    text_mask = jnp.arange(caption_slots)[None, :] < text_len[:, None]
    region_mask = jnp.arange(region_slots)[None, :] < region_count[:, None]
    self_triple = project(text, selfproject, selfbiases)
    self_keys = lax.all_gather(self_triple[:, :, 1:], "seq", axis=1, tiled=True)
    self_mixed, self_logsum = attend(self_triple[:, :, 0], self_keys, text_mask, HT)
    self_sum = text.astype(jnp.float32) + linear(self_mixed, selfoutput) + text_bias[0]
    text_one = layer_norm(self_sum, text_factor[0], text_offset[0]).astype(jnp.bfloat16)
    text_triple = project(text_one, textcoproject, textcobiases)
    image_triple = project(image, imagecoproject, imagecobiases)
    text_keys, image_keys = (
        lax.all_gather(text_triple[:, :, 1:], "seq", axis=1, tiled=True),
        lax.all_gather(image_triple[:, :, 1:], "seq", axis=1, tiled=True),
    )
    text_mixed, text_logsum = attend(text_triple[:, :, 0], image_keys, region_mask, HC)
    image_mixed, image_logsum = attend(image_triple[:, :, 0], text_keys, text_mask, HC)
    text_sum = text_one.astype(jnp.float32) + linear(text_mixed, textcooutput) + text_bias[1]
    text_two = layer_norm(text_sum, text_factor[1], text_offset[1]).astype(jnp.bfloat16)
    image_sum = image.astype(jnp.float32) + linear(image_mixed, imagecooutput) + image_bias[0]
    image_two = layer_norm(image_sum, image_factor[0], image_offset[0]).astype(jnp.bfloat16)
    text_inner, text_active, text_total = feed_forward(
        text_two, textffinner, textffinbias, textffouter, text_bias[2]
    )
    text_three = layer_norm(text_total, text_factor[2], text_offset[2]).astype(jnp.bfloat16)
    image_inner, image_active, image_total = feed_forward(
        image_two, imageffinner, imageffinbias, imageffouter, image_bias[1]
    )
    image_three = layer_norm(image_total, image_factor[1], image_offset[1]).astype(jnp.bfloat16)
    (
        text_twograd,
        textin_grad,
        textinb_grad,
        textout_grad,
        textoutb_grad,
        factor_tthree,
        offset_tthree,
    ) = feed_back(
        text_cot.astype(jnp.float32),
        text_two,
        text_inner,
        text_active,
        text_total,
        text_factor[2],
        text_offset[2],
        textffinner,
        textffouter,
    )
    (
        image_twograd,
        imagein_grad,
        imageinb_grad,
        imageout_grad,
        imageoutb_grad,
        factor_itwo,
        offset_itwo,
    ) = feed_back(
        image_cot.astype(jnp.float32),
        image_two,
        image_inner,
        image_active,
        image_total,
        image_factor[1],
        image_offset[1],
        imageffinner,
        imageffouter,
    )
    textsum_grad, factor_ttwo, offset_ttwo = norm_back(
        text_sum, text_factor[1], text_offset[1], text_twograd
    )
    textbranch_grad = textsum_grad.astype(jnp.bfloat16)
    textco_outgrad = linear_weight(text_mixed, textbranch_grad)
    textco_biasgrad = row_total(textbranch_grad)
    textmix_grad = linear_input(textbranch_grad, textcooutput).astype(jnp.bfloat16)
    imagesum_grad, factor_ione, offset_ione = norm_back(
        image_sum, image_factor[0], image_offset[0], image_twograd
    )
    imagebranch_grad = imagesum_grad.astype(jnp.bfloat16)
    imageco_outgrad = linear_weight(image_mixed, imagebranch_grad)
    imageco_biasgrad = row_total(imagebranch_grad)
    imagemix_grad = linear_input(imagebranch_grad, imagecooutput).astype(jnp.bfloat16)
    textquery_grad, imagekv_part = attend_back(
        textmix_grad, text_triple[:, :, 0], image_keys, region_mask, text_logsum, HC
    )
    imagequery_grad, textkv_part = attend_back(
        imagemix_grad, image_triple[:, :, 0], text_keys, text_mask, image_logsum, HC
    )
    textkv_grad, imagekv_grad = (
        lax.psum_scatter(
            textkv_part.astype(jnp.bfloat16), "seq", scatter_dimension=1, tiled=True
        ).astype(jnp.float32),
        lax.psum_scatter(
            imagekv_part.astype(jnp.bfloat16), "seq", scatter_dimension=1, tiled=True
        ).astype(jnp.float32),
    )
    texttriple_grad = jnp.concatenate(
        [textquery_grad[:, :, None].astype(jnp.bfloat16), textkv_grad.astype(jnp.bfloat16)], axis=2
    )
    imagetriple_grad = jnp.concatenate(
        [imagequery_grad[:, :, None].astype(jnp.bfloat16), imagekv_grad.astype(jnp.bfloat16)],
        axis=2,
    )
    textco_projgrad, textco_qvgrad, textone_grad = project_back(
        text_one, texttriple_grad, textcoproject
    )
    textone_grad = textone_grad + textsum_grad
    imageco_projgrad, imageco_qvgrad, image_ingrad = project_back(
        image, imagetriple_grad, imagecoproject
    )
    image_ingrad = image_ingrad + imagesum_grad
    selfsum_grad, factor_tone, offset_tone = norm_back(
        self_sum, text_factor[0], text_offset[0], textone_grad
    )
    selfbranch_grad = selfsum_grad.astype(jnp.bfloat16)
    selfout_grad = linear_weight(self_mixed, selfbranch_grad)
    selfbias_grad = row_total(selfbranch_grad)
    selfmix_grad = linear_input(selfbranch_grad, selfoutput).astype(jnp.bfloat16)
    selfquery_grad, selfkv_part = attend_back(
        selfmix_grad, self_triple[:, :, 0], self_keys, text_mask, self_logsum, HT
    )
    selfkv_grad = lax.psum_scatter(
        selfkv_part.astype(jnp.bfloat16), "seq", scatter_dimension=1, tiled=True
    )
    selftriple_grad = jnp.concatenate(
        [selfquery_grad[:, :, None].astype(jnp.bfloat16), selfkv_grad], axis=2
    )
    selfproj_grad, selfqv_grad, text_ingrad = project_back(text, selftriple_grad, selfproject)
    text_ingrad = text_ingrad + selfsum_grad
    gradients = (
        selfproj_grad,
        selfqv_grad,
        selfout_grad,
        textco_projgrad,
        textco_qvgrad,
        imageco_projgrad,
        imageco_qvgrad,
        textco_outgrad,
        imageco_outgrad,
        textin_grad,
        textinb_grad,
        textout_grad,
        imagein_grad,
        imageinb_grad,
        imageout_grad,
        jnp.stack([factor_tone, factor_ttwo, factor_tthree]),
        jnp.stack([offset_tone, offset_ttwo, offset_tthree]),
        jnp.stack([selfbias_grad, textco_biasgrad, textoutb_grad]),
        jnp.stack([factor_ione, factor_itwo]),
        jnp.stack([offset_ione, offset_itwo]),
        jnp.stack([imageco_biasgrad, imageoutb_grad]),
    )
    outputs = (
        text_three,
        image_three,
        text_ingrad.astype(jnp.bfloat16),
        image_ingrad.astype(jnp.bfloat16),
    )
    return (outputs, gradients)


def local(
    text,
    image,
    text_len,
    region_count,
    text_cot,
    image_cot,
    selfproject,
    selfbiases,
    selfoutput,
    textcoproject,
    textcobiases,
    imagecoproject,
    imagecobiases,
    textcooutput,
    imagecooutput,
    textffinner,
    textffinbias,
    textffouter,
    imageffinner,
    imageffinbias,
    imageffouter,
    textgains,
    textshifts,
    textbiases,
    imagegains,
    imageshifts,
    imagebiases,
):
    seq_count = lax.axis_size("seq")
    micro_pairs = text.shape[0] // MB
    shards = (
        selfproject,
        selfbiases,
        selfoutput,
        textcoproject,
        textcobiases,
        imagecoproject,
        imagecobiases,
        textcooutput,
        imagecooutput,
        textffinner,
        textffinbias,
        textffouter,
        imageffinner,
        imageffinbias,
        imageffouter,
        textgains,
        textshifts,
        textbiases,
        imagegains,
        imageshifts,
        imagebiases,
    )
    accumulated = None
    text_rows = []
    image_rows = []
    textgrad_rows = []
    imagegrad_rows = []
    for micro_index in range(MB):
        fetched = (
            lax.all_gather(shards[0], "dp", axis=0, tiled=True),
            lax.all_gather(shards[1], "dp", axis=1, tiled=True),
            lax.all_gather(shards[2], "dp", axis=0, tiled=True),
            lax.all_gather(shards[3], "dp", axis=0, tiled=True),
            lax.all_gather(shards[4], "dp", axis=1, tiled=True),
            lax.all_gather(shards[5], "dp", axis=0, tiled=True),
            lax.all_gather(shards[6], "dp", axis=1, tiled=True),
            lax.all_gather(shards[7], "dp", axis=0, tiled=True),
            lax.all_gather(shards[8], "dp", axis=0, tiled=True),
            lax.all_gather(shards[9], "dp", axis=0, tiled=True),
            lax.all_gather(shards[10], "dp", axis=0, tiled=True),
            lax.all_gather(shards[11], "dp", axis=0, tiled=True),
            lax.all_gather(shards[12], "dp", axis=0, tiled=True),
            lax.all_gather(shards[13], "dp", axis=0, tiled=True),
            lax.all_gather(shards[14], "dp", axis=0, tiled=True),
            lax.all_gather(shards[15], "dp", axis=1, tiled=True),
            lax.all_gather(shards[16], "dp", axis=1, tiled=True),
            lax.all_gather(shards[17], "dp", axis=1, tiled=True),
            lax.all_gather(shards[18], "dp", axis=1, tiled=True),
            lax.all_gather(shards[19], "dp", axis=1, tiled=True),
            lax.all_gather(shards[20], "dp", axis=1, tiled=True),
        )
        begin_row = micro_index * micro_pairs
        end_row = begin_row + micro_pairs
        outputs, gradients = micro_step(
            fetched,
            text[begin_row:end_row],
            image[begin_row:end_row],
            text_len[begin_row:end_row],
            region_count[begin_row:end_row],
            text_cot[begin_row:end_row],
            image_cot[begin_row:end_row],
            text.shape[1] * seq_count,
            image.shape[1] * seq_count,
        )
        text_rows.append(outputs[0])
        image_rows.append(outputs[1])
        textgrad_rows.append(outputs[2])
        imagegrad_rows.append(outputs[3])
        pieces = (
            lax.psum_scatter(gradients[0], "dp", scatter_dimension=0, tiled=True),
            lax.psum_scatter(gradients[1], "dp", scatter_dimension=1, tiled=True),
            lax.psum_scatter(gradients[2], "dp", scatter_dimension=0, tiled=True),
            lax.psum_scatter(gradients[3], "dp", scatter_dimension=0, tiled=True),
            lax.psum_scatter(gradients[4], "dp", scatter_dimension=1, tiled=True),
            lax.psum_scatter(gradients[5], "dp", scatter_dimension=0, tiled=True),
            lax.psum_scatter(gradients[6], "dp", scatter_dimension=1, tiled=True),
            lax.psum_scatter(gradients[7], "dp", scatter_dimension=0, tiled=True),
            lax.psum_scatter(gradients[8], "dp", scatter_dimension=0, tiled=True),
            lax.psum_scatter(gradients[9], "dp", scatter_dimension=0, tiled=True),
            lax.psum_scatter(gradients[10], "dp", scatter_dimension=0, tiled=True),
            lax.psum_scatter(gradients[11], "dp", scatter_dimension=0, tiled=True),
            lax.psum_scatter(gradients[12], "dp", scatter_dimension=0, tiled=True),
            lax.psum_scatter(gradients[13], "dp", scatter_dimension=0, tiled=True),
            lax.psum_scatter(gradients[14], "dp", scatter_dimension=0, tiled=True),
            lax.psum_scatter(gradients[15], "dp", scatter_dimension=1, tiled=True),
            lax.psum_scatter(gradients[16], "dp", scatter_dimension=1, tiled=True),
            lax.psum_scatter(gradients[17], "dp", scatter_dimension=1, tiled=True),
            lax.psum_scatter(gradients[18], "dp", scatter_dimension=1, tiled=True),
            lax.psum_scatter(gradients[19], "dp", scatter_dimension=1, tiled=True),
            lax.psum_scatter(gradients[20], "dp", scatter_dimension=1, tiled=True),
        )
        accumulated = pieces if accumulated is None else jax.tree.map(jnp.add, accumulated, pieces)
    summed = (
        lax.psum(accumulated[0].astype(jnp.bfloat16), "seq").astype(jnp.float32),
        lax.psum(accumulated[1].astype(jnp.bfloat16), "seq").astype(jnp.float32),
        lax.psum(accumulated[2].astype(jnp.bfloat16), "seq").astype(jnp.float32),
        lax.psum(accumulated[3].astype(jnp.bfloat16), "seq").astype(jnp.float32),
        lax.psum(accumulated[4].astype(jnp.bfloat16), "seq").astype(jnp.float32),
        lax.psum(accumulated[5].astype(jnp.bfloat16), "seq").astype(jnp.float32),
        lax.psum(accumulated[6].astype(jnp.bfloat16), "seq").astype(jnp.float32),
        lax.psum(accumulated[7].astype(jnp.bfloat16), "seq").astype(jnp.float32),
        lax.psum(accumulated[8].astype(jnp.bfloat16), "seq").astype(jnp.float32),
        lax.psum(accumulated[9].astype(jnp.bfloat16), "seq").astype(jnp.float32),
        lax.psum(accumulated[10].astype(jnp.bfloat16), "seq").astype(jnp.float32),
        lax.psum(accumulated[11].astype(jnp.bfloat16), "seq").astype(jnp.float32),
        lax.psum(accumulated[12].astype(jnp.bfloat16), "seq").astype(jnp.float32),
        lax.psum(accumulated[13].astype(jnp.bfloat16), "seq").astype(jnp.float32),
        lax.psum(accumulated[14].astype(jnp.bfloat16), "seq").astype(jnp.float32),
        lax.psum(accumulated[15].astype(jnp.bfloat16), "seq").astype(jnp.float32),
        lax.psum(accumulated[16].astype(jnp.bfloat16), "seq").astype(jnp.float32),
        lax.psum(accumulated[17].astype(jnp.bfloat16), "seq").astype(jnp.float32),
        lax.psum(accumulated[18].astype(jnp.bfloat16), "seq").astype(jnp.float32),
        lax.psum(accumulated[19].astype(jnp.bfloat16), "seq").astype(jnp.float32),
        lax.psum(accumulated[20].astype(jnp.bfloat16), "seq").astype(jnp.float32),
    )
    text_out = jnp.concatenate(text_rows, axis=0)
    image_out = jnp.concatenate(image_rows, axis=0)
    text_grad = jnp.concatenate(textgrad_rows, axis=0)
    image_grad = jnp.concatenate(imagegrad_rows, axis=0)
    return (text_out, image_out, text_grad, image_grad) + tuple(summed)


def solution(mesh):
    in_specs = (
        P("dp", "seq", None),
        P("dp", "seq", None),
        P("dp"),
        P("dp"),
        P("dp", "seq", None),
        P("dp", "seq", None),
        P("dp", None, None),
        P(None, "dp"),
        P("dp", None),
        P("dp", None, None),
        P(None, "dp"),
        P("dp", None, None),
        P(None, "dp"),
        P("dp", None),
        P("dp", None),
        P("dp", None),
        P("dp"),
        P("dp", None),
        P("dp", None),
        P("dp"),
        P("dp", None),
        P(None, "dp"),
        P(None, "dp"),
        P(None, "dp"),
        P(None, "dp"),
        P(None, "dp"),
        P(None, "dp"),
    )
    out_specs = (
        P("dp", "seq", None),
        P("dp", "seq", None),
        P("dp", "seq", None),
        P("dp", "seq", None),
        P("dp", None, None),
        P(None, "dp"),
        P("dp", None),
        P("dp", None, None),
        P(None, "dp"),
        P("dp", None, None),
        P(None, "dp"),
        P("dp", None),
        P("dp", None),
        P("dp", None),
        P("dp"),
        P("dp", None),
        P("dp", None),
        P("dp"),
        P("dp", None),
        P(None, "dp"),
        P(None, "dp"),
        P(None, "dp"),
        P(None, "dp"),
        P(None, "dp"),
        P(None, "dp"),
    )
    return jax.shard_map(local, mesh=mesh, in_specs=in_specs, out_specs=out_specs, check_vma=False)
```

profile of v0, /device:TPU:0, one launch (start us, length us, event | category | flops | bytes accessed | tf_op | source)
XLA Modules:
  0.0 2086.9 jit_solution(11755097951213884500)
XLA Ops:
  8.0 10.3 all-gather
  18.5 28.1 %all-gather.23.cloned.1.call-done = bf16[768,3,768]{2,0,1:T(8,128)(2,1)} async-done(((bf16[96,3,768]{2,0,1:T(8,128)(2,1)}), bf16[768,3,768]{2,0,1:T(8,128)(2,1)}) %all-gather.23.cloned.1.call-update) | async-done | bytes 3538960 | tf_op jit(solution)/shard_map/all_gather | solution.py:403
  55.6 8.8 all-gather.1
  72.6 8.8 all-gather.3
  89.3 8.7 all_gather.110
  104.3 21.3 %all-gather.25.cloned.1.call-done = bf16[4,128,2,768]{3,1,2,0:T(8,128)(2,1)} async-done(((bf16[4,32,2,768]{3,1,2,0:T(8,128)(2,1)}), bf16[4,128,2,768]{3,1,2,0:T(8,128)(2,1)}) %all-gather.25.cloned.1.call-update) | async-done | bytes 1572880 | tf_op jit(solution)/shard_map/all_gather | solution.py:187
  132.2 18.1 all-gather.27.cloned.1.call-done
  153.8 37.2 %all-gather.33.cloned.1.call-done = bf16[768,3,1024]{2,0,1:T(8,128)(2,1)} async-done(((bf16[96,3,1024]{2,0,1:T(8,128)(2,1)}), bf16[768,3,1024]{2,0,1:T(8,128)(2,1)}) %all-gather.33.cloned.1.call-update) | async-done | bytes 4718608 | tf_op jit(solution)/shard_map/all_gather | solution.py:406
  203.5 34.9 %all-gather.29.cloned.1.call-done = bf16[1024,3,1024]{2,0,1:T(8,128)(2,1)} async-done(((bf16[128,3,1024]{2,0,1:T(8,128)(2,1)}), bf16[1024,3,1024]{2,0,1:T(8,128)(2,1)}) %all-gather.29.cloned.1.call-update) | async-done | bytes 6291472 | tf_op jit(solution)/shard_map/all_gather | solution.py:408
  249.7 8.7 all_gather.122
  266.8 8.7 all_gather.124
  291.2 23.8 %all-gather.47.cloned.1.call-done = bf16[1024,1024]{1,0:T(8,128)(2,1)} async-done(((bf16[128,1024]{1,0:T(8,128)(2,1)}), bf16[1024,1024]{1,0:T(8,128)(2,1)}) %all-gather.47.cloned.1.call-update) | async-done | bytes 2097168 | tf_op jit(solution)/shard_map/all_gather | solution.py:411
  318.7 44.4 %all-gather.45.cloned.1.call-done = bf16[4,128,2,1024]{3,1,2,0:T(8,128)(2,1)} async-done(((bf16[4,32,2,1024]{3,1,2,0:T(8,128)(2,1)}), bf16[4,128,2,1024]{3,1,2,0:T(8,128)(2,1)}) %all-gather.45.cloned.1.call-update) | async-done | bytes 2097168 | tf_op jit(solution)/shard_map/all_gather | solution.py:194
  371.8 19.7 all-gather.49.cloned.1.call-done
  395.1 26.3 %all-gather.51.cloned.1.call-done = bf16[1024,1024]{1,0:T(8,128)(2,1)} async-done(((bf16[128,1024]{1,0:T(8,128)(2,1)}), bf16[1024,1024]{1,0:T(8,128)(2,1)}) %all-gather.51.cloned.1.call-update) | async-done | bytes 2097168 | tf_op jit(solution)/shard_map/all_gather | solution.py:417
  457.0 9.0 all-gather.4
  484.7 10.9 all-gather.35.cloned.1.call-done
  497.7 45.9 %all-gather.31.cloned.1.call-done = bf16[4,128,2,1024]{3,1,2,0:T(8,128)(2,1)} async-done(((bf16[4,32,2,1024]{3,1,2,0:T(8,128)(2,1)}), bf16[4,128,2,1024]{3,1,2,0:T(8,128)(2,1)}) %all-gather.31.cloned.1.call-update) | async-done | bytes 2097168 | tf_op jit(solution)/shard_map/all_gather | solution.py:195
  551.4 31.7 %all-gather.37.cloned.1.call-done = bf16[768,3072]{1,0:T(8,128)(2,1)} async-done(((bf16[96,3072]{1,0:T(8,128)(2,1)}), bf16[768,3072]{1,0:T(8,128)(2,1)}) %all-gather.37.cloned.1.call-update) | async-done | bytes 4718608 | tf_op jit(solution)/shard_map/all_gather | solution.py:412
  592.4 31.3 %all-gather.39.cloned.1.call-done = bf16[3072,768]{1,0:T(8,128)(2,1)} async-done(((bf16[384,768]{1,0:T(8,128)(2,1)}), bf16[3072,768]{1,0:T(8,128)(2,1)}) %all-gather.39.cloned.1.call-update) | async-done | bytes 4718608 | tf_op jit(solution)/shard_map/all_gather | solution.py:414
  661.6 8.2 reduce-scatter.50.cloned.1.call-done
  675.1 40.1 %reduce-scatter.46.cloned.1.call-done = bf16[4,32,2,1024]{3,1,2,0:T(8,128)(2,1)} async-done(((bf16[4,128,2,1024]{3,1,2,0:T(8,128)(2,1)}), bf16[4,32,2,1024]{3,1,2,0:T(8,128)(2,1)}) %reduce-scatter.46.cloned.1.call-update) | async-done | bytes 524304 | tf_op jit(solution)/shard_map/reduce_scatter | solution.py:270
  824.2 8.0 copy.404
  842.4 13.2 reduce-scatter.54.cloned.1.call-done
  863.1 38.1 %reduce-scatter.56.cloned.1.call-done = bf16[4,32,2,1024]{3,1,2,0:T(8,128)(2,1)} async-done(((bf16[4,128,2,1024]{3,1,2,0:T(8,128)(2,1)}), bf16[4,32,2,1024]{3,1,2,0:T(8,128)(2,1)}) %reduce-scatter.56.cloned.1.call-update) | async-done | bytes 524304 | tf_op jit(solution)/shard_map/reduce_scatter | solution.py:273
  901.2 11.9 fusion
  925.4 29.9 %reduce-scatter.74.cloned.1.call-done = f32[128,1024]{1,0:T(8,128)} async-done(((f32[1024,1024]{1,0:T(8,128)}), f32[128,1024]{1,0:T(8,128)}) %reduce-scatter.74.cloned.1.call-update) | async-done | bytes 524304 | tf_op jit(solution)/shard_map/reduce_scatter | solution.py:457
  957.1 53.2 %reduce-scatter.72.cloned.1.call-done = f32[128,1024]{1,0:T(8,128)} async-done(((f32[1024,1024]{1,0:T(8,128)}), f32[128,1024]{1,0:T(8,128)}) %reduce-scatter.72.cloned.1.call-update) | async-done | bytes 524304 | tf_op jit(solution)/shard_map/reduce_scatter | solution.py:455
  1012.0 52.9 %reduce-scatter.66.cloned.1.call-done = f32[128,1024]{1,0:T(8,128)} async-done(((f32[1024,1024]{1,0:T(8,128)}), f32[128,1024]{1,0:T(8,128)}) %reduce-scatter.66.cloned.1.call-update) | async-done | bytes 524304 | tf_op jit(solution)/shard_map/reduce_scatter | solution.py:451
  1066.7 48.1 %reduce-scatter.64.cloned.1.call-done = f32[128,768]{1,0:T(8,128)} async-done(((f32[1024,768]{1,0:T(8,128)}), f32[128,768]{1,0:T(8,128)}) %reduce-scatter.64.cloned.1.call-update) | async-done | bytes 393232 | tf_op jit(solution)/shard_map/reduce_scatter | solution.py:450
  1116.5 44.0 %reduce-scatter.58.cloned.1.call-done = f32[96,768]{1,0:T(8,128)} async-done(((f32[768,768]{1,0:T(8,128)}), f32[96,768]{1,0:T(8,128)}) %reduce-scatter.58.cloned.1.call-update) | async-done | bytes 294928 | tf_op jit(solution)/shard_map/reduce_scatter | solution.py:445
  1162.2 78.8 %reduce-scatter.68.cloned.1.call-done = f32[96,3072]{1,0:T(8,128)} async-done(((f32[768,3072]{1,0:T(8,128)}), f32[96,3072]{1,0:T(8,128)}) %reduce-scatter.68.cloned.1.call-update) | async-done | bytes 1179664 | tf_op jit(solution)/shard_map/reduce_scatter | solution.py:452
  1243.1 78.3 %reduce-scatter.70.cloned.1.call-done = f32[384,768]{1,0:T(8,128)} async-done(((f32[3072,768]{1,0:T(8,128)}), f32[384,768]{1,0:T(8,128)}) %reduce-scatter.70.cloned.1.call-update) | async-done | bytes 1179664 | tf_op jit(solution)/shard_map/reduce_scatter | solution.py:454
  1323.5 67.2 %reduce-scatter.76.cloned.1.call-done = f32[96,2304]{1,0:T(8,128)} async-done(((f32[768,2304]{1,0:T(8,128)}), f32[96,2304]{1,0:T(8,128)}) %reduce-scatter.76.cloned.1.call-update) | async-done | bytes 884752
  1392.9 77.8 %reduce-scatter.60.cloned.1.call-done = f32[96,3,1024]{2,0,1:T(8,128)} async-done(((f32[768,3,1024]{2,0,1:T(8,128)}), f32[96,3,1024]{2,0,1:T(8,128)}) %reduce-scatter.60.cloned.1.call-update) | async-done | bytes 1179664 | tf_op jit(solution)/shard_map/reduce_scatter | solution.py:446
  1472.9 93.8 %reduce-scatter.62.cloned.1.call-done = f32[128,3,1024]{0,2,1:T(8,128)} async-done(((f32[1024,3,1024]{0,2,1:T(8,128)}), f32[128,3,1024]{0,2,1:T(8,128)}) %reduce-scatter.62.cloned.1.call-update) | async-done | bytes 1572880 | tf_op jit(solution)/shard_map/reduce_scatter | solution.py:448
  1573.5 30.3 %reduce-scatter.94.cloned.1.call-done = f32[128,2]{1,0:T(8,128)} async-done(((f32[1024,2]{1,0:T(8,128)}), f32[128,2]{1,0:T(8,128)}) %reduce-scatter.94.cloned.1.call-update) | async-done | bytes 1040
  1604.6 37.2 %reduce-scatter.90.cloned.1.call-done = f32[128,2]{1,0:T(8,128)} async-done(((f32[1024,2]{1,0:T(8,128)}), f32[128,2]{1,0:T(8,128)}) %reduce-scatter.90.cloned.1.call-update) | async-done | bytes 1040
  1642.8 36.3 %reduce-scatter.92.cloned.1.call-done = f32[128,2]{1,0:T(8,128)} async-done(((f32[1024,2]{1,0:T(8,128)}), f32[128,2]{1,0:T(8,128)}) %reduce-scatter.92.cloned.1.call-update) | async-done | bytes 1040
  1680.0 23.0 %all-reduce.2 = (bf16[3072]{0:T(1024)(128)(2,1)S(1)}, bf16[1024]{0:T(1024)(128)(2,1)S(1)}) all-reduce(f32[3072]{0:T(1024)S(1)} %add.771, f32[1024]{0:T(1024)S(1)} %add.774), channel_id=39, replica_groups=mesh['dp'=8,'seq'=4] {'dp'}, use_global_device_ids=true, to_apply=%region_101.102.clone | all-reduce | flops 4096 | bytes 24576
  1704.9 12.1 reduce-scatter.80.cloned.1.call-done
  1717.9 35.9 %reduce-scatter.88.cloned.1.call-done = f32[96,3]{1,0:T(8,128)} async-done(((f32[768,3]{1,0:T(8,128)}), f32[96,3]{1,0:T(8,128)}) %reduce-scatter.88.cloned.1.call-update) | async-done | bytes 1168
  1754.7 36.1 %reduce-scatter.86.cloned.1.call-done = f32[96,3]{1,0:T(8,128)} async-done(((f32[768,3]{1,0:T(8,128)}), f32[96,3]{1,0:T(8,128)}) %reduce-scatter.86.cloned.1.call-update) | async-done | bytes 1168
  1791.6 36.5 %reduce-scatter.84.cloned.1.call-done = f32[96,3]{1,0:T(8,128)} async-done(((f32[768,3]{1,0:T(8,128)}), f32[96,3]{1,0:T(8,128)}) %reduce-scatter.84.cloned.1.call-update) | async-done | bytes 1168
  1837.5 28.3 %reduce-scatter.82.cloned.1.call-done = f32[128,2]{1,0:T(8,128)} async-done(((f32[1024,2]{1,0:T(8,128)}), f32[128,2]{1,0:T(8,128)}) %reduce-scatter.82.cloned.1.call-update) | async-done | bytes 1040
  1872.6 30.5 %reduce-scatter.78.cloned.1.call-done = f32[96,2]{1,0:T(8,128)} async-done(((f32[768,2]{1,0:T(8,128)}), f32[96,2]{1,0:T(8,128)}) %reduce-scatter.78.cloned.1.call-update) | async-done | bytes 784
  1903.9 12.0 all-reduce.3
  1922.1 146.8 %all-reduce.7.cloned.1.call-done = (bf16[96,3,768]{0,2,1:T(8,128)(2,1)}, bf16[128,3,1024]{0,2,1:T(8,128)(2,1)}, bf16[96,768]{1,0:T(8,128)(2,1)}, bf16[96,3,1024]...) async-done(((bf16[96,3,768]{0,2,1:T(8,128)(2,1)}, ...) | async-done | bytes 4128784 | tf_op jit(solution)/shard_map/psum | solution.py:467
  (1112 shorter events, 421.7 us)
Async XLA Ops:
  7.2 39.4 %all-gather.23.cloned.1.call-start = ((), (), s32[]{:S(2)}) async-start(), calls=%async_computation.25 | async-start | bytes 3981312 | tf_op jit(solution)/shard_map/all_gather | solution.py:403
  7.9 91.7 %all-gather.41.cloned.1.call-start = ((), (), s32[]{:S(2)}) async-start(), calls=%async_computation.34 | async-start | bytes 1966080 | tf_op jit(solution)/shard_map/all_gather | solution.py:187
  50.2 75.4 %all-gather.25.cloned.1.call-start = ((), (), s32[]{:S(2)}) async-start(), calls=%async_computation.26 | async-start | bytes 1966080 | tf_op jit(solution)/shard_map/all_gather | solution.py:187
  53.8 96.5 %all-gather.27.cloned.1.call-start = ((), (), s32[]{:S(2)}) async-start(), calls=%async_computation.27 | async-start | bytes 1327104 | tf_op jit(solution)/shard_map/all_gather | solution.py:405
  54.4 136.6 %all-gather.33.cloned.1.call-start = ((), (), s32[]{:S(2)}) async-start(), calls=%async_computation.30 | async-start | bytes 5308416 | tf_op jit(solution)/shard_map/all_gather | solution.py:406
  55.0 183.4 %all-gather.29.cloned.1.call-start = ((), (), s32[]{:S(2)}) async-start(), calls=%async_computation.28 | async-start | bytes 7077888 | tf_op jit(solution)/shard_map/all_gather | solution.py:408
  55.5 230.9 %all-gather.53.cloned.1.call-start = ((), (), s32[]{:S(2)}) async-start(), calls=%async_computation.40 | async-start | bytes 2621440 | tf_op jit(solution)/shard_map/all_gather | solution.py:194
  195.9 119.1 %all-gather.47.cloned.1.call-start = ((), (), s32[]{:S(2)}) async-start(), calls=%async_computation.37 | async-start | bytes 2359296 | tf_op jit(solution)/shard_map/all_gather | solution.py:411
  196.7 166.4 %all-gather.45.cloned.1.call-start = ((), (), s32[]{:S(2)}) async-start(), calls=%async_computation.36 | async-start | bytes 2621440 | tf_op jit(solution)/shard_map/all_gather | solution.py:194
  201.6 189.9 %all-gather.49.cloned.1.call-start = ((), (), s32[]{:S(2)}) async-start(), calls=%async_computation.38 | async-start | bytes 2359296 | tf_op jit(solution)/shard_map/all_gather | solution.py:415
  202.2 219.1 %all-gather.51.cloned.1.call-start = ((), (), s32[]{:S(2)}) async-start(), calls=%async_computation.39 | async-start | bytes 2359296 | tf_op jit(solution)/shard_map/all_gather | solution.py:417
  203.0 276.9 %all-gather.43.cloned.1.call-start = ((), (), s32[]{:S(2)}) async-start(), calls=%async_computation.35 | async-start | bytes 2621440 | tf_op jit(solution)/shard_map/all_gather | solution.py:195
  243.0 252.6 %all-gather.35.cloned.1.call-start = ((), (), s32[]{:S(2)}) async-start(), calls=%async_computation.31 | async-start | bytes 1769472 | tf_op jit(solution)/shard_map/all_gather | solution.py:410
  243.8 299.8 %all-gather.31.cloned.1.call-start = ((), (), s32[]{:S(2)}) async-start(), calls=%async_computation.29 | async-start | bytes 2621440 | tf_op jit(solution)/shard_map/all_gather | solution.py:195
  248.5 334.5 %all-gather.37.cloned.1.call-start = ((), (), s32[]{:S(2)}) async-start(), calls=%async_computation.32 | async-start | bytes 5308416 | tf_op jit(solution)/shard_map/all_gather | solution.py:412
  249.1 374.6 %all-gather.39.cloned.1.call-start = ((), (), s32[]{:S(2)}) async-start(), calls=%async_computation.33 | async-start | bytes 5308416 | tf_op jit(solution)/shard_map/all_gather | solution.py:414
  249.7 420.1 %reduce-scatter.50.cloned.1.call-start = ((), (), s32[]{:S(2)}) async-start(), calls=%async_computation.43 | async-start | bytes 2621440 | tf_op jit(solution)/shard_map/reduce_scatter | solution.py:270
  456.3 258.9 %reduce-scatter.46.cloned.1.call-start = ((), (), s32[]{:S(2)}) async-start(), calls=%async_computation.41 | async-start | bytes 2621440 | tf_op jit(solution)/shard_map/reduce_scatter | solution.py:270
  479.6 332.1 %reduce-scatter.48.cloned.1.call-start = ((), (), s32[]{:S(2)}) async-start(), calls=%async_computation.42 | async-start | bytes 1966080 | tf_op jit(solution)/shard_map/reduce_scatter | solution.py:302
  738.7 78.0 %reduce-scatter.52.cloned.1.call-start = ((), (), s32[]{:S(2)}) async-start(), calls=%async_computation.44 | async-start | bytes 1966080 | tf_op jit(solution)/shard_map/reduce_scatter | solution.py:302
  754.9 100.7 %reduce-scatter.54.cloned.1.call-start = ((), (), s32[]{:S(2)}) async-start(), calls=%async_computation.45 | async-start | bytes 2621440 | tf_op jit(solution)/shard_map/reduce_scatter | solution.py:273
  762.8 138.4 %reduce-scatter.56.cloned.1.call-start = ((), (), s32[]{:S(2)}) async-start(), calls=%async_computation.46 | async-start | bytes 2621440 | tf_op jit(solution)/shard_map/reduce_scatter | solution.py:273
  769.9 185.4 %reduce-scatter.74.cloned.1.call-start = ((), (), s32[]{:S(2)}) async-start(), calls=%async_computation.55 | async-start | bytes 4718592 | tf_op jit(solution)/shard_map/reduce_scatter | solution.py:457
  776.6 233.6 %reduce-scatter.72.cloned.1.call-start = ((), (), s32[]{:S(2)}) async-start(), calls=%async_computation.54 | async-start | bytes 4718592 | tf_op jit(solution)/shard_map/reduce_scatter | solution.py:455
  781.2 283.7 %reduce-scatter.66.cloned.1.call-start = ((), (), s32[]{:S(2)}) async-start(), calls=%async_computation.51 | async-start | bytes 4718592 | tf_op jit(solution)/shard_map/reduce_scatter | solution.py:451
  785.7 329.1 %reduce-scatter.64.cloned.1.call-start = ((), (), s32[]{:S(2)}) async-start(), calls=%async_computation.50 | async-start | bytes 3538944 | tf_op jit(solution)/shard_map/reduce_scatter | solution.py:450
  789.6 370.9 %reduce-scatter.58.cloned.1.call-start = ((), (), s32[]{:S(2)}) async-start(), calls=%async_computation.47 | async-start | bytes 2654208 | tf_op jit(solution)/shard_map/reduce_scatter | solution.py:445
  793.1 447.9 %reduce-scatter.68.cloned.1.call-start = ((), (), s32[]{:S(2)}) async-start(), calls=%async_computation.52 | async-start | bytes 10616832 | tf_op jit(solution)/shard_map/reduce_scatter | solution.py:452
  800.8 520.6 %reduce-scatter.70.cloned.1.call-start = ((), (), s32[]{:S(2)}) async-start(), calls=%async_computation.53 | async-start | bytes 10616832 | tf_op jit(solution)/shard_map/reduce_scatter | solution.py:454
  808.4 582.3 %reduce-scatter.76.cloned.1.call-start = ((), (), s32[]{:S(2)}) async-start(), calls=%async_computation.56 | async-start | bytes 7962624
  810.6 113.4 %copy-start.141 = (bf16[4,32,1,768]{3,1,0,2:T(8,128)(2,1)}, bf16[4,32,1,768]{3,1,0,2:T(8,128)(2,1)S(1)}, u32[]{:S(2)}) copy-start(bf16[4,32,1,768]{3,1,0,2:T(8,128)(2,1)S(1)} %convert_element_type.714) | copy-start | bytes 589828
  811.7 112.6 %copy-start.85 = (bf16[4,32,1,768]{3,1,0,2:T(8,128)(2,1)}, bf16[4,32,1,768]{3,1,0,2:T(8,128)(2,1)S(1)}, u32[]{:S(2)}) copy-start(bf16[4,32,1,768]{3,1,0,2:T(8,128)(2,1)S(1)} %convert_element_type.738) | copy-start | bytes 589828
  832.3 638.4 %reduce-scatter.60.cloned.1.call-start = ((), (), s32[]{:S(2)}) async-start(), calls=%async_computation.48 | async-start | bytes 10616832 | tf_op jit(solution)/shard_map/reduce_scatter | solution.py:446
  839.9 726.7 %reduce-scatter.62.cloned.1.call-start = ((), (), s32[]{:S(2)}) async-start(), calls=%async_computation.49 | async-start | bytes 14155776 | tf_op jit(solution)/shard_map/reduce_scatter | solution.py:448
  913.2 690.5 %reduce-scatter.94.cloned.1.call-start = ((), (), s32[]{:S(2)}) async-start(), calls=%async_computation.65 | async-start | bytes 589824
  915.1 726.8 %reduce-scatter.90.cloned.1.call-start = ((), (), s32[]{:S(2)}) async-start(), calls=%async_computation.63 | async-start | bytes 589824
  916.3 762.8 %reduce-scatter.92.cloned.1.call-start = ((), (), s32[]{:S(2)}) async-start(), calls=%async_computation.64 | async-start | bytes 589824
  917.5 799.6 %reduce-scatter.80.cloned.1.call-start = ((), (), s32[]{:S(2)}) async-start(), calls=%async_computation.58 | async-start | bytes 589824
  919.3 834.5 %reduce-scatter.88.cloned.1.call-start = ((), (), s32[]{:S(2)}) async-start(), calls=%async_computation.62 | async-start | bytes 442368
  920.4 870.3 %reduce-scatter.86.cloned.1.call-start = ((), (), s32[]{:S(2)}) async-start(), calls=%async_computation.61 | async-start | bytes 442368
  921.5 906.6 %reduce-scatter.84.cloned.1.call-start = ((), (), s32[]{:S(2)}) async-start(), calls=%async_computation.60 | async-start | bytes 442368
  922.5 943.3 %reduce-scatter.82.cloned.1.call-start = ((), (), s32[]{:S(2)}) async-start(), calls=%async_computation.59 | async-start | bytes 589824
  924.0 979.0 %reduce-scatter.78.cloned.1.call-start = ((), (), s32[]{:S(2)}) async-start(), calls=%async_computation.57 | async-start | bytes 442368
  925.4 1143.6 %all-reduce.7.cloned.1.call-start = ((), (), s32[]{:S(2)}) async-start(), calls=%async_computation.66 | async-start | bytes 8552448 | tf_op jit(solution)/shard_map/psum | solution.py:467
  1569.0 110.9 %copy-start.254 = (f32[3072]{0:T(1024)S(1)}, f32[3072]{0:T(1024)}, u32[]{:S(2)}) copy-start(f32[3072]{0:T(1024)} %get-tuple-element.383) | copy-start | bytes 36868
  1569.0 265.4 %slice-start = ((s8[6291456]{0:T(1024)(128)(4,1)}), s8[2097152]{0:T(1024)(128)(4,1)S(1)}, s32[]{:S(2)}) async-start(s8[6291456]{0:T(1024)(128)(4,1)} %bitcast.752), calls=%async_computation.67 | async-start | bytes 4194304
  1569.1 259.9 %copy-start.33 = (f32[4,32,1024]{2,1,0:T(8,128)S(1)}, f32[4,32,1024]{2,1,0:T(8,128)}, u32[]{:S(2)}) copy-start(f32[4,32,1024]{2,1,0:T(8,128)} %get-tuple-element.240) | copy-start | bytes 1572868
  1569.1 259.9 %copy-start.211 = (f32[4,32]{1,0:T(4,128)S(1)}, f32[4,32]{1,0:T(4,128)}, u32[]{:S(2)}) copy-start(f32[4,32]{1,0:T(4,128)} %copy-done.210) | copy-start | bytes 1540
  (317 other events, 2508.1 us)
Sparse Core Ops, SparseCore 0:
  9.9 36.6 all-gather.22
  50.3 37.0 all-gather.40
  89.6 35.9 all-gather.24
  127.3 22.9 all-gather.26
  152.0 38.9 all-gather.32
  192.8 45.5 all-gather.28
  240.5 45.9 all-gather.52
  288.3 26.5 all-gather.46
  317.1 45.9 all-gather.44
  364.8 26.5 all-gather.48
  393.4 27.8 all-gather.50
  423.3 45.9 all-gather.42
  471.2 24.3 all-gather.34
  497.6 45.9 all-gather.30
  545.3 37.7 all-gather.36
  584.8 38.9 all-gather.38
  625.9 43.8 reduce-scatter.49
  672.0 43.1 reduce-scatter.45
  738.8 34.6 reduce-scatter.47
  776.2 34.2 reduce-scatter.51
  812.8 42.8 reduce-scatter.53
  858.0 43.1 reduce-scatter.55
  904.6 50.6 reduce-scatter.73
  958.9 51.3 reduce-scatter.71
  1013.6 51.2 reduce-scatter.65
  1068.5 46.2 reduce-scatter.63
  1118.0 42.4 reduce-scatter.57
  1164.4 76.4 reduce-scatter.67
  1244.9 76.4 reduce-scatter.69
  1325.2 65.4 reduce-scatter.75
  1394.2 76.4 reduce-scatter.59
  1474.2 92.3 reduce-scatter.61
  1569.5 34.1 reduce-scatter.93
  1607.7 34.1 reduce-scatter.89
  1644.9 34.0 reduce-scatter.91
  1682.8 34.1 reduce-scatter.79
  1720.0 33.8 reduce-scatter.87
  1756.9 33.8 reduce-scatter.85
  1794.2 33.8 reduce-scatter.83
  1831.8 34.0 reduce-scatter.81
  1869.2 33.8 reduce-scatter.77
  1907.8 161.1 all-reduce.6
where the time goes:
time: 2100 us; the launch traced here: 2090 us
  waiting for transfers between devices  1540 us (73%)
  matrix products  190 us (9%)
  blocking collectives  129 us (6%)
  local copies, waits for them, and re-layouts  117 us (6%)
  other arithmetic  92.4 us (4%)
    unnamed x52, waiting for transfers between devices  357 us
    psum x1, waiting for transfers between devices, local(): lax.psum(accumulated[0].astype(jnp.bfloat16), 'seq').astype(jnp.float32)  147 us
    reduce_scatter x1, waiting for transfers between devices, local(): lax.psum_scatter(gradients[5], 'dp', scatter_dimension=0, tiled=True)  93.8 us
    reduce_scatter x1, waiting for transfers between devices, local(): lax.psum_scatter(gradients[9], 'dp', scatter_dimension=0, tiled=True)  78.8 us
    reduce_scatter x1, waiting for transfers between devices, local(): lax.psum_scatter(gradients[11], 'dp', scatter_dimension=0, tiled=True)  78.3 us
    reduce_scatter x1, waiting for transfers between devices, local(): lax.psum_scatter(gradients[3], 'dp', scatter_dimension=0, tiled=True)  77.8 us
    unnamed x682, local copies, waits for them, and re-layouts  67.8 us
    reduce_scatter x1, waiting for transfers between devices, local(): lax.psum_scatter(gradients[12], 'dp', scatter_dimension=0, tiled=True)  53.2 us
  transfers between devices with their start and end apart: 42, of which 38 were waited for; matrix products, arithmetic and copies ran while one was open for 16% of the time, Pallas kernels for 0%

commit v1 on v0

--- a/solution.py
+++ b/solution.py
@@ -1,6 +1,10 @@
+import functools
+
 import jax
 import jax.numpy as jnp
 from jax import lax
+from jax.experimental import pallas as pl
+from jax.experimental.pallas import tpu as pltpu
 from jax.sharding import PartitionSpec as P
 
 HT = 12
@@ -339,7 +343,7 @@
     return (outputs, gradients)
 
 
-def local(
+def local_plain(
     text,
     image,
     text_len,
@@ -493,6 +497,753 @@
     return (text_out, image_out, text_grad, image_grad) + tuple(summed)
 
 
+MESH = pl.DeviceIdType.MESH
+ANY = pl.BlockSpec(memory_space=pl.ANY)
+VMEM = pl.BlockSpec(memory_space=pltpu.VMEM)
+
+
+def place():
+    dp = lax.axis_index("dp")
+    z = lax.axis_index("seq")
+    row = dp // 4
+    col = (dp // 2) % 2
+    core = dp % 2
+    return (dp, z, row, col, core)
+
+
+def partners(row, col, core, first_row):
+    near_row = row + first_row * (1 - 2 * row)
+    near_col = col + (1 - first_row) * (1 - 2 * col)
+    far_row = row + (1 - first_row) * (1 - 2 * row)
+    far_col = col + first_row * (1 - 2 * col)
+    near = near_row * 4 + near_col * 2 + core
+    far = far_row * 4 + far_col * 2 + core
+    return (near, far)
+
+
+def greet(devices):
+    barrier = pltpu.get_barrier_semaphore()
+    for device in devices:
+        pl.semaphore_signal(barrier, inc=1, device_id=device, device_id_type=MESH)
+    pl.semaphore_wait(barrier, len(devices))
+
+
+def remote(source, target, send_sem, recv_sem, device):
+    return pltpu.make_async_remote_copy(
+        src_ref=source,
+        dst_ref=target,
+        send_sem=send_sem,
+        recv_sem=recv_sem,
+        device_id=device,
+        device_id_type=MESH,
+    )
+
+
+def gather_kernel(weight_count, *refs):
+    total = weight_count + 4
+    blocks = refs[:weight_count]
+    states = refs[weight_count:total]
+    wholes = refs[total : total + weight_count]
+    pairs = refs[total + weight_count : 2 * total]
+    send_sem, recv_sem, swap_send, swap_recv, own_sem = refs[2 * total :]
+    dp, z, row, col, core = place()
+    near, far = partners(row, col, core, 1 - core)
+    sibling = dp + 1 - 2 * core
+    diagonal = (1 - row) * 4 + (1 - col) * 2 + core
+    others = [lax.rem(z + step, 4) for step in (1, 2, 3)]
+    greet([(near, z), (far, z), (sibling, z)] + [(dp, other) for other in others])
+
+    def rows_of(whole, index):
+        depth = whole.shape[1] // 8
+        return whole.at[:, pl.ds(pl.multiple_of(index * depth, 16), depth), :]
+
+    started = []
+
+    def send(array, lane, source, index, device):
+        copy = remote(
+            source,
+            rows_of(wholes[array], index),
+            send_sem.at[array, lane],
+            recv_sem.at[array, lane],
+            (device, z),
+        )
+        copy.start()
+        started.append(copy)
+        return copy
+
+    locals_ = []
+    first = []
+    for array in range(weight_count):
+        block = blocks[array]
+        first.append(
+            (
+                send(array, 0, block, dp, near),
+                send(array, 1, block, dp, far),
+                send(array, 2, block, dp, sibling),
+            )
+        )
+        keep = pltpu.make_async_copy(block, rows_of(wholes[array], dp), own_sem.at[array])
+        keep.start()
+        locals_.append(keep)
+    swaps = []
+    for array in range(4):
+        source, target = states[array], pairs[array]
+        count = source.shape[0] // 4
+        slots = source.shape[1]
+        here = target.at[:, pl.ds(pl.multiple_of(z * slots, 16), slots), :]
+        for step, other in enumerate(others):
+            copy = remote(
+                source.at[pl.ds(other * count, count)],
+                here,
+                swap_send.at[array, step],
+                swap_recv.at[array, step],
+                (dp, other),
+            )
+            copy.start()
+            swaps.append(copy)
+        keep = pltpu.make_async_copy(
+            source.at[pl.ds(z * count, count)], here, own_sem.at[weight_count + array]
+        )
+        keep.start()
+        locals_.append(keep)
+    second = []
+    for array in range(weight_count):
+        first[array][0].wait_recv()
+        arrived = rows_of(wholes[array], near)
+        second.append(
+            (
+                send(array, 3, arrived, near, far),
+                send(array, 4, arrived, near, sibling),
+            )
+        )
+    for array in range(weight_count):
+        first[array][1].wait_recv()
+        second.append((send(array, 5, rows_of(wholes[array], far), far, sibling),))
+    for array in range(weight_count):
+        second[array][0].wait_recv()
+        second.append((send(array, 6, rows_of(wholes[array], diagonal), diagonal, sibling),))
+    for array in range(weight_count):
+        first[array][2].wait_recv()
+        second[array][1].wait_recv()
+        second[weight_count + array][0].wait_recv()
+        second[2 * weight_count + array][0].wait_recv()
+    for copy in started:
+        copy.wait_send()
+    for copy in swaps:
+        copy.wait()
+    for copy in locals_:
+        copy.wait()
+
+
+def gather(blocks, states):
+    weight_count = len(blocks)
+    out_shape = [
+        jax.ShapeDtypeStruct((b.shape[0], b.shape[1] * 8, b.shape[2]), b.dtype) for b in blocks
+    ] + [
+        jax.ShapeDtypeStruct((s.shape[0] // 4, s.shape[1] * 4, s.shape[2]), s.dtype) for s in states
+    ]
+    dma = pltpu.SemaphoreType.DMA
+    results = pl.pallas_call(
+        functools.partial(gather_kernel, weight_count),
+        out_shape=out_shape,
+        in_specs=[ANY] * (weight_count + 4),
+        out_specs=[ANY] * (weight_count + 4),
+        scratch_shapes=[
+            dma((weight_count, 7)),
+            dma((weight_count, 7)),
+            dma((4, 3)),
+            dma((4, 3)),
+            dma((weight_count + 4,)),
+        ],
+        compiler_params=pltpu.CompilerParams(collective_id=0, has_side_effects=True),
+        name="gather",
+    )(*blocks, *states)
+    return (results[:weight_count], results[weight_count:])
+
+
+CHUNKS = (9, 9, 3)
+TILES = (4, 3, 1)
+ROWS = (96, 128, 384)
+STARTS = ((9, 12, 24), (12, 15, 19, 23), ())
+STEPS = 21
+LAG_NEAR, LAG_FAR, LAG_SUM, LAG_MID, LAG_END = 1, 3, 5, 7, 9
+
+
+def reduce_kernel(*refs):
+    inputs = refs[0:3]
+    grads = refs[3:6]
+    small = refs[6]
+    states = refs[7:11]
+    result, small_result = refs[11:13]
+    pairs = refs[13:17]
+    (
+        out_box, chip, near_sum, plane, line, cross,
+        s_out, s_chip, s_near, s_plane, s_line, s_cross,
+        core_send, core_recv, near_send, near_recv, far_send, far_recv,
+        end_send, end_recv, mid_send, mid_recv, back_send, back_recv,
+        write_sem, swap_send, swap_recv, own_sem,
+    ) = refs[17:]
+    dp, z, row, col, core = place()
+    near, far = partners(row, col, core, core)
+    sibling = dp + 1 - 2 * core
+    others = [lax.rem(z + step, 4) for step in (1, 2, 3)]
+    near_bit = col + core * (row - col)
+    far_bit = row + core * (col - row)
+
+    def block_of(near_index, far_index):
+        return near_index * (1 + core) + far_index * (2 - core)
+
+    is_end = (z == 0) | (z == 3)
+    is_mid = (z == 1) | (z == 2)
+    middle = 1 + z // 2
+    other_mid = 3 - z
+    end = 3 * (z // 2)
+    greet([(near, z), (far, z), (sibling, z)] + [(dp, other) for other in others])
+
+    copies = []
+    for array in range(4):
+        source, target = states[array], pairs[array]
+        count = source.shape[0]
+        slots = source.shape[1] // 4
+        there = target.at[pl.ds(z * count, count)]
+        for step, other in enumerate(others):
+            copy = remote(
+                source.at[:, pl.ds(pl.multiple_of(other * slots, 16), slots), :],
+                there,
+                swap_send.at[array, step],
+                swap_recv.at[array, step],
+                (dp, other),
+            )
+            copy.start()
+            copies.append(copy)
+        keep = pltpu.make_async_copy(
+            source.at[:, pl.ds(pl.multiple_of(z * slots, 16), slots), :], there, own_sem.at[array]
+        )
+        keep.start()
+        copies.append(keep)
+
+    def products(index, half, use):
+        base = 0
+        for kind in range(3):
+            count, tiles, rows = CHUNKS[kind], TILES[kind], ROWS[kind]
+            chosen = (index >= base) & (index < base + count)
+
+            def work(kind=kind, base=base, tiles=tiles, rows=rows):
+                for tile in range(tiles):
+                    which = (index - base) * tiles + tile
+                    weight = 0
+                    for bound in STARTS[kind]:
+                        weight = weight + jnp.where(which >= bound, 1, 0)
+                    left = inputs[kind][weight, half]
+                    right = grads[kind][:, pl.ds(pl.multiple_of(which * 256, 256), 256)]
+                    part = jnp.dot(left, right, preferred_element_type=jnp.float32)
+                    for block in range(4):
+                        for side in range(2):
+                            use(
+                                block,
+                                (tile * 2 + side) * rows,
+                                rows,
+                                part[block * rows : (block + 1) * rows, side * 128 : side * 128 + 128],
+                            )
+
+            pl.when(chosen)(work)
+            base += count
+
+    def core_copy(index):
+        return remote(
+            out_box.at[lax.rem(index, 2)], chip.at[index], core_send.at[index], core_recv.at[index], (sibling, z)
+        )
+
+    def near_copy(index, far_index):
+        return remote(
+            chip.at[index, block_of(1 - near_bit, far_index)],
+            near_sum.at[index, far_index],
+            near_send.at[index, far_index],
+            near_recv.at[index, far_index],
+            (near, z),
+        )
+
+    def far_copy(index):
+        return remote(
+            near_sum.at[index, 1 - far_bit], plane.at[index], far_send.at[index], far_recv.at[index], (far, z)
+        )
+
+    def end_copy(index):
+        return remote(plane.at[index], line.at[index], end_send.at[index], end_recv.at[index], (dp, middle))
+
+    def mid_copy(index):
+        return remote(line.at[index], cross.at[index], mid_send.at[index], mid_recv.at[index], (dp, other_mid))
+
+    def back_copy(index):
+        return remote(cross.at[index], line.at[index], back_send.at[index], back_recv.at[index], (dp, end))
+
+    def mid_write(index):
+        return pltpu.make_async_copy(cross.at[index], result.at[index], write_sem.at[index])
+
+    def end_write(index):
+        return pltpu.make_async_copy(line.at[index], result.at[index], write_sem.at[index])
+
+    def wide(values):
+        return values.astype(jnp.float32)
+
+    def stage_core(index):
+        @pl.when(index >= 2)
+        def _():
+            core_copy(index - 2).wait_send()
+
+        slot = lax.rem(index, 2)
+
+        def put(block, first, rows, values):
+            out_box[slot, block, first : first + rows, :] = values.astype(jnp.bfloat16)
+
+        products(index, 1 - core, put)
+        core_copy(index).start()
+
+    def stage_near(index):
+        core_copy(index).wait_recv()
+
+        def add(block, first, rows, values):
+            window = (index, block, slice(first, first + rows), slice(None))
+            chip[window] = (wide(chip[window]) + values).astype(jnp.bfloat16)
+
+        products(index, core, add)
+        near_copy(index, 1 - far_bit).start()
+        near_copy(index, far_bit).start()
+
+    def stage_far(index):
+        for far_index in (1 - far_bit, far_bit):
+            near_copy(index, far_index).wait_recv()
+            mine = chip[index, block_of(near_bit, far_index)]
+            near_sum[index, far_index] = (wide(near_sum[index, far_index]) + wide(mine)).astype(jnp.bfloat16)
+            if far_index is not far_bit:
+                far_copy(index).start()
+
+    def stage_sum(index):
+        far_copy(index).wait_recv()
+        plane[index] = (wide(plane[index]) + wide(near_sum[index, far_bit])).astype(jnp.bfloat16)
+
+        @pl.when(is_end)
+        def _():
+            end_copy(index).start()
+
+    def stage_mid(index):
+        @pl.when(is_mid)
+        def _():
+            end_copy(index).wait_recv()
+            line[index] = (wide(line[index]) + wide(plane[index])).astype(jnp.bfloat16)
+            mid_copy(index).start()
+
+    def stage_end(index):
+        @pl.when(is_mid)
+        def _():
+            mid_copy(index).wait_recv()
+            cross[index] = (wide(cross[index]) + wide(line[index])).astype(jnp.bfloat16)
+            back_copy(index).start()
+            mid_write(index).start()
+
+    def stage_write(index):
+        @pl.when(is_end)
+        def _():
+            back_copy(index).wait_recv()
+            end_write(index).start()
+
+    stages = (
+        (stage_core, 0),
+        (stage_near, LAG_NEAR),
+        (stage_far, LAG_FAR),
+        (stage_sum, LAG_SUM),
+        (stage_mid, LAG_MID),
+        (stage_end, LAG_END),
+        (stage_write, LAG_END + 2),
+    )
+
+    last = STEPS
+    sm_core = remote(small.at[1 - core], s_chip, core_send.at[last], core_recv.at[last], (sibling, z))
+    sm_near = [
+        remote(
+            s_chip.at[block_of(1 - near_bit, j)], s_near.at[j], near_send.at[last, j], near_recv.at[last, j], (near, z)
+        )
+        for j in (0, 1)
+    ]
+    sm_far = remote(s_near.at[1 - far_bit], s_plane, far_send.at[last], far_recv.at[last], (far, z))
+    sm_end = remote(s_plane, s_line, end_send.at[last], end_recv.at[last], (dp, middle))
+    sm_mid = remote(s_line, s_cross, mid_send.at[last], mid_recv.at[last], (dp, other_mid))
+    sm_back = remote(s_cross, s_line, back_send.at[last], back_recv.at[last], (dp, end))
+    sm_core.start()
+
+    def small_steps(turn):
+        @pl.when(turn == 1)
+        def _():
+            sm_core.wait_recv()
+            s_chip[...] += small[core]
+            for copy in sm_near:
+                copy.start()
+
+        @pl.when(turn == 3)
+        def _():
+            for j in (0, 1):
+                sm_near[j].wait_recv()
+                s_near[j] += s_chip[block_of(near_bit, j)]
+            sm_far.start()
+
+        @pl.when(turn == 5)
+        def _():
+            sm_far.wait_recv()
+            s_plane[...] += s_near[far_bit]
+
+        @pl.when((turn == 5) & is_end)
+        def _():
+            sm_end.start()
+
+        @pl.when((turn == 7) & is_mid)
+        def _():
+            sm_end.wait_recv()
+            s_line[...] += s_plane[...]
+            sm_mid.start()
+
+        @pl.when((turn == 9) & is_mid)
+        def _():
+            sm_mid.wait_recv()
+            s_cross[...] += s_line[...]
+            sm_back.start()
+            small_result[...] = s_cross[...]
+
+        @pl.when((turn == 11) & is_end)
+        def _():
+            sm_back.wait_recv()
+            small_result[...] = s_line[...]
+
+    def turn_body(turn, carry):
+        for stage, lag in stages:
+            index = turn - lag
+
+            @pl.when((index >= 0) & (index < STEPS))
+            def _(stage=stage, index=index):
+                stage(index)
+
+        small_steps(turn)
+        return carry
+
+    lax.fori_loop(0, STEPS + LAG_END + 2, turn_body, 0)
+
+    core_copy(STEPS - 2).wait_send()
+    core_copy(STEPS - 1).wait_send()
+    sm_core.wait_send()
+    for copy in sm_near:
+        copy.wait_send()
+    sm_far.wait_send()
+
+    def settle(index, carry):
+        near_copy(index, 0).wait_send()
+        near_copy(index, 1).wait_send()
+        far_copy(index).wait_send()
+
+        @pl.when(is_end)
+        def _():
+            end_copy(index).wait_send()
+            end_write(index).wait()
+
+        @pl.when(is_mid)
+        def _():
+            mid_copy(index).wait_send()
+            back_copy(index).wait_send()
+            mid_write(index).wait()
+
+        return carry
+
+    lax.fori_loop(0, STEPS, settle, 0)
+
+    @pl.when(is_end)
+    def _():
+        sm_end.wait_send()
+
+    @pl.when(is_mid)
+    def _():
+        sm_mid.wait_send()
+        sm_back.wait_send()
+
+    for copy in copies:
+        copy.wait()
+
+
+def reduce_all(inputs, grads, small, states):
+    dma = pltpu.SemaphoreType.DMA
+    narrow = jnp.bfloat16
+    block = (768, 128)
+    tiny = small.shape[2:]
+    steps = STEPS + 1
+    one = [dma((steps,))] * 2
+    results = pl.pallas_call(
+        reduce_kernel,
+        out_shape=[
+            jax.ShapeDtypeStruct((STEPS,) + block, narrow),
+            jax.ShapeDtypeStruct(tiny, jnp.float32),
+        ]
+        + [jax.ShapeDtypeStruct((s.shape[0] * 4, s.shape[1] // 4, s.shape[2]), s.dtype) for s in states],
+        in_specs=[VMEM] * 7 + [ANY] * 4,
+        out_specs=[ANY, VMEM] + [ANY] * 4,
+        scratch_shapes=[
+            pltpu.VMEM((2, 4) + block, narrow),
+            pltpu.VMEM((STEPS, 4) + block, narrow),
+            pltpu.VMEM((STEPS, 2) + block, narrow),
+            pltpu.VMEM((STEPS,) + block, narrow),
+            pltpu.VMEM((STEPS,) + block, narrow),
+            pltpu.VMEM((STEPS,) + block, narrow),
+            pltpu.VMEM((4,) + tiny, jnp.float32),
+            pltpu.VMEM((4,) + tiny, jnp.float32),
+            pltpu.VMEM((2,) + tiny, jnp.float32),
+            pltpu.VMEM(tiny, jnp.float32),
+            pltpu.VMEM(tiny, jnp.float32),
+            pltpu.VMEM(tiny, jnp.float32),
+        ]
+        + one
+        + [dma((steps, 2))] * 2
+        + one * 4
+        + [dma((steps,)), dma((4, 3)), dma((4, 3)), dma((4,))],
+        compiler_params=pltpu.CompilerParams(
+            collective_id=1, has_side_effects=True, vmem_limit_bytes=61 * 2**20
+        ),
+        name="reduce_all",
+    )(*inputs, *grads, small, *states)
+    return (results[0], results[1], results[2:])
+
+
+SMALL = ((2, 96), (2, 128), (2, 128), (1, 384), (1, 128), (3, 96), (3, 96), (3, 96), (2, 128), (2, 128), (2, 128))
+SMALL_ROWS = 32
+
+
+def pack_small(arrays):
+    rows = []
+    for (count, width), array in zip(SMALL, arrays):
+        flat = array.reshape(count, width)
+        if width > 128:
+            flat = flat.reshape(width // 128, 128)
+        rows.append(jnp.pad(flat, ((0, 0), (0, 128 - flat.shape[1]))))
+    packed = jnp.concatenate(rows, axis=0)
+    return jnp.pad(packed, ((0, SMALL_ROWS - packed.shape[0]), (0, 0)))
+
+
+def unpack_small(packed, lead):
+    arrays = []
+    first = 0
+    for count, width in SMALL:
+        lines = count * max(width // 128, 1)
+        part = packed[:, first : first + lines, : min(width, 128)]
+        first += lines
+        if width > 128:
+            arrays.append(part.reshape(lead * width))
+        else:
+            whole = part.transpose(1, 0, 2).reshape(count, lead * width)
+            arrays.append(whole)
+    return arrays
+
+
+def spread_small(arrays):
+    rows = []
+    for (count, width), array in zip(SMALL, arrays):
+        if width > 128:
+            part = array.reshape(8, width // 128, 128)
+        else:
+            part = array.reshape(count, 8, width).transpose(1, 0, 2)
+        rows.append(jnp.pad(part, ((0, 0), (0, 0), (0, 128 - part.shape[2]))))
+    packed = jnp.concatenate(rows, axis=1)
+    return jnp.pad(packed, ((0, 0), (0, SMALL_ROWS - packed.shape[1]), (0, 0)))
+
+
+def mm(left, right):
+    return jnp.dot(left, right, preferred_element_type=jnp.float32)
+
+
+def mm_t(left, right):
+    return lax.dot_general(left, right, (((1,), (1,)), ((), ())), preferred_element_type=jnp.float32)
+
+
+def triple_of(inputs, weight, biases):
+    narrow = jnp.bfloat16
+    query = (mm(inputs, weight[0]) + biases[0].astype(jnp.float32)).astype(narrow)
+    key = mm(inputs, weight[1]).astype(narrow)
+    value = (mm(inputs, weight[2]) + biases[1].astype(jnp.float32)).astype(narrow)
+    return (query, key, value)
+
+
+def heads_of(values, heads):
+    return values.reshape(-1, 128, heads, values.shape[-1] // heads)
+
+
+def att(query, key, value, mask, heads):
+    q, k, v = (heads_of(a, heads) for a in (query, key, value))
+    shrink = q.shape[-1] ** (-0.5)
+    scores = jnp.einsum("pthd,pshd->phts", q, k, preferred_element_type=jnp.float32) * shrink
+    scores = jnp.where(mask[:, None, None, :], scores, NEG_FILL)
+    powers = jnp.exp(scores - jnp.max(scores, axis=-1, keepdims=True))
+    table = powers / jnp.sum(powers, axis=-1, keepdims=True)
+    mixed = jnp.einsum("phts,pshd->pthd", table.astype(jnp.bfloat16), v, preferred_element_type=jnp.float32)
+    return (mixed.reshape(query.shape).astype(jnp.bfloat16), table)
+
+
+def att_back(upstream, query, key, value, table, heads):
+    q, k, v, o = (heads_of(a, heads) for a in (query, key, value, upstream))
+    narrow = jnp.bfloat16
+    shrink = q.shape[-1] ** (-0.5)
+    value_grad = jnp.einsum("phts,pthd->pshd", table.astype(narrow), o, preferred_element_type=jnp.float32)
+    table_grad = jnp.einsum("pthd,pshd->phts", o, v, preferred_element_type=jnp.float32)
+    score_grad = table * (table_grad - jnp.sum(table_grad * table, axis=-1, keepdims=True))
+    score_grad = score_grad.astype(narrow)
+    query_grad = jnp.einsum("phts,pshd->pthd", score_grad, k, preferred_element_type=jnp.float32) * shrink
+    key_grad = jnp.einsum("phts,pthd->pshd", score_grad, q, preferred_element_type=jnp.float32) * shrink
+    return tuple(g.reshape(query.shape).astype(narrow) for g in (query_grad, key_grad, value_grad))
+
+
+def by_owner(inputs):
+    tokens, rows = inputs.shape
+    flipped = inputs.T.reshape(4, 2, rows // 8, tokens)
+    return flipped.transpose(1, 0, 2, 3).reshape(2, rows // 2, tokens)
+
+
+def col_sum(values):
+    return jnp.sum(values, axis=0, dtype=jnp.float32)
+
+
+def ff_back(upstream, inputs, inner, active, totals, factor, offset, weight_in, weight_out):
+    total_grad, factor_grad, offset_grad = norm_back(totals, factor, offset, upstream)
+    branch = total_grad.astype(jnp.bfloat16)
+    inner_grad = gelu_back(inner, mm_t(branch, weight_out)).astype(jnp.bfloat16)
+    return (branch, inner_grad, mm_t(inner_grad, weight_in) + total_grad, factor_grad, offset_grad)
+
+
+def project_input(grads, weight):
+    return mm_t(grads[0], weight[0]) + mm_t(grads[1], weight[1]) + mm_t(grads[2], weight[2])
+
+
+def local_fast(
+    text, image, text_len, region_count, text_cot, image_cot,
+    selfproject, selfbiases, selfoutput, textcoproject, textcobiases, imagecoproject, imagecobiases,
+    textcooutput, imagecooutput, textffinner, textffinbias, textffouter,
+    imageffinner, imageffinbias, imageffouter,
+    textgains, textshifts, textbiases, imagegains, imageshifts, imagebiases,
+):
+    narrow, wide = jnp.bfloat16, jnp.float32
+    z = lax.axis_index("seq")
+    packed = pack_small(
+        (
+            selfbiases, textcobiases, imagecobiases, textffinbias, imageffinbias,
+            textgains, textshifts, textbiases, imagegains, imageshifts, imagebiases,
+        )
+    )
+    blocks = [
+        selfproject.transpose(1, 0, 2), selfoutput[None], textcoproject.transpose(1, 0, 2),
+        imagecoproject.transpose(1, 0, 2), textcooutput[None], imagecooutput[None],
+        textffinner[None], textffouter[None], imageffinner[None], imageffouter[None], packed[None],
+    ]
+    wholes, pairs = gather(blocks, [text, image, text_cot, image_cot])
+    w_self, w_selfout, w_textco, w_imageco = wholes[0], wholes[1][0], wholes[2], wholes[3]
+    w_textout, w_imageout = wholes[4][0], wholes[5][0]
+    w_tin, w_tout, w_iin, w_iout = (w[0] for w in wholes[6:10])
+    (
+        selfbiases, textcobiases, imagecobiases, textffinbias, imageffinbias,
+        textgains, textshifts, textbiases, imagegains, imageshifts, imagebiases,
+    ) = [a.astype(wide) for a in unpack_small(wholes[10].reshape(8, SMALL_ROWS, 128), 8)]
+    imageffinbias = imageffinbias.reshape(-1)
+    text, image, text_cot, image_cot = (p.reshape(-1, p.shape[-1]) for p in pairs)
+    lengths = lax.dynamic_slice(text_len, (z * 2,), (2,))
+    counts = lax.dynamic_slice(region_count, (z * 2,), (2,))
+    text_mask = jnp.arange(128)[None, :] < lengths[:, None]
+    region_mask = jnp.arange(128)[None, :] < counts[:, None]
+
+    self_q, self_k, self_v = triple_of(text, w_self, selfbiases)
+    self_mixed, self_table = att(self_q, self_k, self_v, text_mask, HT)
+    self_sum = text.astype(wide) + mm(self_mixed, w_selfout) + textbiases[0]
+    text_one = layer_norm(self_sum, textgains[0], textshifts[0]).astype(narrow)
+    text_q, text_k, text_v = triple_of(text_one, w_textco, textcobiases)
+    image_q, image_k, image_v = triple_of(image, w_imageco, imagecobiases)
+    text_mixed, text_table = att(text_q, image_k, image_v, region_mask, HC)
+    image_mixed, image_table = att(image_q, text_k, text_v, text_mask, HC)
+    text_sum = text_one.astype(wide) + mm(text_mixed, w_textout) + textbiases[1]
+    text_two = layer_norm(text_sum, textgains[1], textshifts[1]).astype(narrow)
+    image_sum = image.astype(wide) + mm(image_mixed, w_imageout) + imagebiases[0]
+    image_two = layer_norm(image_sum, imagegains[0], imageshifts[0]).astype(narrow)
+    text_inner = mm(text_two, w_tin) + textffinbias
+    text_active = gelu_exact(text_inner).astype(narrow)
+    text_total = text_two.astype(wide) + mm(text_active, w_tout) + textbiases[2]
+    text_out = layer_norm(text_total, textgains[2], textshifts[2]).astype(narrow)
+    image_inner = mm(image_two, w_iin) + imageffinbias
+    image_active = gelu_exact(image_inner).astype(narrow)
+    image_total = image_two.astype(wide) + mm(image_active, w_iout) + imagebiases[1]
+    image_out = layer_norm(image_total, imagegains[1], imageshifts[1]).astype(narrow)
+
+    b_tff, d_tin, g_two, f_t2, o_t2 = ff_back(
+        text_cot.astype(wide), text_two, text_inner, text_active, text_total,
+        textgains[2], textshifts[2], w_tin, w_tout,
+    )
+    b_iff, d_iin, g_itwo, f_i1, o_i1 = ff_back(
+        image_cot.astype(wide), image_two, image_inner, image_active, image_total,
+        imagegains[1], imageshifts[1], w_iin, w_iout,
+    )
+    text_sumgrad, f_t1, o_t1 = norm_back(text_sum, textgains[1], textshifts[1], g_two)
+    b_tco = text_sumgrad.astype(narrow)
+    textmix_grad = mm_t(b_tco, w_textout).astype(narrow)
+    image_sumgrad, f_i0, o_i0 = norm_back(image_sum, imagegains[0], imageshifts[0], g_itwo)
+    b_ico = image_sumgrad.astype(narrow)
+    imagemix_grad = mm_t(b_ico, w_imageout).astype(narrow)
+    d_tq, d_ik, d_iv = att_back(textmix_grad, text_q, image_k, image_v, text_table, HC)
+    d_iq, d_tk, d_tv = att_back(imagemix_grad, image_q, text_k, text_v, image_table, HC)
+    one_grad = project_input((d_tq, d_tk, d_tv), w_textco) + text_sumgrad
+    image_grad = project_input((d_iq, d_ik, d_iv), w_imageco) + image_sumgrad
+    self_sumgrad, f_t0, o_t0 = norm_back(self_sum, textgains[0], textshifts[0], one_grad)
+    b_self = self_sumgrad.astype(narrow)
+    selfmix_grad = mm_t(b_self, w_selfout).astype(narrow)
+    d_sq, d_sk, d_sv = att_back(selfmix_grad, self_q, self_k, self_v, self_table, HT)
+    text_grad = project_input((d_sq, d_sk, d_sv), w_self) + self_sumgrad
+
+    small = spread_small(
+        (
+            jnp.stack([col_sum(d_sq), col_sum(d_sv)]),
+            jnp.stack([col_sum(d_tq), col_sum(d_tv)]),
+            jnp.stack([col_sum(d_iq), col_sum(d_iv)]),
+            col_sum(d_tin)[None],
+            col_sum(d_iin)[None],
+            jnp.stack([f_t0, f_t1, f_t2]),
+            jnp.stack([o_t0, o_t1, o_t2]),
+            jnp.stack([col_sum(b_self), col_sum(b_tco), col_sum(b_tff)]),
+            jnp.stack([f_i0, f_i1]),
+            jnp.stack([o_i0, o_i1]),
+            jnp.stack([col_sum(b_ico), col_sum(b_iff)]),
+        )
+    )
+    small = small.reshape(4, 2, SMALL_ROWS, 128).transpose(1, 0, 2, 3)
+    inputs = [
+        jnp.stack([by_owner(a) for a in (text, self_mixed, text_one, text_two)]),
+        jnp.stack([by_owner(a) for a in (image, text_mixed, image_mixed, image_two, image_active)]),
+        by_owner(text_active)[None],
+    ]
+    grads = [
+        jnp.concatenate((d_sq, d_sk, d_sv, b_self, d_tq, d_tk, d_tv, d_tin), axis=1),
+        jnp.concatenate((d_iq, d_ik, d_iv, b_tco, b_ico, d_iin, b_iff), axis=1),
+        b_tff,
+    ]
+    states = [a.astype(narrow).reshape(2, 128, -1) for a in (text_out, image_out, text_grad, image_grad)]
+    summed, small_sum, outputs = reduce_all(inputs, grads, small, states)
+
+    def columns(kind):
+        start = sum(CHUNKS[:kind])
+        part = summed[start : start + CHUNKS[kind]].reshape(-1, ROWS[kind], 128)
+        return part.transpose(1, 0, 2).reshape(ROWS[kind], -1).astype(wide)
+
+    flat = [columns(kind) for kind in range(3)]
+
+    def threefold(part):
+        return part.reshape(part.shape[0], 3, -1)
+
+    one, two = flat[0], flat[1]
+    s = unpack_small(small_sum[None], 1)
+    return tuple(outputs) + (
+        threefold(one[:, :2304]), s[0], one[:, 2304:3072], threefold(one[:, 3072:6144]), s[1],
+        threefold(two[:, :3072]), s[2], two[:, 3072:3840], two[:, 3840:4864],
+        one[:, 6144:], s[3], flat[2], two[:, 4864:5888], s[4].reshape(-1), two[:, 5888:],
+        s[5], s[6], s[7], s[8], s[9], s[10],
+    )
+
+
 def solution(mesh):
     in_specs = (
         P("dp", "seq", None),
@@ -550,4 +1301,6 @@
         P(None, "dp"),
         P(None, "dp"),
     )
+    sizes = mesh.shape
+    local = local_fast if (sizes["dp"], sizes["seq"]) == (8, 4) else local_plain
     return jax.shard_map(local, mesh=mesh, in_specs=in_specs, out_specs=out_specs, check_vma=False)

time: 2100 us -> 613 us (0.29)
  waiting for transfers between devices: 1540 us -> 0 us
  Pallas kernels: 0 us -> 326 us
  blocking collectives: 129 us -> 0 us
  matrix products: 190 us -> 104 us
  other arithmetic: 92.4 us -> 26.2 us
  local copies, waits for them, and re-layouts: 117 us -> 142 us
    reduce_scatter x15 -> x0, waiting for transfers between devices: 656 us -> none  [the longest x1 93.8 us: local(): lax.psum_scatter(gradients[5], 'dp', scatter_dimension=0, tiled=True)]
    all_gather x16 -> x0, waiting for transfers between devices: 375 us -> none  [the longest x2 46.2 us: micro_step(): lax.all_gather(text_triple[:, :, 1:], 'seq', axis=1, tiled=True)]
    unnamed x52 -> x0, waiting for transfers between devices: 357 us -> none
    pallas_call x0 -> x2, Pallas kernels: none -> 326 us  [the longest x1 179 us: reduce_all(): pl.pallas_call(reduce_kernel, out_shape=[jax.ShapeDtypeStruct((STEPS,) +...]
    psum x1 -> x0, waiting for transfers between devices: 147 us -> none  [local(): lax.psum(accumulated[0].astype(jnp.bfloat16), 'seq').astype(jnp.float32)]
    all_gather x11 -> x0, blocking collectives: 94.4 us -> none  [the longest x1 10.3 us: local(): lax.all_gather(shards[1], 'dp', axis=1, tiled=True)]
    dot_general x96 -> x47, matrix products: 190 us -> 102 us  [the longest x16 49.6 us: mm(): return jnp.dot(left, right, preferred_element_type=jnp.float32)]
    convert_element_type x45 -> x10, other arithmetic: 45.3 us -> 2.84 us  [the longest x5 1.57 us: local_fast(): a.astype(wide)]
  transfers between devices with their start and end apart: 42 -> 0, of which waited for: 38 -> 0; matrix products, arithmetic and copies ran while one was open for 16% -> 0% of each run, Pallas kernels for 0% -> 0%
where the time goes in v1:
time: 613 us; the launch traced here: 602 us
  Pallas kernels  326 us (53%)
  local copies, waits for them, and re-layouts  142 us (23%)
  matrix products  104 us (17%)
  other arithmetic  26.2 us (4%)
    pallas_call x1, Pallas kernels, reduce_all(): pl.pallas_call(reduce_kernel, out_shape=[jax.ShapeDtypeStruct((STEPS,) +...  179 us
    pallas_call x1, Pallas kernels, gather(): pl.pallas_call(functools.partial(gather_kernel, weight_count), out_shape=...  147 us
    unnamed x307, local copies, waits for them, and re-layouts  56.1 us
    dot_general x16, matrix products, mm(): return jnp.dot(left, right, preferred_element_type=jnp.float32)  49.6 us
    dot_general x16, matrix products, mm_t(): lax.dot_general(left, right, (((1,), (1,)), ((), ())), preferred_element_...  36.1 us

profile of v1, /device:TPU:0, one launch (start us, length us, event | category | flops | bytes accessed | tf_op | source)
XLA Modules:
  0.0 601.9 jit_solution(1599306164294879132)
XLA Ops:
  3.4 3.6 concatenate.21
  7.6 147.1 %gather.1 = (bf16[3,768,768]{2,1,0:T(8,128)(2,1)}, bf16[1,768,768]{2,1,0:T(8,128)(2,1)}, bf16[3,768,1024]{2,1,0:T(8,128)(2,1)}, bf16[3,1024,1024]{2,1,0:T(8,128)...) custom-call(bf16[3,96,768]{2,1,0:T(8,128)(2,1)} %bitcast.803, ...), custom_call_target="tpu_custom_call" | custom-call | tf_op jit(solution)/shard_map/gather/pallas_call | solution.py:646
  162.4 2.2 fusion.196
  169.5 2.1 fusion.201
  172.6 2.3 fusion.214
  176.5 2.1 fusion.230
  181.6 2.7 fusion.396
  184.7 4.1 fusion.248
  188.9 2.9 fusion.397
  194.0 3.8 convert_reduce_fusion.4
  206.2 3.5 fusion.51
  209.7 2.0 fusion.227
  212.3 2.5 fusion.220
  216.5 2.3 fusion.211
  222.7 2.2 fusion.392
  225.9 10.6 %fusion.16 = (bf16[3072,256]{0,1:T(8,128)(2,1)}, f32[256,3072]{1,0:T(8,128)S(1)}) fusion(f32[3072]{0:T(1024)S(1)} %reshape.593, bf16[1,768,3072]{2,1,0:T(8,128)(2,1)} %get-tuple-element.56, f32[256,768]{1,0:T(8,128)S(1)} %get-tuple-element.178, f32[768]{0:T(1024)S(1)} %add.333, f32[768]{0:T(1024)S(1)} %mul.457, f32[256]{0:T(256)S(1)} %fusion.336, ...), kind=kOutput, calls=%fused_computation.18 | convolution fusion | flops 1260847104 | bytes 10244096 | tf_op jit(solution)/shard_map/dot_general | solution.py:1054
  238.3 7.5 %fusion.17 = f32[256,3072]{1,0:T(8,128)} fusion(f32[256,3072]{1,0:T(8,128)S(1)} %get-tuple-element.186), kind=kLoop, calls=%fused_computation.19 | loop fusion | flops 48758784 | bytes 6291456 | tf_op jit(solution)/shard_map/erfc | solution.py:31
  245.8 5.7 fusion.398
  253.4 2.3 fusion.372
  255.8 5.6 convert_reduce_fusion
  268.8 3.3 fusion.115
  272.1 2.8 convert_reduce_fusion.5
  276.4 3.9 fusion.139
  283.6 3.1 fusion.70
  286.7 2.8 convert_reduce_fusion.7
  291.8 2.0 fusion.74
  293.8 2.4 multiply_reduce_fusion.8
  302.5 2.2 multiply_reduce_fusion
  319.0 2.0 bitcast_dynamic-update-slice_fusion
  327.2 2.0 copy.169
  332.9 2.0 constant_dynamic-update-slice_fusion.9
  343.4 5.2 reshape.579
  348.6 4.9 copy.142
  353.5 2.3 reshape.578
  355.8 2.0 copy.141
  358.8 2.3 reshape.577
  363.3 2.0 copy.138
  369.4 2.3 reshape.571
  371.6 2.0 copy.130
  382.7 179.0 %reduce_all.1 = (bf16[21,768,128]{2,1,0:T(8,128)(2,1)}, f32[32,128]{1,0:T(8,128)}, bf16[8,32,768]{2,1,0:T(8,128)(2,1)}, bf16[8,32,1024]{2,1,0:T(8,128)(2,1)}, bf...) custom-call(bf16[4,2,384,256]{3,2,1,0:T(8,128)(2,1)} %pad_maximum_fusion.refs_0_, ...), custom_call_target="tpu_custom_call" | custom-call | tf_op jit(solution)/shard_map/reduce_all/pallas_call | solution.py:976
  561.7 3.6 fusion.375
  567.9 4.0 copy.182
  571.9 2.7 slice.328
  574.6 3.0 copy.186
  577.6 2.5 fusion.376
  580.1 2.0 copy.188
  582.2 2.0 copy.190
  584.2 2.0 copy.191
  (485 shorter events, 129.1 us)
Async XLA Ops:
  165.7 6.0 copy-start.42
  169.2 127.1 %copy-start.84 = (f32[256]{0:T(256)}, f32[256]{0:T(256)S(1)}, u32[]{:S(2)}) copy-start(f32[256]{0:T(256)S(1)} %fusion.335) | copy-start | bytes 3076
  169.2 5.6 copy-start.80
  171.8 6.9 %copy-start.60 = (bf16[32,8,8,128]{3,2,1,0:T(8,128)(2,1)}, bf16[32,8,8,128]{3,2,1,0:T(8,128)(2,1)S(1)}, u32[]{:S(2)}) copy-start(bf16[32,8,8,128]{3,2,1,0:T(8,128)(2,1)S(1)} %copy.213) | copy-start | bytes 1572868
  181.6 7.2 %copy-start.22 = (bf16[2,128,8,128]{3,2,1,0:T(8,128)(2,1)}, bf16[2,128,8,128]{3,2,1,0:T(8,128)(2,1)S(1)}, u32[]{:S(2)}) copy-start(bf16[2,128,8,128]{3,2,1,0:T(8,128)(2,1)S(1)} %copy.137) | copy-start | bytes 1572868
  184.3 15.1 %copy-start.88 = (f32[256]{0:T(256)}, f32[256]{0:T(256)S(1)}, u32[]{:S(2)}) copy-start(f32[256]{0:T(256)S(1)} %broadcast_multiply_fusion.1) | copy-start | bytes 3076
  184.6 14.8 %copy-start.102 = (f32[256]{0:T(256)}, f32[256]{0:T(256)S(1)}, u32[]{:S(2)}) copy-start(f32[256]{0:T(256)S(1)} %fusion.337) | copy-start | bytes 3076
  204.9 4.8 copy-start.118
  206.2 5.6 copy-start.26
  212.3 6.7 %copy-start.20 = (bf16[2,128,8,128]{1,3,2,0:T(8,128)(2,1)}, bf16[2,128,8,128]{1,3,2,0:T(8,128)(2,1)S(1)}, u32[]{:S(2)}) copy-start(bf16[2,128,8,128]{1,3,2,0:T(8,128)(2,1)S(1)} %copy.174) | copy-start | bytes 1572868
  222.6 13.9 %copy-start.24 = (bf16[2,128,8,128]{3,2,1,0:T(8,128)(2,1)}, bf16[2,128,8,128]{3,2,1,0:T(8,128)(2,1)S(1)}, u32[]{:S(2)}) copy-start(bf16[2,128,8,128]{3,2,1,0:T(8,128)(2,1)S(1)} %copy.127) | copy-start | bytes 1572868
  224.9 38.3 %copy-start.86 = (f32[256]{0:T(256)}, f32[256]{0:T(256)S(1)}, u32[]{:S(2)}) copy-start(f32[256]{0:T(256)S(1)} %broadcast_multiply_fusion.3) | copy-start | bytes 3076
  225.7 37.5 %copy-start.90 = (f32[256]{0:T(256)}, f32[256]{0:T(256)S(1)}, u32[]{:S(2)}) copy-start(f32[256]{0:T(256)S(1)} %fusion.336) | copy-start | bytes 3076
  225.8 20.0 %copy-start.82 = (f32[768]{0:T(1024)}, f32[768]{0:T(1024)S(1)}, u32[]{:S(2)}) copy-start(f32[768]{0:T(1024)S(1)} %add.333) | copy-start | bytes 9220
  238.3 7.5 %copy-start.97 = (f32[8,96]{1,0:T(8,128)S(1)}, f32[8,96]{1,0:T(8,128)}, u32[]{:S(2)}) copy-start(f32[8,96]{1,0:T(8,128)} %get-tuple-element.218) | copy-start | bytes 9220
  245.8 6.0 copy-start.94
  245.8 7.5 %copy-start.96 = (f32[8,96]{1,0:T(8,128)S(1)}, f32[8,96]{1,0:T(8,128)}, u32[]{:S(2)}) copy-start(f32[8,96]{1,0:T(8,128)} %get-tuple-element.105) | copy-start | bytes 9220
  253.4 8.1 %slice-start = ((s8[4718592]{0:T(1024)(128)(4,1)}), s8[4194304]{0:T(1024)(128)(4,1)S(1)}, s32[]{:S(2)}) async-start(s8[4718592]{0:T(1024)(128)(4,1)} %bitcast.855), calls=%async_computation | async-start | bytes 8388608
  255.8 5.6 copy-start.53
  255.8 5.6 slice-start.1
  274.9 5.5 copy-start.17
  274.9 5.5 copy-start.64
  276.4 5.5 copy-start.15
  276.4 5.5 copy-start.19
  309.8 5.1 copy-start.100
  309.8 5.2 copy-start.116
  311.6 6.4 %copy-start.5 = (bf16[2,128,8,128]{3,2,1,0:T(8,128)(2,1)S(1)}, bf16[2,128,8,128]{3,2,1,0:T(8,128)(2,1)}, u32[]{:S(2)}) copy-start(bf16[2,128,8,128]{3,2,1,0:T(8,128)(2,1)} %copy-done.4) | copy-start | bytes 1572868
  315.3 7.4 %copy-start.35 = (bf16[256,1024]{1,0:T(8,128)(2,1)S(1)}, bf16[256,1024]{1,0:T(8,128)(2,1)}, u32[]{:S(2)}) copy-start(bf16[256,1024]{1,0:T(8,128)(2,1)} %copy-done.34) | copy-start | bytes 1572868
  315.4 8.3 %copy-start.38 = (bf16[256,1024]{1,0:T(8,128)(2,1)S(1)}, bf16[256,1024]{1,0:T(8,128)(2,1)}, u32[]{:S(2)}) copy-start(bf16[256,1024]{1,0:T(8,128)(2,1)} %copy-done.37) | copy-start | bytes 1572868
  315.4 9.2 %copy-start.33 = (bf16[256,1024]{1,0:T(8,128)(2,1)S(1)}, bf16[256,1024]{1,0:T(8,128)(2,1)}, u32[]{:S(2)}) copy-start(bf16[256,1024]{1,0:T(8,128)(2,1)} %copy-done.32) | copy-start | bytes 1572868
  318.0 7.4 %copy-start.12 = (bf16[2,128,12,64]{1,0,3,2:T(2,128)(2,1)S(1)}, bf16[2,128,12,64]{1,0,3,2:T(2,128)(2,1)}, u32[]{:S(2)}) copy-start(bf16[2,128,12,64]{1,0,3,2:T(2,128)(2,1)} %copy-done.11) | copy-start | bytes 1179652
  319.0 7.4 %copy-start.9 = (bf16[2,128,12,64]{1,0,3,2:T(2,128)(2,1)S(1)}, bf16[2,128,12,64]{1,0,3,2:T(2,128)(2,1)}, u32[]{:S(2)}) copy-start(bf16[2,128,12,64]{1,0,3,2:T(2,128)(2,1)} %copy-done.8) | copy-start | bytes 1179652
  326.4 12.9 %copy-start.3 = (bf16[2,128,8,128]{3,2,1,0:T(8,128)(2,1)S(1)}, bf16[2,128,8,128]{3,2,1,0:T(8,128)(2,1)}, u32[]{:S(2)}) copy-start(bf16[2,128,8,128]{3,2,1,0:T(8,128)(2,1)} %copy.147) | copy-start | bytes 1572868
  327.2 9.5 %copy-start.45 = (bf16[256,768]{1,0:T(8,128)(2,1)S(1)}, bf16[256,768]{1,0:T(8,128)(2,1)}, u32[]{:S(2)}) copy-start(bf16[256,768]{1,0:T(8,128)(2,1)} %copy.170) | copy-start | bytes 1179652
  332.9 7.3 %copy-start.28 = (bf16[2,128,8,128]{3,2,1,0:T(8,128)(2,1)S(1)}, bf16[2,128,8,128]{3,2,1,0:T(8,128)(2,1)}, u32[]{:S(2)}) copy-start(bf16[2,128,8,128]{3,2,1,0:T(8,128)(2,1)} %copy-done.27) | copy-start | bytes 1572868
  332.9 8.2 %copy-start.30 = (bf16[2,128,8,128]{3,2,1,0:T(8,128)(2,1)S(1)}, bf16[2,128,8,128]{3,2,1,0:T(8,128)(2,1)}, u32[]{:S(2)}) copy-start(bf16[2,128,8,128]{3,2,1,0:T(8,128)(2,1)} %copy-done.29) | copy-start | bytes 1572868
  332.9 9.2 %copy-start.41 = (bf16[256,3072]{1,0:T(8,128)(2,1)S(1)}, bf16[256,3072]{1,0:T(8,128)(2,1)}, u32[]{:S(2)}) copy-start(bf16[256,3072]{1,0:T(8,128)(2,1)} %copy-done.40) | copy-start | bytes 4718596
  348.6 9.1 %copy-start.89 = (f32[256]{0:T(256)S(1)}, f32[256]{0:T(256)}, u32[]{:S(2)}) copy-start(f32[256]{0:T(256)} %copy-done.88) | copy-start | bytes 3076
  348.6 9.1 %copy-start.93 = (f32[1,8,128]{2,0,1:T(1,128)S(1)}, f32[1,8,128]{2,0,1:T(1,128)}, u32[]{:S(2)}) copy-start(f32[1,8,128]{2,0,1:T(1,128)} %copy-done.92) | copy-start | bytes 12292
  348.6 9.1 %copy-start.103 = (f32[256]{0:T(256)S(1)}, f32[256]{0:T(256)}, u32[]{:S(2)}) copy-start(f32[256]{0:T(256)} %copy-done.102) | copy-start | bytes 3076
  353.5 8.9 %copy-start.23 = (bf16[2,128,8,128]{3,2,1,0:T(8,128)(2,1)S(1)}, bf16[2,128,8,128]{3,2,1,0:T(8,128)(2,1)}, u32[]{:S(2)}) copy-start(bf16[2,128,8,128]{3,2,1,0:T(8,128)(2,1)} %copy-done.22) | copy-start | bytes 1572868
  358.8 7.6 %copy-start.25 = (bf16[2,128,8,128]{3,2,1,0:T(8,128)(2,1)S(1)}, bf16[2,128,8,128]{3,2,1,0:T(8,128)(2,1)}, u32[]{:S(2)}) copy-start(bf16[2,128,8,128]{3,2,1,0:T(8,128)(2,1)} %copy-done.24) | copy-start | bytes 1572868
  369.4 9.8 %copy-start.31 = (bf16[2,4,128,256]{3,2,1,0:T(8,128)(2,1)S(1)}, bf16[2,4,128,256]{3,2,1,0:T(8,128)(2,1)}, u32[]{:S(2)}) copy-start(bf16[2,4,128,256]{3,2,1,0:T(8,128)(2,1)} %copy.141) | copy-start | bytes 1572868
  371.6 8.3 %copy-start.81 = (f32[768]{0:T(1024)S(1)}, f32[768]{0:T(1024)}, u32[]{:S(2)}) copy-start(f32[768]{0:T(1024)} %copy-done.80) | copy-start | bytes 9220
  371.6 8.3 %copy-start.85 = (f32[256]{0:T(256)S(1)}, f32[256]{0:T(256)}, u32[]{:S(2)}) copy-start(f32[256]{0:T(256)} %copy-done.84) | copy-start | bytes 3076
  591.7 7.4 %copy-start.70 = (bf16[8,32,1024]{2,1,0:T(8,128)(2,1)S(1)}, bf16[8,32,1024]{2,1,0:T(8,128)(2,1)}, u32[]{:S(2)}) copy-start(bf16[8,32,1024]{2,1,0:T(8,128)(2,1)} %get-tuple-element.251) | copy-start | bytes 1572868
  592.9 7.0 %copy-start.75 = (bf16[8,32,768]{2,1,0:T(8,128)(2,1)S(1)}, bf16[8,32,768]{2,1,0:T(8,128)(2,1)}, u32[]{:S(2)}) copy-start(bf16[8,32,768]{2,1,0:T(8,128)(2,1)} %get-tuple-element.252) | copy-start | bytes 1179652
  592.9 7.8 %copy-start.69 = (bf16[8,32,1024]{2,1,0:T(8,128)(2,1)S(1)}, bf16[8,32,1024]{2,1,0:T(8,128)(2,1)}, u32[]{:S(2)}) copy-start(bf16[8,32,1024]{2,1,0:T(8,128)(2,1)} %get-tuple-element.253) | copy-start | bytes 1572868
  (85 other events, 219.8 us)

commit v2 on v0

--- a/solution.py
+++ b/solution.py
@@ -1,6 +1,11 @@
+import functools
+import types
+
 import jax
 import jax.numpy as jnp
 from jax import lax
+from jax.experimental import pallas as pl
+from jax.experimental.pallas import tpu as pltpu
 from jax.sharding import PartitionSpec as P
 
 HT = 12
@@ -339,7 +344,7 @@
     return (outputs, gradients)
 
 
-def local(
+def local_plain(
     text,
     image,
     text_len,
@@ -493,6 +498,1269 @@
     return (text_out, image_out, text_grad, image_grad) + tuple(summed)
 
 
+MESH = pl.DeviceIdType.MESH
+ANY = pl.BlockSpec(memory_space=pl.ANY)
+VMEM = pl.BlockSpec(memory_space=pltpu.VMEM)
+
+
+def place():
+    dp = lax.axis_index("dp")
+    z = lax.axis_index("seq")
+    row = dp // 4
+    col = (dp // 2) % 2
+    core = dp % 2
+    return (dp, z, row, col, core)
+
+
+def partners(row, col, core, first_row):
+    near_row = row + first_row * (1 - 2 * row)
+    near_col = col + (1 - first_row) * (1 - 2 * col)
+    far_row = row + (1 - first_row) * (1 - 2 * row)
+    far_col = col + first_row * (1 - 2 * col)
+    near = near_row * 4 + near_col * 2 + core
+    far = far_row * 4 + far_col * 2 + core
+    return (near, far)
+
+
+def greet(devices):
+    barrier = pltpu.get_barrier_semaphore()
+    for device in devices:
+        pl.semaphore_signal(barrier, inc=1, device_id=device, device_id_type=MESH)
+    pl.semaphore_wait(barrier, len(devices))
+
+
+def remote(source, target, send_sem, recv_sem, device):
+    return pltpu.make_async_remote_copy(
+        src_ref=source,
+        dst_ref=target,
+        send_sem=send_sem,
+        recv_sem=recv_sem,
+        device_id=device,
+        device_id_type=MESH,
+    )
+
+
+SMALL_PLACES = (
+    (0, 2, 96),
+    (16, 2, 128),
+    (18, 2, 128),
+    (27, 3, 128),
+    (20, 1, 128),
+    (2, 3, 96),
+    (5, 3, 96),
+    (8, 3, 96),
+    (21, 2, 128),
+    (23, 2, 128),
+    (25, 2, 128),
+)
+SMALL_COUNT = len(SMALL_PLACES)
+SMALL_ROWS = 32
+ROOT_HALF = 0.7071067811865476
+ROOT_TURN = 0.3989422804014327
+WEIGHT_SHAPES = (
+    (3, 768, 768), (1, 768, 768), (3, 1024, 1024), (3, 768, 1024), (1, 1024, 768),
+    (1, 1024, 1024), (1, 768, 3072), (1, 3072, 768), (1, 1024, 1024), (1, 1024, 1024),
+)
+W_SELF, W_SELFOUT, W_IMAGECO, W_TEXTCO, W_TEXTOUT, W_IMAGEOUT, W_TIN, W_TOUT, W_IIN, W_IOUT, W_SMALL = range(11)
+SAVED = dict(
+    qkv_s=((3, 256, 768), jnp.bfloat16),
+    qkv_t=((3, 256, 1024), jnp.bfloat16),
+    qkv_i=((3, 256, 1024), jnp.bfloat16),
+    tab_s=((12, 256, 128), jnp.bfloat16),
+    tab_t=((16, 128, 128), jnp.bfloat16),
+    tab_i=((16, 128, 128), jnp.bfloat16),
+    sum_s=((256, 768), jnp.float32),
+    sum_t=((256, 768), jnp.float32),
+    sum_i=((256, 1024), jnp.float32),
+    tot_t=((256, 768), jnp.float32),
+    tot_i=((256, 1024), jnp.float32),
+    slope_t=((256, 3072), jnp.bfloat16),
+    slope_i=((256, 1024), jnp.bfloat16),
+    xt768=((4, 2, 384, 256), jnp.bfloat16),
+    xt1024=((5, 2, 512, 256), jnp.bfloat16),
+    xt3072=((1, 2, 1536, 256), jnp.bfloat16),
+    out_t=((256, 768), jnp.bfloat16),
+    out_i=((256, 1024), jnp.bfloat16),
+    vec96=((16, 768), jnp.float32),
+    vec128=((16, 1024), jnp.float32),
+)
+WORK = dict(
+    text=((2, 128, 768), jnp.bfloat16),
+    image=((2, 128, 1024), jnp.bfloat16),
+    mix_s=((256, 768), jnp.bfloat16),
+    one=((256, 768), jnp.bfloat16),
+    mix_t=((256, 1024), jnp.bfloat16),
+    mix_i=((256, 1024), jnp.bfloat16),
+    two_t=((256, 768), jnp.bfloat16),
+    two_i=((256, 1024), jnp.bfloat16),
+    bias_in=((8, 3072), jnp.float32),
+    pack=((SMALL_ROWS, 128), jnp.float32),
+)
+
+
+def mm(left, right):
+    return jnp.dot(left, right, preferred_element_type=jnp.float32)
+
+
+def mm_t(left, right):
+    return lax.dot_general(left, right, (((1,), (1,)), ((), ())), preferred_element_type=jnp.float32)
+
+
+def mm_0(left, right):
+    return lax.dot_general(left, right, (((0,), (0,)), ((), ())), preferred_element_type=jnp.float32)
+
+
+def lanes(index, width):
+    return pl.ds(pl.multiple_of(index * width, width), width)
+
+
+def head_masks():
+    spot = lax.broadcasted_iota(jnp.int32, (1, 128), 1)
+    low = jnp.where(spot < 64, 1.0, 0.0)
+    return (low, 1.0 - low)
+
+
+def key_mask(length):
+    return lax.broadcasted_iota(jnp.int32, (1, 128), 1) < length
+
+
+def table_of(scores, keep, shrink):
+    scores = jnp.where(keep, scores * shrink, NEG_FILL)
+    powers = jnp.exp(scores - jnp.max(scores, axis=-1, keepdims=True))
+    return (powers / jnp.sum(powers, axis=-1, keepdims=True)).astype(jnp.bfloat16)
+
+
+def forward_kernel(*refs):
+    refs = list(refs)
+
+    def take(count):
+        taken = refs[:count]
+        del refs[:count]
+        return taken
+
+    narrow, wide = jnp.bfloat16, jnp.float32
+    weight_count = len(WEIGHT_SHAPES)
+    array_count = weight_count + 1
+    blocks = take(weight_count)
+    small_in = take(SMALL_COUNT)
+    states = take(4)
+    text_len, region_count = take(2)
+    whole_out = take(weight_count)
+    saved_out = take(len(SAVED))
+    cots = take(2)
+    wholes = take(array_count)
+    saved_refs = take(len(SAVED))
+    saved = types.SimpleNamespace(**dict(zip(SAVED, saved_refs)))
+    work = types.SimpleNamespace(**dict(zip(WORK, take(len(WORK)))))
+    send_sem, recv_sem, swap_send, swap_recv, own_sem, out_sem, save_sem = refs
+    dp, z, row, col, core = place()
+    near, far = partners(row, col, core, 1 - core)
+    sibling = dp + 1 - 2 * core
+    diagonal = (1 - row) * 4 + (1 - col) * 2 + core
+    others = [lax.rem(z + step, 4) for step in (1, 2, 3)]
+
+    pack = work.pack
+    pack[...] = jnp.zeros((SMALL_ROWS, 128), wide)
+    for (first, rows, width), ref in zip(SMALL_PLACES, small_in):
+        pack[first : first + rows, :width] = ref[...].astype(wide)
+    sources = blocks + [pack]
+
+    greet([(near, z), (far, z), (sibling, z)] + [(dp, other) for other in others])
+
+    def rows_of(whole, index):
+        depth = whole.shape[1] // 8
+        return whole.at[:, pl.ds(pl.multiple_of(index * depth, 16), depth), :]
+
+    def own(array):
+        source = sources[array]
+        return source if array < weight_count else source.reshape(1, SMALL_ROWS, 128)
+
+    def copy_of(array, lane, source, index, device):
+        return remote(
+            source, rows_of(wholes[array], index), send_sem.at[array, lane], recv_sem.at[array, lane], (device, z)
+        )
+
+    sent = {}
+
+    def send(array, lane, source, index, device):
+        copy = copy_of(array, lane, source, index, device)
+        copy.start()
+        sent[array, lane] = copy
+
+    kept = {}
+
+    def start(array):
+        send(array, 0, own(array), dp, near)
+        send(array, 1, own(array), dp, far)
+        send(array, 2, own(array), dp, sibling)
+        kept[array] = pltpu.make_async_copy(own(array), rows_of(wholes[array], dp), own_sem.at[array])
+        kept[array].start()
+
+    def relay(array):
+        sent[array, 0].wait_recv()
+        arrived = rows_of(wholes[array], near)
+        send(array, 3, arrived, near, far)
+        send(array, 4, arrived, near, sibling)
+        sent[array, 1].wait_recv()
+        send(array, 5, rows_of(wholes[array], far), far, sibling)
+
+    def pass_on(array):
+        sent[array, 3].wait_recv()
+        send(array, 6, rows_of(wholes[array], diagonal), diagonal, sibling)
+
+    outs = []
+
+    def ready(array):
+        for lane in (2, 4, 5, 6):
+            sent[array, lane].wait_recv()
+        kept[array].wait()
+        if array < weight_count:
+            copy = pltpu.make_async_copy(wholes[array], whole_out[array], out_sem.at[array])
+            copy.start()
+            outs.append(copy)
+
+    def save(ref):
+        spot = [ref is other for other in saved_refs].index(True)
+        copy = pltpu.make_async_copy(ref, saved_out[spot], save_sem.at[spot])
+        copy.start()
+        outs.append(copy)
+
+    swaps = []
+
+    def swap(array, target):
+        source = states[array]
+        count = source.shape[0] // 4
+        slots = source.shape[1]
+        here = target.at[:, pl.ds(pl.multiple_of(z * slots, 16), slots), :]
+        made = []
+        for step, other in enumerate(others):
+            copy = remote(
+                source.at[pl.ds(other * count, count)],
+                here,
+                swap_send.at[array, step],
+                swap_recv.at[array, step],
+                (dp, other),
+            )
+            copy.start()
+            made.append(copy)
+        keep = pltpu.make_async_copy(source.at[pl.ds(z * count, count)], here, own_sem.at[array_count + array])
+        keep.start()
+        made.append(keep)
+        return made
+
+    order = (W_SMALL, W_SELF, W_SELFOUT, W_IMAGECO, W_TEXTCO, W_TEXTOUT, W_IMAGEOUT, W_TIN, W_TOUT, W_IIN, W_IOUT)
+    progress = [0, 0, 0, 0]
+
+    def advance(started, relayed, passed, completed):
+        while progress[0] < min(started, len(order)):
+            start(order[progress[0]])
+            progress[0] += 1
+        while progress[1] < min(relayed, len(order)):
+            relay(order[progress[1]])
+            progress[1] += 1
+        while progress[2] < min(passed, len(order)):
+            pass_on(order[progress[2]])
+            progress[2] += 1
+        while progress[3] < min(completed, len(order)):
+            ready(order[progress[3]])
+            progress[3] += 1
+
+    def upto(array):
+        at = order.index(array) + 1
+        advance(at + 3, 0, 0, 0)
+        advance(at + 3, at + 1, at, at)
+
+    text_in = swap(0, work.text)
+    advance(2, 0, 0, 0)
+    image_in = swap(1, work.image)
+    advance(4, 0, 0, 0)
+    swaps += swap(2, cots[0]) + swap(3, cots[1])
+
+    vec96, vec128, bias_in = saved.vec96, saved.vec128, work.bias_in
+
+    def flip(values, width, target, which, first_block):
+        turned = values.T
+        for block in range(values.shape[1] // width):
+            owner = first_block + block
+            target[which, owner % 2, owner // 2 * width : (owner // 2 + 1) * width, :] = turned[
+                block * width : (block + 1) * width
+            ]
+
+    def norm_rows(source, gain, shift, targets):
+        def body(step, carry):
+            window = pl.ds(pl.multiple_of(step * 32, 32), 32)
+            hidden = source[window, :]
+            centre = hidden - jnp.mean(hidden, axis=-1, keepdims=True)
+            spread = jnp.mean(centre * centre, axis=-1, keepdims=True)
+            result = centre * lax.rsqrt(spread + EPSILON) * gain + shift
+            targets[window, :] = result.astype(narrow)
+            return carry
+
+        lax.fori_loop(0, 8, body, 0)
+
+    def project_all(inputs, array, target, biases):
+        width = target.shape[2]
+        for k in range(3):
+
+            def body(tile, carry, k=k):
+                where = lanes(tile, 256)
+                part = mm(inputs, wholes[array][k, :, where])
+                if k == 0:
+                    part = part + biases[0][:, where]
+                if k == 2:
+                    part = part + biases[1][:, where]
+                target[k, :, where] = part.astype(narrow)
+                return carry
+
+            lax.fori_loop(0, width // 256, body, 0)
+
+    def branch(inputs, array, base, bias, target):
+        width = target.shape[1]
+
+        def body(tile, carry):
+            where = lanes(tile, 256)
+            part = mm(inputs, wholes[array][0, :, where])
+            target[:, where] = part + base[..., where].reshape(256, 256).astype(wide) + bias[:, where]
+            return carry
+
+        lax.fori_loop(0, width // 256, body, 0)
+
+    class Row:
+        def __init__(self, ref, index):
+            self.ref, self.index = ref, index
+
+        def __getitem__(self, key):
+            return self.ref[self.index : self.index + 1, key[1]]
+
+    upto(W_SMALL)
+    packed = wholes[W_SMALL]
+    for owner in range(8):
+        base = owner * SMALL_ROWS
+        vec96[:, owner * 96 : owner * 96 + 96] = packed[0, base : base + 16, :96]
+        vec128[:, owner * 128 : owner * 128 + 128] = packed[0, base + 16 : base + 32, :]
+        for part in range(3):
+            at = owner * 384 + part * 128
+            bias_in[0:1, at : at + 128] = packed[0, base + 27 + part : base + 28 + part, :]
+    save(saved.vec96)
+    save(saved.vec128)
+    text_lengths = [text_len[z * 2 + pair] for pair in range(2)]
+    region_counts = [region_count[z * 2 + pair] for pair in range(2)]
+    low, high = head_masks()
+    low_narrow, high_narrow = low.astype(narrow), high.astype(narrow)
+
+    for copy in text_in:
+        copy.wait()
+    upto(W_SELF)
+    text = work.text[...].reshape(256, 768)
+    qkv_s = saved.qkv_s
+    project_all(text, W_SELF, qkv_s, (Row(vec96, 0), Row(vec96, 1)))
+    save(saved.qkv_s)
+
+    def self_heads(tile, carry):
+        where = lanes(tile, 128)
+        for pair in range(2):
+            rows = slice(pair * 128, pair * 128 + 128)
+            q2, k2, v2 = (qkv_s[k, rows, where] for k in range(3))
+            both = jnp.concatenate([q2 * low_narrow, q2 * high_narrow], axis=0)
+            table = table_of(mm_t(both, k2), key_mask(text_lengths[pair]), 0.125)
+            saved.tab_s[pair * 6 + tile] = table
+            mixed = mm(table, v2)
+            work.mix_s[rows, where] = (mixed[:128] * low + mixed[128:] * high).astype(narrow)
+        return carry
+
+    lax.fori_loop(0, 6, self_heads, 0)
+    save(saved.tab_s)
+    flip(text, 96, saved.xt768, 0, 0)
+    flip(work.mix_s[...], 96, saved.xt768, 1, 0)
+    upto(W_SELFOUT)
+    branch(work.mix_s[...], W_SELFOUT, work.text, Row(vec96, 8), saved.sum_s)
+    norm_rows(saved.sum_s, vec96[2:3], vec96[5:6], work.one)
+    save(saved.sum_s)
+    flip(work.one[...], 96, saved.xt768, 2, 0)
+
+    for copy in image_in:
+        copy.wait()
+    upto(W_IMAGECO)
+    image = work.image[...].reshape(256, 1024)
+    qkv_i, qkv_t = saved.qkv_i, saved.qkv_t
+    project_all(image, W_IMAGECO, qkv_i, (Row(vec128, 2), Row(vec128, 3)))
+    save(saved.qkv_i)
+    flip(image, 128, saved.xt1024, 0, 0)
+    upto(W_TEXTCO)
+    project_all(work.one[...], W_TEXTCO, qkv_t, (Row(vec128, 0), Row(vec128, 1)))
+    save(saved.qkv_t)
+
+    def co_heads(head, carry):
+        where = lanes(head, 128)
+        shrink = 128**-0.5
+        for pair in range(2):
+            rows = slice(pair * 128, pair * 128 + 128)
+            tq, tk, tv = (qkv_t[k, rows, where] for k in range(3))
+            iq, ik, iv = (qkv_i[k, rows, where] for k in range(3))
+            table = table_of(mm_t(tq, ik), key_mask(region_counts[pair]), shrink)
+            saved.tab_t[pair * 8 + head] = table
+            work.mix_t[rows, where] = mm(table, iv).astype(narrow)
+            table = table_of(mm_t(iq, tk), key_mask(text_lengths[pair]), shrink)
+            saved.tab_i[pair * 8 + head] = table
+            work.mix_i[rows, where] = mm(table, tv).astype(narrow)
+        return carry
+
+    lax.fori_loop(0, 8, co_heads, 0)
+    save(saved.tab_t)
+    save(saved.tab_i)
+    flip(work.mix_t[...], 128, saved.xt1024, 1, 0)
+    flip(work.mix_i[...], 128, saved.xt1024, 2, 0)
+    upto(W_TEXTOUT)
+    branch(work.mix_t[...], W_TEXTOUT, work.one, Row(vec96, 9), saved.sum_t)
+    norm_rows(saved.sum_t, vec96[3:4], vec96[6:7], work.two_t)
+    save(saved.sum_t)
+    flip(work.two_t[...], 96, saved.xt768, 3, 0)
+    save(saved.xt768)
+    upto(W_IMAGEOUT)
+    branch(work.mix_i[...], W_IMAGEOUT, work.image, Row(vec128, 9), saved.sum_i)
+    norm_rows(saved.sum_i, vec128[5:6], vec128[7:8], work.two_i)
+    save(saved.sum_i)
+    flip(work.two_i[...], 128, saved.xt1024, 3, 0)
+
+    def activate(inner):
+        share = 0.5 + 0.5 * lax.erf(inner * ROOT_HALF)
+        slope = share + inner * (ROOT_TURN * jnp.exp(-0.5 * inner * inner))
+        return ((inner * share).astype(narrow), slope.astype(narrow))
+
+    upto(W_TIN)
+    upto(W_TOUT)
+    two_t = work.two_t
+    tot_t = saved.tot_t
+    tot_t[...] = two_t[...].astype(wide) + vec96[10:11]
+
+    def text_inner(owner, carry):
+        where = lanes(owner, 384)
+        inner = mm(two_t[...], wholes[W_TIN][0, :, where]) + bias_in[0:1, where]
+        active, slope = activate(inner)
+        saved.slope_t[:, where] = slope
+        saved.xt3072[0, lax.rem(owner, 2), pl.ds(pl.multiple_of(lax.div(owner, 2) * 384, 384), 384), :] = active.T
+        tot_t[...] += mm(active, wholes[W_TOUT][0, where, :])
+        return carry
+
+    lax.fori_loop(0, 8, text_inner, 0)
+    save(saved.slope_t)
+    save(saved.xt3072)
+    save(saved.tot_t)
+    norm_rows(tot_t, vec96[4:5], vec96[7:8], saved.out_t)
+    save(saved.out_t)
+
+    upto(W_IIN)
+    two_i = work.two_i
+    tot_i = saved.tot_i
+    for part in range(4):
+        where = slice(part * 256, part * 256 + 256)
+        inner = mm(two_i[...], wholes[W_IIN][0, :, where]) + vec128[4:5, where]
+        active, slope = activate(inner)
+        saved.slope_i[:, where] = slope
+        flip(active, 128, saved.xt1024, 4, part * 2)
+        work.mix_i[:, where] = active
+    save(saved.slope_i)
+    save(saved.xt1024)
+    upto(W_IOUT)
+    branch(work.mix_i[...], W_IOUT, two_i, Row(vec128, 10), tot_i)
+    save(saved.tot_i)
+    norm_rows(tot_i, vec128[6:7], vec128[8:9], saved.out_i)
+    save(saved.out_i)
+
+    for copy in sent.values():
+        copy.wait_send()
+    for copy in swaps:
+        copy.wait()
+    for copy in outs:
+        copy.wait()
+
+
+def forward_all(blocks, small, states, text_len, region_count):
+    dma = pltpu.SemaphoreType.DMA
+    narrow = jnp.bfloat16
+    count = len(WEIGHT_SHAPES)
+    shape = jax.ShapeDtypeStruct
+    out_shape = [shape(w, narrow) for w in WEIGHT_SHAPES]
+    out_shape += [shape(dims, kind) for dims, kind in SAVED.values()]
+    out_shape += [shape((s.shape[0] // 4, s.shape[1] * 4, s.shape[2]), s.dtype) for s in states[2:]]
+    scratch = [pltpu.VMEM(w, narrow) for w in WEIGHT_SHAPES]
+    scratch += [pltpu.VMEM((1, 8 * SMALL_ROWS, 128), jnp.float32)]
+    scratch += [pltpu.VMEM(dims, kind) for dims, kind in (*SAVED.values(), *WORK.values())]
+    scratch += [
+        dma((count + 1, 7)),
+        dma((count + 1, 7)),
+        dma((4, 3)),
+        dma((4, 3)),
+        dma((count + 5,)),
+        dma((count,)),
+        dma((len(SAVED),)),
+    ]
+    results = pl.pallas_call(
+        forward_kernel,
+        out_shape=out_shape,
+        in_specs=[ANY] * count
+        + [VMEM] * SMALL_COUNT
+        + [ANY] * 4
+        + [pl.BlockSpec(memory_space=pltpu.SMEM)] * 2,
+        out_specs=[ANY] * len(out_shape),
+        scratch_shapes=scratch,
+        compiler_params=pltpu.CompilerParams(
+            collective_id=0, has_side_effects=True, vmem_limit_bytes=62 * 2**20
+        ),
+        name="forward_all",
+    )(*blocks, *small, *states, text_len, region_count)
+    wholes = results[:count]
+    saved = types.SimpleNamespace(**dict(zip(SAVED, results[count : count + len(SAVED)])))
+    return (wholes, saved, results[count + len(SAVED) :])
+
+
+CHUNKS = (9, 9, 3)
+TILES = (4, 3, 1)
+ROWS = (96, 128, 384)
+STARTS = ((9, 12, 24), (12, 15, 19, 23), ())
+ORDER = ((2, 0, 3), (0, 6, 3), (1, 4, 5), (0, 3, 3), (1, 0, 4), (0, 0, 3))
+STEPS = 21
+LAG_NEAR, LAG_FAR, LAG_SUM, LAG_MID, LAG_END, LAG_WRITE = 1, 3, 5, 7, 9, 11
+SMALL_TURN = 18
+CHIP_SLOTS, NEAR_SLOTS, PLANE_SLOTS = 7, 9, 9
+AT_BSELF, AT_TEXTCO, AT_TIN = 2304, 3072, 6144
+AT_BTEXT, AT_BIMAGE, AT_IIN, AT_BIFF = 3072, 3840, 4864, 5888
+
+
+def backward_kernel(*refs):
+    refs = list(refs)
+
+    def take(count):
+        taken = refs[:count]
+        del refs[:count]
+        return taken
+
+    narrow, wide = jnp.bfloat16, jnp.float32
+    weights = take(len(WEIGHT_SHAPES))
+    saved = types.SimpleNamespace(**dict(zip(SAVED, take(len(SAVED)))))
+    cot_t, cot_i = take(2)
+    result, small_result = take(2)
+    pairs = take(4)
+    out_box, chip, near_sum, plane, line, cross = take(6)
+    s_own, s_chip, s_near, s_plane, s_line, s_cross = take(6)
+    w_p, w_q, w_i, w_o = take(4)
+    dz768, dz1024, dz3072 = take(3)
+    xt = take(3)
+    tab_s, tab_t, tab_i, sum_s, sum_t, sum_i, tot_t, tot_i, vec96, vec128 = take(10)
+    mix_t, mix_i, back_t, back_i, sums96, sums128, sums_in = take(7)
+    (
+        core_send, core_recv, near_send, near_recv, far_send, far_recv,
+        end_send, end_recv, mid_send, mid_recv, back_send, back_recv,
+        write_sem, swap_send, swap_recv, own_sem, load_sem,
+    ) = refs
+    dp, z, row, col, core = place()
+    near, far = partners(row, col, core, core)
+    sibling = dp + 1 - 2 * core
+    others = [lax.rem(z + step, 4) for step in (1, 2, 3)]
+    near_bit = col + core * (row - col)
+    far_bit = row + core * (col - row)
+
+    def block_of(near_index, far_index):
+        return near_index * (1 + core) + far_index * (2 - core)
+
+    is_end = (z == 0) | (z == 3)
+    is_mid = (z == 1) | (z == 2)
+    middle = 1 + z // 2
+    other_mid = 3 - z
+    end = 3 * (z // 2)
+
+    def span(ref, first, width):
+        return ref.at[:, first : first + width]
+
+    loads = []
+
+    def load(*moves):
+        made = []
+        for source, target in moves:
+            copy = pltpu.make_async_copy(source, target, load_sem.at[len(loads)])
+            loads.append(copy)
+            made.append(copy)
+        return made
+
+    def begin(group):
+        for copy in group:
+            copy.start()
+
+    def finish(group):
+        for copy in group:
+            copy.wait()
+
+    get_text3 = load(
+        (saved.tot_t, tot_t),
+        (cot_t.reshape(256, 768), span(dz768, AT_BSELF, 768)),
+        (saved.vec96, vec96),
+        *((weights[W_TOUT].at[0, pl.ds(i * 768, 768), :], w_q.at[i]) for i in range(4)),
+    )
+    get_text_in = load(
+        (saved.xt3072, xt[2]),
+        (saved.xt768, xt[0]),
+        (saved.slope_t, span(dz768, AT_TIN, 3072)),
+        *((weights[W_TIN].at[0, :, pl.ds(i * 1024, 1024)], w_p.at[i]) for i in range(3)),
+    )
+    get_image = load(
+        (saved.tot_i, tot_i),
+        (cot_i.reshape(256, 1024), span(dz1024, AT_BIMAGE, 1024)),
+        (saved.vec128, vec128),
+        (weights[W_IOUT].at[0], w_i.at[0]),
+        (saved.slope_i, span(dz1024, AT_IIN, 1024)),
+        (weights[W_IIN].at[0], w_i.at[1]),
+    )
+    get_co = load(
+        (saved.sum_t, sum_t),
+        (weights[W_TEXTOUT].at[0], w_o),
+        (saved.sum_i, sum_i),
+        (weights[W_IMAGEOUT].at[0], w_i.at[2]),
+    )
+    get_heads = load(
+        (saved.xt1024, xt[1]),
+        *((saved.qkv_t.at[k], span(dz768, AT_TEXTCO + k * 1024, 1024)) for k in range(3)),
+        *((saved.qkv_i.at[k], span(dz1024, k * 1024, 1024)) for k in range(3)),
+        (saved.tab_t, tab_t),
+        (saved.tab_i, tab_i),
+    )
+    get_self = load(
+        (saved.sum_s, sum_s),
+        *((saved.qkv_s.at[k], span(dz768, k * 768, 768)) for k in range(3)),
+        (saved.tab_s, tab_s),
+    )
+    get_textco = load((weights[W_TEXTCO], w_p))
+    get_selfs = load((weights[W_SELF], w_q.at[pl.ds(0, 3)]), (weights[W_SELFOUT].at[0], w_q.at[3]))
+    get_imageco = load((weights[W_IMAGECO], w_i))
+    for group in (get_text3, get_text_in, get_image, get_co, get_heads, get_self):
+        begin(group)
+    sums96[...] = jnp.zeros((16, 768), wide)
+    sums128[...] = jnp.zeros((16, 1024), wide)
+    s_own[...] = jnp.zeros((2, 4, SMALL_ROWS, 128), wide)
+
+    greet([(near, z), (far, z), (sibling, z)] + [(dp, other) for other in others])
+
+    def swap(array, source):
+        target = pairs[array]
+        count, slots = source.shape[0], source.shape[1] // 4
+        there = target.at[pl.ds(z * count, count)]
+
+        def part(other):
+            return source.at[:, pl.ds(pl.multiple_of(other * slots, 16), slots), :]
+
+        made = [
+            remote(part(other), there, swap_send.at[array, step], swap_recv.at[array, step], (dp, other))
+            for step, other in enumerate(others)
+        ]
+        made.append(pltpu.make_async_copy(part(z), there, own_sem.at[array]))
+        return made
+
+    swaps = [
+        swap(0, saved.out_t.reshape(2, 128, 768)),
+        swap(1, saved.out_i.reshape(2, 128, 1024)),
+        swap(2, back_t),
+        swap(3, back_i),
+    ]
+    begin(swaps[0] + swaps[1])
+
+    grads = (dz768, dz1024, dz3072)
+
+    def products(index, half, use):
+        place_ = 0
+        for kind in range(3):
+            chunk, chosen = 0, False
+            first = 0
+            for kind_, start, count in ORDER:
+                if kind_ == kind:
+                    inside = (index >= first) & (index < first + count)
+                    chunk = jnp.where(inside, index - first + start, chunk)
+                    chosen = chosen | inside
+                first += count
+
+            def work(kind=kind, chunk=chunk):
+                tiles, rows = TILES[kind], ROWS[kind]
+                for tile in range(tiles):
+                    which = chunk * tiles + tile
+                    weight = 0
+                    for bound in STARTS[kind]:
+                        weight = weight + jnp.where(which >= bound, 1, 0)
+                    part = mm(xt[kind][weight, half], grads[kind][:, lanes(which, 256)])
+                    for block in range(4):
+                        for side in range(2):
+                            use(
+                                block,
+                                (tile * 2 + side) * rows,
+                                rows,
+                                part[block * rows : (block + 1) * rows, side * 128 : side * 128 + 128],
+                            )
+
+            pl.when(chosen)(work)
+
+    def core_copy(index):
+        return remote(
+            out_box.at[lax.rem(index, 2)],
+            chip.at[lax.rem(index, CHIP_SLOTS)],
+            core_send.at[index],
+            core_recv.at[index],
+            (sibling, z),
+        )
+
+    def near_copy(index, far_index):
+        return remote(
+            chip.at[lax.rem(index, CHIP_SLOTS), block_of(1 - near_bit, far_index)],
+            near_sum.at[lax.rem(index, NEAR_SLOTS), far_index],
+            near_send.at[index, far_index],
+            near_recv.at[index, far_index],
+            (near, z),
+        )
+
+    def far_copy(index):
+        return remote(
+            near_sum.at[lax.rem(index, NEAR_SLOTS), 1 - far_bit],
+            plane.at[lax.rem(index, PLANE_SLOTS)],
+            far_send.at[index],
+            far_recv.at[index],
+            (far, z),
+        )
+
+    def end_copy(index):
+        return remote(
+            plane.at[lax.rem(index, PLANE_SLOTS)], line.at[index], end_send.at[index], end_recv.at[index], (dp, middle)
+        )
+
+    def mid_copy(index):
+        return remote(line.at[index], cross.at[index], mid_send.at[index], mid_recv.at[index], (dp, other_mid))
+
+    def back_copy(index):
+        return remote(cross.at[index], line.at[index], back_send.at[index], back_recv.at[index], (dp, end))
+
+    def mid_write(index):
+        return pltpu.make_async_copy(cross.at[index], result.at[index], write_sem.at[index])
+
+    def end_write(index):
+        return pltpu.make_async_copy(line.at[index], result.at[index], write_sem.at[index])
+
+    def add(left, right):
+        return (left.astype(wide) + right.astype(wide)).astype(narrow)
+
+    def stage_core(index):
+        @pl.when(index >= 2)
+        def _():
+            core_copy(index - 2).wait_send()
+
+        slot = lax.rem(index, 2)
+
+        def put(block, first, rows, values):
+            out_box[slot, block, first : first + rows, :] = values.astype(narrow)
+
+        products(index, 1 - core, put)
+        core_copy(index).start()
+
+    def stage_near(index):
+        core_copy(index).wait_recv()
+        slot = lax.rem(index, CHIP_SLOTS)
+
+        def put(block, first, rows, values):
+            window = (slot, block, slice(first, first + rows), slice(None))
+            chip[window] = (chip[window].astype(wide) + values).astype(narrow)
+
+        products(index, core, put)
+        near_copy(index, 1 - far_bit).start()
+        near_copy(index, far_bit).start()
+
+    def stage_far(index):
+        chip_slot, slot = lax.rem(index, CHIP_SLOTS), lax.rem(index, NEAR_SLOTS)
+        for far_index in (1 - far_bit, far_bit):
+            near_copy(index, far_index).wait_recv()
+            near_sum[slot, far_index] = add(near_sum[slot, far_index], chip[chip_slot, block_of(near_bit, far_index)])
+            if far_index is not far_bit:
+                far_copy(index).start()
+        near_copy(index, 0).wait_send()
+        near_copy(index, 1).wait_send()
+
+    def stage_sum(index):
+        slot = lax.rem(index, PLANE_SLOTS)
+        far_copy(index).wait_recv()
+        plane[slot] = add(plane[slot], near_sum[lax.rem(index, NEAR_SLOTS), far_bit])
+
+        @pl.when(is_end)
+        def _():
+            end_copy(index).start()
+
+        far_copy(index).wait_send()
+
+    def stage_mid(index):
+        @pl.when(is_mid)
+        def _():
+            end_copy(index).wait_recv()
+            line[index] = add(line[index], plane[lax.rem(index, PLANE_SLOTS)])
+            mid_copy(index).start()
+
+        @pl.when(is_end)
+        def _():
+            end_copy(index).wait_send()
+
+    def stage_end(index):
+        @pl.when(is_mid)
+        def _():
+            mid_copy(index).wait_recv()
+            cross[index] = add(cross[index], line[index])
+            back_copy(index).start()
+            mid_write(index).start()
+
+    def stage_write(index):
+        @pl.when(is_end)
+        def _():
+            back_copy(index).wait_recv()
+            end_write(index).start()
+
+    stages = (
+        (stage_core, 0),
+        (stage_near, LAG_NEAR),
+        (stage_far, LAG_FAR),
+        (stage_sum, LAG_SUM),
+        (stage_mid, LAG_MID),
+        (stage_end, LAG_END),
+        (stage_write, LAG_WRITE),
+    )
+
+    last = STEPS
+    sm_core = remote(s_own.at[1 - core], s_chip, core_send.at[last], core_recv.at[last], (sibling, z))
+    sm_near = [
+        remote(
+            s_chip.at[block_of(1 - near_bit, j)], s_near.at[j], near_send.at[last, j], near_recv.at[last, j], (near, z)
+        )
+        for j in (0, 1)
+    ]
+    sm_far = remote(s_near.at[1 - far_bit], s_plane, far_send.at[last], far_recv.at[last], (far, z))
+    sm_end = remote(s_plane, s_line, end_send.at[last], end_recv.at[last], (dp, middle))
+    sm_mid = remote(s_line, s_cross, mid_send.at[last], mid_recv.at[last], (dp, other_mid))
+    sm_back = remote(s_cross, s_line, back_send.at[last], back_recv.at[last], (dp, end))
+
+    def small_start():
+        for owner in range(8):
+            spot = s_own.at[owner % 2, owner // 2]
+            spot[0:16, :96] = sums96[:, owner * 96 : owner * 96 + 96]
+            spot[16:27, :] = sums128[0:11, owner * 128 : owner * 128 + 128]
+            for part in range(3):
+                at = owner * 384 + part * 128
+                spot[27 + part : 28 + part, :] = sums_in[0:1, at : at + 128]
+        sm_core.start()
+
+    def small_near():
+        sm_core.wait_recv()
+        s_chip[...] += s_own[core]
+        begin(sm_near)
+
+    def small_far():
+        for j in (0, 1):
+            sm_near[j].wait_recv()
+            s_near[j] += s_chip[block_of(near_bit, j)]
+        sm_far.start()
+
+    def small_sum():
+        sm_far.wait_recv()
+        s_plane[...] += s_near[far_bit]
+        pl.when(is_end)(sm_end.start)
+
+    def small_mid():
+        @pl.when(is_mid)
+        def _():
+            sm_end.wait_recv()
+            s_line[...] += s_plane[...]
+            sm_mid.start()
+
+    def small_end():
+        @pl.when(is_mid)
+        def _():
+            sm_mid.wait_recv()
+            s_cross[...] += s_line[...]
+            sm_back.start()
+            small_result[...] = s_cross[...]
+
+    def small_write():
+        @pl.when(is_end)
+        def _():
+            sm_back.wait_recv()
+            small_result[...] = s_line[...]
+
+    def norm_step(source, upstream, gain, target, first, sums, rows):
+        width = source.shape[1]
+
+        def body(step, carry):
+            window = pl.ds(pl.multiple_of(step * 32, 32), 32)
+            hidden = source[window, :]
+            dy = upstream[window, first[0] : first[0] + width].astype(wide)
+            centre = hidden - jnp.mean(hidden, axis=-1, keepdims=True)
+            spread = jnp.mean(centre * centre, axis=-1, keepdims=True)
+            scale = lax.rsqrt(spread + EPSILON)
+            unit = centre * scale
+            inner = dy * gain
+            back = scale * (
+                inner
+                - jnp.mean(inner, axis=-1, keepdims=True)
+                - unit * jnp.mean(inner * unit, axis=-1, keepdims=True)
+            )
+            rounded = back.astype(narrow)
+            source[window, :] = back
+            target[window, first[1] : first[1] + width] = rounded
+            parts = (dy * unit, dy, rounded.astype(wide))
+            return tuple(c + p.reshape(4, 8, width).sum(axis=0) for c, p in zip(carry, parts))
+
+        zero = jnp.zeros((8, width), wide)
+        totals = lax.fori_loop(0, 8, body, (zero, zero, zero))
+        for at, total in zip(rows, totals):
+            sums[at : at + 1, :] = jnp.sum(total, axis=0, keepdims=True)
+
+    def col_sum(values):
+        return jnp.sum(values.astype(wide), axis=0, keepdims=True)
+
+    def text_three():
+        finish(get_text3)
+        norm_step(tot_t, dz768, vec96[4:5], dz3072, (AT_BSELF, 0), sums96, (4, 7, 10))
+
+    def text_inner(turn):
+        for part in range(4):
+            which = turn * 4 + part
+            where = pl.ds(pl.multiple_of(AT_TIN + which * 256, 256), 256)
+            out_rows = w_q[lax.div(which, 3), pl.ds(pl.multiple_of(lax.rem(which, 3) * 256, 256), 256), :]
+            inner = (dz768[:, where].astype(wide) * mm_t(dz3072[...], out_rows)).astype(narrow)
+            dz768[:, where] = inner
+            sums_in[0:1, lanes(which, 256)] = col_sum(inner)
+            tot_t[...] += mm_t(inner, w_p[turn, :, part * 256 : part * 256 + 256])
+
+    def image_three():
+        begin(get_textco)
+        begin(get_selfs)
+        finish(get_image)
+        norm_step(tot_i, dz1024, vec128[6:7], dz1024, (AT_BIMAGE, AT_BIFF), sums128, (6, 8, 10))
+        branch = dz1024[:, AT_BIFF : AT_BIFF + 1024]
+        for part in range(4):
+            at = part * 256
+            where = slice(AT_IIN + at, AT_IIN + at + 256)
+            inner = (dz1024[:, where].astype(wide) * mm_t(branch, w_i[0, at : at + 256, :])).astype(narrow)
+            dz1024[:, where] = inner
+            sums128[4:5, at : at + 256] = col_sum(inner)
+            tot_i[...] += mm_t(inner, w_i[1, :, at : at + 256])
+
+    def text_second():
+        finish(get_co)
+        norm_step(sum_t, tot_t, vec96[3:4], dz1024, (0, AT_BTEXT), sums96, (3, 6, 9))
+        mix_t[...] = mm_t(dz1024[:, AT_BTEXT : AT_BTEXT + 768], w_o[...]).astype(narrow)
+
+    def image_second():
+        norm_step(sum_i, tot_i, vec128[5:6], dz1024, (0, AT_BIMAGE), sums128, (5, 7, 9))
+        mix_i[...] = mm_t(dz1024[:, AT_BIMAGE : AT_BIMAGE + 1024], w_i[2]).astype(narrow)
+        begin(get_imageco)
+        finish(get_heads)
+
+    def table_back(table, upper_value):
+        probs = table.astype(wide)
+        return (probs * (upper_value - jnp.sum(upper_value * probs, axis=-1, keepdims=True))).astype(narrow)
+
+    def co_head(head):
+        shrink = 128**-0.5
+        for pair in range(2):
+            rows = slice(pair * 128, pair * 128 + 128)
+            t_at = [pl.ds(pl.multiple_of(AT_TEXTCO + k * 1024 + head * 128, 128), 128) for k in range(3)]
+            i_at = [pl.ds(pl.multiple_of(k * 1024 + head * 128, 128), 128) for k in range(3)]
+            tq, tk, tv = (dz768[rows, at] for at in t_at)
+            iq, ik, iv = (dz1024[rows, at] for at in i_at)
+            for q, k, v, table, mixed, spots in (
+                (tq, ik, iv, tab_t, mix_t, ((dz768, t_at[0]), (dz1024, i_at[1]), (dz1024, i_at[2]))),
+                (iq, tk, tv, tab_i, mix_i, ((dz1024, i_at[0]), (dz768, t_at[1]), (dz768, t_at[2]))),
+            ):
+                probs = table[pair * 8 + head]
+                upper = mixed[rows, lanes(head, 128)]
+                score = table_back(probs, mm_t(upper, v))
+                grads_ = (mm(score, k) * shrink, mm_0(score, q) * shrink, mm_0(probs, upper))
+                for (ref, at), value in zip(spots, grads_):
+                    ref[rows, at] = value.astype(narrow)
+
+    def co_heads(turn):
+        co_head(turn * 2 - 12)
+        co_head(turn * 2 - 11)
+
+    def text_one_back():
+        finish(get_textco)
+        for k in range(3):
+            where = slice(AT_TEXTCO + k * 1024, AT_TEXTCO + (k + 1) * 1024)
+            sum_t[...] += mm_t(dz768[:, where], w_p[k])
+        sums128[0:1, :] = col_sum(dz768[:, AT_TEXTCO : AT_TEXTCO + 1024])
+        sums128[1:2, :] = col_sum(dz768[:, AT_TEXTCO + 2048 : AT_TEXTCO + 3072])
+
+    def self_second():
+        finish(get_self)
+        finish(get_selfs)
+        norm_step(sum_s, sum_t, vec96[2:3], dz768, (0, AT_BSELF), sums96, (2, 5, 8))
+        mix_t[:, 0:768] = mm_t(dz768[:, AT_BSELF : AT_BSELF + 768], w_q[3]).astype(narrow)
+
+    def image_back():
+        finish(get_imageco)
+        for k in range(3):
+            sum_i[...] += mm_t(dz1024[:, k * 1024 : (k + 1) * 1024], w_i[k])
+        sums128[2:3, :] = col_sum(dz1024[:, 0:1024])
+        sums128[3:4, :] = col_sum(dz1024[:, 2048:3072])
+        back_i[...] = sum_i[...].astype(narrow).reshape(2, 128, 1024)
+        begin(swaps[3])
+
+    low, high = head_masks()
+    low_narrow, high_narrow = low.astype(narrow), high.astype(narrow)
+
+    def self_heads(turn):
+        tile = turn - 12
+        for pair in range(2):
+            rows = slice(pair * 128, pair * 128 + 128)
+            at = [pl.ds(pl.multiple_of(k * 768 + tile * 128, 128), 128) for k in range(3)]
+            q2, k2, v2 = (dz768[rows, where] for where in at)
+            upper = mix_t[rows, lanes(tile, 128)]
+            uppers = jnp.concatenate([upper * low_narrow, upper * high_narrow], axis=0)
+            queries = jnp.concatenate([q2 * low_narrow, q2 * high_narrow], axis=0)
+            probs = tab_s[pair * 6 + tile]
+            score = table_back(probs, mm_t(uppers, v2))
+            query = mm(score, k2)
+            dz768[rows, at[0]] = ((query[:128] * low + query[128:] * high) * 0.125).astype(narrow)
+            dz768[rows, at[1]] = (mm_0(score, queries) * 0.125).astype(narrow)
+            dz768[rows, at[2]] = mm_0(probs, uppers).astype(narrow)
+
+    def text_back():
+        for k in range(3):
+            sum_s[...] += mm_t(dz768[:, k * 768 : (k + 1) * 768], w_q[k])
+        sums96[0:1, :] = col_sum(dz768[:, 0:768])
+        sums96[1:2, :] = col_sum(dz768[:, 1536:2304])
+        back_t[...] = sum_s[...].astype(narrow).reshape(2, 128, 768)
+        begin(swaps[2])
+        small_start()
+
+    text_three()
+    finish(get_text_in)
+
+    def turn_body(turn, carry):
+        for stage, lag in stages:
+            index = turn - lag
+
+            @pl.when((index >= 0) & (index < STEPS))
+            def _(stage=stage, index=index):
+                stage(index)
+
+        pl.when(turn < 3)(lambda: text_inner(turn))
+        pl.when(turn == 3)(image_three)
+        pl.when(turn == 4)(text_second)
+        pl.when(turn == 5)(image_second)
+        pl.when((turn >= 6) & (turn < 10))(lambda: co_heads(turn))
+
+        @pl.when(turn == 10)
+        def _():
+            text_one_back()
+            image_back()
+
+        pl.when(turn == 11)(self_second)
+        pl.when((turn >= 12) & (turn < 18))(lambda: self_heads(turn))
+        pl.when(turn == SMALL_TURN)(text_back)
+        for lag, step in (
+            (LAG_NEAR, small_near),
+            (LAG_FAR, small_far),
+            (LAG_SUM, small_sum),
+            (LAG_MID, small_mid),
+            (LAG_END, small_end),
+            (LAG_WRITE, small_write),
+        ):
+            pl.when(turn == SMALL_TURN + lag)(step)
+        return carry
+
+    lax.fori_loop(0, STEPS + LAG_WRITE, turn_body, 0)
+
+    core_copy(STEPS - 2).wait_send()
+    core_copy(STEPS - 1).wait_send()
+    sm_core.wait_send()
+    for copy in sm_near:
+        copy.wait_send()
+    sm_far.wait_send()
+
+    def settle(index, carry):
+        @pl.when(is_end)
+        def _():
+            end_write(index).wait()
+
+        @pl.when(is_mid)
+        def _():
+            mid_copy(index).wait_send()
+            back_copy(index).wait_send()
+            mid_write(index).wait()
+
+        return carry
+
+    lax.fori_loop(0, STEPS, settle, 0)
+
+    @pl.when(is_end)
+    def _():
+        sm_end.wait_send()
+
+    @pl.when(is_mid)
+    def _():
+        sm_mid.wait_send()
+        sm_back.wait_send()
+
+    for group in swaps:
+        finish(group)
+
+
+def backward_all(weights, saved, cots):
+    dma = pltpu.SemaphoreType.DMA
+    shape = jax.ShapeDtypeStruct
+    vmem = pltpu.VMEM
+    narrow, wide = jnp.bfloat16, jnp.float32
+    block = (768, 128)
+    tiny = (SMALL_ROWS, 128)
+    kept = [getattr(saved, name) for name in SAVED]
+    one = [dma((STEPS + 1,))] * 2
+    results = pl.pallas_call(
+        backward_kernel,
+        out_shape=[
+            shape((STEPS,) + block, narrow),
+            shape(tiny, wide),
+            shape((8, 32, 768), narrow),
+            shape((8, 32, 1024), narrow),
+            shape((8, 32, 768), narrow),
+            shape((8, 32, 1024), narrow),
+        ],
+        in_specs=[ANY] * (len(weights) + len(kept) + 2),
+        out_specs=[ANY, VMEM] + [ANY] * 4,
+        scratch_shapes=[
+            vmem((2, 4) + block, narrow),
+            vmem((CHIP_SLOTS, 4) + block, narrow),
+            vmem((NEAR_SLOTS, 2) + block, narrow),
+            vmem((PLANE_SLOTS,) + block, narrow),
+            vmem((STEPS,) + block, narrow),
+            vmem((STEPS,) + block, narrow),
+            vmem((2, 4) + tiny, wide),
+            vmem((4,) + tiny, wide),
+            vmem((2,) + tiny, wide),
+            vmem(tiny, wide),
+            vmem(tiny, wide),
+            vmem(tiny, wide),
+            vmem((3, 768, 1024), narrow),
+            vmem((4, 768, 768), narrow),
+            vmem((3, 1024, 1024), narrow),
+            vmem((1024, 768), narrow),
+            vmem((256, 9216), narrow),
+            vmem((256, 6912), narrow),
+            vmem((256, 768), narrow),
+            vmem((4, 2, 384, 256), narrow),
+            vmem((5, 2, 512, 256), narrow),
+            vmem((1, 2, 1536, 256), narrow),
+            vmem((12, 256, 128), narrow),
+            vmem((16, 128, 128), narrow),
+            vmem((16, 128, 128), narrow),
+            vmem((256, 768), wide),
+            vmem((256, 768), wide),
+            vmem((256, 1024), wide),
+            vmem((256, 768), wide),
+            vmem((256, 1024), wide),
+            vmem((16, 768), wide),
+            vmem((16, 1024), wide),
+            vmem((256, 1024), narrow),
+            vmem((256, 1024), narrow),
+            vmem((2, 128, 768), narrow),
+            vmem((2, 128, 1024), narrow),
+            vmem((16, 768), wide),
+            vmem((16, 1024), wide),
+            vmem((8, 3072), wide),
+        ]
+        + one
+        + [dma((STEPS + 1, 2))] * 2
+        + one * 4
+        + [dma((STEPS,)), dma((4, 3)), dma((4, 3)), dma((4,)), dma((48,))],
+        compiler_params=pltpu.CompilerParams(
+            collective_id=1, has_side_effects=True, vmem_limit_bytes=62 * 2**20
+        ),
+        name="backward_all",
+    )(*weights, *kept, *cots)
+    return (results[0], results[1], results[2:])
+
+
+UNPACK = (
+    ((0, 18, 6), (1, 6, 6), (3, 24, 8), (6, 24, 24)),
+    ((2, 24, 8), (4, 6, 6), (5, 8, 8), (8, 8, 8), (9, 8, 8)),
+    ((7, 6, 6),),
+)
+
+
+def unpack_kernel(*refs):
+    summed, small = refs[:2]
+    states = refs[2:6]
+    weights = refs[6:16]
+    smalls = refs[16 : 16 + SMALL_COUNT]
+    targets = refs[16 + SMALL_COUNT : 20 + SMALL_COUNT]
+    sem = refs[-1]
+    copies = [pltpu.make_async_copy(states[i], targets[i], sem.at[i]) for i in range(4)]
+    for copy in copies:
+        copy.start()
+    places = [{}, {}, {}]
+    turn = 0
+    for kind, start, count in ORDER:
+        for chunk in range(start, start + count):
+            places[kind][chunk] = turn
+            turn += 1
+    for kind in range(3):
+        rows = ROWS[kind]
+        tile = 0
+        for weight, tiles, width in UNPACK[kind]:
+            for own_tile in range(tiles):
+                at, side = divmod(tile, TILES[kind] * 2)
+                values = summed[places[kind][at], side * rows : (side + 1) * rows, :]
+                part, column = divmod(own_tile, width)
+                weights[weight][part, :, column * 128 : column * 128 + 128] = values.astype(jnp.float32)
+                tile += 1
+    for (first, rows, width), ref in zip(SMALL_PLACES, smalls):
+        ref[...] = small[first : first + rows, :width]
+    for copy in copies:
+        copy.wait()
+
+
+def unpack(summed, small, states):
+    shape = jax.ShapeDtypeStruct
+    out_shape = [shape((w[0], w[1] // 8, w[2]), jnp.float32) for w in WEIGHT_SHAPES]
+    out_shape += [shape((rows, width), jnp.float32) for first, rows, width in SMALL_PLACES]
+    out_shape += [shape(s.shape, s.dtype) for s in states]
+    results = pl.pallas_call(
+        unpack_kernel,
+        out_shape=out_shape,
+        in_specs=[VMEM] * 2 + [ANY] * 4,
+        out_specs=[VMEM] * (10 + SMALL_COUNT) + [ANY] * 4,
+        scratch_shapes=[pltpu.SemaphoreType.DMA((4,))],
+        compiler_params=pltpu.CompilerParams(vmem_limit_bytes=40 * 2**20),
+        name="unpack",
+    )(summed, small, *states)
+    return (results[:10], results[10 : 10 + SMALL_COUNT], results[10 + SMALL_COUNT :])
+
+
+def local_fast(
+    text, image, text_len, region_count, text_cot, image_cot,
+    selfproject, selfbiases, selfoutput, textcoproject, textcobiases, imagecoproject, imagecobiases,
+    textcooutput, imagecooutput, textffinner, textffinbias, textffouter,
+    imageffinner, imageffinbias, imageffouter,
+    textgains, textshifts, textbiases, imagegains, imageshifts, imagebiases,
+):
+    blocks = [
+        selfproject.transpose(1, 0, 2), selfoutput[None], imagecoproject.transpose(1, 0, 2),
+        textcoproject.transpose(1, 0, 2), textcooutput[None], imagecooutput[None],
+        textffinner[None], textffouter[None], imageffinner[None], imageffouter[None],
+    ]
+    small = [
+        selfbiases, textcobiases, imagecobiases, textffinbias.reshape(3, 128), imageffinbias.reshape(1, 128),
+        textgains, textshifts, textbiases, imagegains, imageshifts, imagebiases,
+    ]
+    weights, saved, cots = forward_all(blocks, small, [text, image, text_cot, image_cot], text_len, region_count)
+    summed, small_sum, outputs = backward_all(weights, saved, cots)
+    g, s, outputs = unpack(summed, small_sum, outputs)
+    return tuple(outputs) + (
+        g[W_SELF].transpose(1, 0, 2), s[0], g[W_SELFOUT][0], g[W_TEXTCO].transpose(1, 0, 2), s[1],
+        g[W_IMAGECO].transpose(1, 0, 2), s[2], g[W_TEXTOUT][0], g[W_IMAGEOUT][0],
+        g[W_TIN][0], s[3].reshape(-1), g[W_TOUT][0], g[W_IIN][0], s[4].reshape(-1), g[W_IOUT][0],
+        s[5], s[6], s[7], s[8], s[9], s[10],
+    )
+
+
 def solution(mesh):
     in_specs = (
         P("dp", "seq", None),
@@ -550,4 +1818,6 @@
         P(None, "dp"),
         P(None, "dp"),
     )
+    sizes = mesh.shape
+    local = local_fast if (sizes["dp"], sizes["seq"]) == (8, 4) else local_plain
     return jax.shard_map(local, mesh=mesh, in_specs=in_specs, out_specs=out_specs, check_vma=False)

time: 2100 us -> 351 us (0.17)
  waiting for transfers between devices: 1540 us -> 0 us
  Pallas kernels: 0 us -> 343 us
  matrix products: 190 us -> 0 us
  blocking collectives: 129 us -> 0 us
  local copies, waits for them, and re-layouts: 117 us -> 6.95 us
  other arithmetic: 92.4 us -> 0 us
    reduce_scatter x15 -> x0, waiting for transfers between devices: 656 us -> none  [the longest x1 93.8 us: local(): lax.psum_scatter(gradients[5], 'dp', scatter_dimension=0, tiled=True)]
    all_gather x16 -> x0, waiting for transfers between devices: 375 us -> none  [the longest x2 46.2 us: micro_step(): lax.all_gather(text_triple[:, :, 1:], 'seq', axis=1, tiled=True)]
    unnamed x52 -> x0, waiting for transfers between devices: 357 us -> none
    pallas_call x0 -> x3, Pallas kernels: none -> 343 us  [the longest x1 177 us: backward_all(): pl.pallas_call(backward_kernel, out_shape=[shape((STEPS,) + block, narrow...]
    dot_general x96 -> x0, matrix products: 190 us -> none  [the longest x6 38.2 us: project_back(): jnp.einsum('pte,ptkf->ekf', inputs, gradient, preferred_element_type=jnp....]
    psum x1 -> x0, waiting for transfers between devices: 147 us -> none  [local(): lax.psum(accumulated[0].astype(jnp.bfloat16), 'seq').astype(jnp.float32)]
    all_gather x11 -> x0, blocking collectives: 94.4 us -> none  [the longest x1 10.3 us: local(): lax.all_gather(shards[1], 'dp', axis=1, tiled=True)]
    unnamed x682 -> x12, local copies, waits for them, and re-layouts: 67.8 us -> 6.95 us
  transfers between devices with their start and end apart: 42 -> 0, of which waited for: 38 -> 0; matrix products, arithmetic and copies ran while one was open for 16% -> 0% of each run, Pallas kernels for 0% -> 0%
where the time goes in v2:
time: 351 us; the launch traced here: 350 us
  Pallas kernels  343 us (98%)
  local copies, waits for them, and re-layouts  6.95 us (2%)
    pallas_call x1, Pallas kernels, backward_all(): pl.pallas_call(backward_kernel, out_shape=[shape((STEPS,) + block, narrow...  177 us
    pallas_call x1, Pallas kernels, forward_all(): pl.pallas_call(forward_kernel, out_shape=out_shape, in_specs=[ANY] * coun...  161 us

profile of v2, /device:TPU:0, one launch (start us, length us, event | category | flops | bytes accessed | tf_op | source)
XLA Modules:
  0.0 350.3 jit_solution(4237024155354157166)
XLA Ops:
  0.7 161.1 %forward_all.1 = (bf16[3,768,768]{2,1,0:T(8,128)(2,1)}, bf16[1,768,768]{2,1,0:T(8,128)(2,1)}, bf16[3,1024,1024]{2,1,0:T(8,128)(2,1)}, bf16[3,768,1024]{2,1,0:T(8...) custom-call(bf16[3,96,768]{2,1,0:T(8,128)(2,1)} %bitcast.28, ...), custom_call_target="tpu_custom_call" | custom-call | tf_op jit(solution)/shard_map/forward_all/pallas_call | solution.py:998
  161.8 176.8 %backward_all.1 = (bf16[21,768,128]{2,1,0:T(8,128)(2,1)}, f32[32,128]{1,0:T(8,128)}, bf16[8,32,768]{2,1,0:T(8,128)(2,1)}, bf16[8,32,1024]{2,1,0:T(8,128)(2,1)}, ...) custom-call(bf16[3,768,768]{2,1,0:T(8,128)(2,1)} %get-tuple-element.88.refs_0_, ...), custom_call_target="tpu_custom_call" | custom-call | tf_op jit(solution)/shard_map/backward_all/pallas_call | solution.py:1616
  338.7 0.0 copy-start
  338.7 2.2 copy-done
  340.8 0.0 copy-start.1
  340.8 1.0 copy-done.1
  341.9 0.0 copy-start.2
  341.9 1.0 copy-done.2
  342.9 0.0 copy-start.3
  342.9 1.0 copy-done.3
  343.9 0.0 copy-start.4
  343.9 1.0 copy-done.4
  344.9 0.0 copy-start.5
  344.9 0.7 copy-done.5
  345.6 4.5 %unpack.1 = (f32[3,96,768]{2,1,0:T(8,128)}, f32[1,96,768]{2,1,0:T(8,128)}, f32[3,128,1024]{2,1,0:T(8,128)}, f32[3,96,1024]{2,1,0:T(8,128)}, f32[1,128,768]{2,1,0...) custom-call(bf16[21,768,128]{2,1,0:T(8,128)(2,1)S(1)} %copy-done, ...), custom_call_target="tpu_custom_call" | custom-call | tf_op jit(solution)/shard_map/unpack/pallas_call | solution.py:1725
Async XLA Ops:
  338.7 2.2 copy-start
  340.8 1.0 copy-start.1
  341.9 1.0 copy-start.2
  342.9 1.0 copy-start.3
  343.9 1.0 copy-start.4
  344.9 0.7 copy-start.5

commit v3 on v2

--- a/solution.py
+++ b/solution.py
@@ -562,6 +562,21 @@
     (1, 1024, 1024), (1, 768, 3072), (1, 3072, 768), (1, 1024, 1024), (1, 1024, 1024),
 )
 W_SELF, W_SELFOUT, W_IMAGECO, W_TEXTCO, W_TEXTOUT, W_IMAGEOUT, W_TIN, W_TOUT, W_IIN, W_IOUT, W_SMALL = range(11)
+PIECES = (
+    (W_SMALL, 0, 0, 32, 0, 128, 2),
+    *((W_SELF, k, 0, 96, 0, 768, k) for k in range(3)),
+    (W_SELFOUT, 0, 0, 96, 0, 768, 2),
+    *((W_IMAGECO, k, 0, 128, 0, 1024, k) for k in range(3)),
+    *((W_TEXTCO, k, 0, 96, 0, 1024, k) for k in range(3)),
+    (W_TEXTOUT, 0, 0, 128, 0, 768, 2),
+    (W_IMAGEOUT, 0, 0, 128, 0, 1024, 2),
+    *((W_TIN, 0, 0, 96, k * 1024, 1024, k) for k in range(3)),
+    *((W_TOUT, 0, k * 128, 128, 0, 768, k) for k in range(3)),
+    (W_IIN, 0, 0, 128, 0, 1024, 2),
+    (W_IOUT, 0, 0, 128, 0, 1024, 2),
+)
+LAG_ACROSS = 5
+AHEAD = 3
 SAVED = dict(
     qkv_s=((3, 256, 768), jnp.bfloat16),
     qkv_t=((3, 256, 1024), jnp.bfloat16),
@@ -593,6 +608,7 @@
     mix_i=((256, 1024), jnp.bfloat16),
     two_t=((256, 768), jnp.bfloat16),
     two_i=((256, 1024), jnp.bfloat16),
+    active=((256, 3072), jnp.bfloat16),
     bias_in=((8, 3072), jnp.float32),
     pack=((SMALL_ROWS, 128), jnp.float32),
 )
@@ -663,61 +679,156 @@
     pack[...] = jnp.zeros((SMALL_ROWS, 128), wide)
     for (first, rows, width), ref in zip(SMALL_PLACES, small_in):
         pack[first : first + rows, :width] = ref[...].astype(wide)
-    sources = blocks + [pack]
 
     greet([(near, z), (far, z), (sibling, z)] + [(dp, other) for other in others])
 
-    def rows_of(whole, index):
-        depth = whole.shape[1] // 8
-        return whole.at[:, pl.ds(pl.multiple_of(index * depth, 16), depth), :]
-
-    def own(array):
-        source = sources[array]
-        return source if array < weight_count else source.reshape(1, SMALL_ROWS, 128)
-
-    def copy_of(array, lane, source, index, device):
-        return remote(
-            source, rows_of(wholes[array], index), send_sem.at[array, lane], recv_sem.at[array, lane], (device, z)
+    def window(piece, index):
+        array, k, row0, rows, col0, cols, planes = PIECES[piece]
+        depth = wholes[array].shape[1] // 8
+        first = pl.multiple_of(index * depth + row0, 16)
+        return wholes[array].at[k, pl.ds(first, rows), pl.ds(col0, cols)]
+
+    def own(piece):
+        array, k, row0, rows, col0, cols, planes = PIECES[piece]
+        if array == W_SMALL:
+            return pack
+        return blocks[array].at[k, pl.ds(row0, rows), pl.ds(col0, cols)]
+
+    partner = z + 1 - 2 * lax.rem(z, 2)
+    always, fetching = [], {0: [], 1: []}
+
+    def copy_of(piece, send_lane, recv_lane, source, index, device):
+        copy = remote(
+            source, window(piece, index), send_sem.at[piece, send_lane], recv_sem.at[piece, recv_lane], device
         )
-
-    sent = {}
-
-    def send(array, lane, source, index, device):
-        copy = copy_of(array, lane, source, index, device)
-        copy.start()
-        sent[array, lane] = copy
-
-    kept = {}
-
-    def start(array):
-        send(array, 0, own(array), dp, near)
-        send(array, 1, own(array), dp, far)
-        send(array, 2, own(array), dp, sibling)
-        kept[array] = pltpu.make_async_copy(own(array), rows_of(wholes[array], dp), own_sem.at[array])
-        kept[array].start()
-
-    def relay(array):
-        sent[array, 0].wait_recv()
-        arrived = rows_of(wholes[array], near)
-        send(array, 3, arrived, near, far)
-        send(array, 4, arrived, near, sibling)
-        sent[array, 1].wait_recv()
-        send(array, 5, rows_of(wholes[array], far), far, sibling)
-
-    def pass_on(array):
-        sent[array, 3].wait_recv()
-        send(array, 6, rows_of(wholes[array], diagonal), diagonal, sibling)
-
-    outs = []
-
-    def ready(array):
+        return copy
+
+    def siblings(piece, lane, source, index):
+        copy = copy_of(piece, lane, lane, source, index, (sibling, z))
+        always.append(copy)
+        return copy
+
+    def by_plane(piece, fetch, other=None):
+        planes = PIECES[piece][6]
+        if planes == 2:
+            if fetch:
+                fetch()
+            return
+        if fetch:
+            pl.when(lax.rem(z, 2) == planes)(fetch)
+        if other:
+            pl.when(lax.rem(z, 2) != planes)(other)
+
+    def begin(copies):
+        for copy in copies:
+            copy.start()
+
+    def noted(piece, *moves):
+        copies = [copy_of(piece, *move) for move in moves]
+        planes = PIECES[piece][6]
+        (always if planes == 2 else fetching[planes]).extend(copies)
+        return copies
+
+    def across(piece, lane, index):
+        if PIECES[piece][6] == 2:
+            return []
+        return noted(piece, (lane + 7, lane, window(piece, index), index, (dp, partner)))
+
+    def arrived(piece, lane, index):
+        copy_of(piece, lane, lane, window(piece, index), index, (sibling, z)).wait_recv()
+
+    def start(piece):
+        block = own(piece)
+        copies = noted(piece, (0, 0, block, dp, (near, z)), (1, 1, block, dp, (far, z)))
+        by_plane(piece, lambda: begin(copies))
+        siblings(piece, 2, block, dp).start()
+
+    onward = {}
+
+    def relay(piece):
+        block, block_far = window(piece, near), window(piece, far)
+        first = noted(piece, (3, 3, block, near, (far, z))) + across(piece, 0, near)
+        second = across(piece, 1, far)
+        onward[piece] = (
+            siblings(piece, 4, block, near),
+            siblings(piece, 5, block_far, far),
+            siblings(piece, 6, window(piece, diagonal), diagonal),
+        )
+
+        def go():
+            arrived(piece, 0, near)
+            begin(first)
+            onward[piece][0].start()
+            arrived(piece, 1, far)
+            begin(second)
+            onward[piece][1].start()
+
+        by_plane(piece, go)
+
+    def pass_on(piece):
+        third = across(piece, 3, diagonal)
+
+        def go():
+            arrived(piece, 3, diagonal)
+            begin(third)
+            onward[piece][2].start()
+
+        by_plane(piece, go)
+
+    def receive(piece):
+        def go():
+            arrived(piece, 0, near)
+            onward[piece][0].start()
+            arrived(piece, 1, far)
+            onward[piece][1].start()
+
+        by_plane(piece, None, go)
+
+    def receive_last(piece):
+        def go():
+            arrived(piece, 3, diagonal)
+            onward[piece][2].start()
+
+        by_plane(piece, None, go)
+
+    outs, kept, met = [], {}, []
+
+    def ready(piece):
+        array = PIECES[piece][0]
         for lane in (2, 4, 5, 6):
-            sent[array, lane].wait_recv()
-        kept[array].wait()
-        if array < weight_count:
+            arrived(piece, lane, near)
+        if array not in met:
+            kept[array].wait()
+        met.append(array)
+        if array < weight_count and met.count(array) == sum(p[0] == array for p in PIECES):
             copy = pltpu.make_async_copy(wholes[array], whole_out[array], out_sem.at[array])
             copy.start()
             outs.append(copy)
+
+    progress = [0, 0]
+
+    def lag_of(piece):
+        return 2 if PIECES[piece][6] == 2 else LAG_ACROSS
+
+    def tick():
+        turn = progress[1]
+        if turn >= len(PIECES) + LAG_ACROSS:
+            return
+        while progress[0] < min(turn + AHEAD, len(PIECES)):
+            start(progress[0])
+            progress[0] += 1
+        for step, lag in ((relay, 0), (pass_on, 1), (receive, LAG_ACROSS - 2), (receive_last, LAG_ACROSS - 1)):
+            if 0 <= turn - lag < len(PIECES):
+                step(turn - lag)
+        for piece in (turn - LAG_ACROSS, turn - 2):
+            if 0 <= piece < len(PIECES) and lag_of(piece) == turn - piece:
+                ready(piece)
+        progress[1] += 1
+
+    def need(array, k=None):
+        last = max(i + lag_of(i) for i, piece in enumerate(PIECES) if piece[0] == array and k in (None, piece[1]))
+        while progress[1] <= last:
+            tick()
 
     def save(ref):
         spot = [ref is other for other in saved_refs].index(True)
@@ -748,33 +859,21 @@
         made.append(keep)
         return made
 
-    order = (W_SMALL, W_SELF, W_SELFOUT, W_IMAGECO, W_TEXTCO, W_TEXTOUT, W_IMAGEOUT, W_TIN, W_TOUT, W_IIN, W_IOUT)
-    progress = [0, 0, 0, 0]
-
-    def advance(started, relayed, passed, completed):
-        while progress[0] < min(started, len(order)):
-            start(order[progress[0]])
-            progress[0] += 1
-        while progress[1] < min(relayed, len(order)):
-            relay(order[progress[1]])
-            progress[1] += 1
-        while progress[2] < min(passed, len(order)):
-            pass_on(order[progress[2]])
-            progress[2] += 1
-        while progress[3] < min(completed, len(order)):
-            ready(order[progress[3]])
-            progress[3] += 1
-
-    def upto(array):
-        at = order.index(array) + 1
-        advance(at + 3, 0, 0, 0)
-        advance(at + 3, at + 1, at, at)
-
+    for array in range(array_count):
+        depth = wholes[array].shape[1] // 8
+        mine = pl.ds(pl.multiple_of(dp * depth, 16), depth)
+        if array == W_SMALL:
+            keep = pltpu.make_async_copy(pack, wholes[array].at[0, mine], own_sem.at[array])
+        else:
+            keep = pltpu.make_async_copy(blocks[array], wholes[array].at[:, mine], own_sem.at[array])
+        kept[array] = keep
     text_in = swap(0, work.text)
-    advance(2, 0, 0, 0)
+    for piece in range(2):
+        start(piece)
     image_in = swap(1, work.image)
-    advance(4, 0, 0, 0)
-    swaps += swap(2, cots[0]) + swap(3, cots[1])
+    progress[0] = 2
+    for keep in kept.values():
+        keep.start()
 
     vec96, vec128, bias_in = saved.vec96, saved.vec128, work.bias_in
 
@@ -801,6 +900,7 @@
     def project_all(inputs, array, target, biases):
         width = target.shape[2]
         for k in range(3):
+            need(array, k)
 
             def body(tile, carry, k=k):
                 where = lanes(tile, 256)
@@ -832,7 +932,7 @@
         def __getitem__(self, key):
             return self.ref[self.index : self.index + 1, key[1]]
 
-    upto(W_SMALL)
+    need(W_SMALL)
     packed = wholes[W_SMALL]
     for owner in range(8):
         base = owner * SMALL_ROWS
@@ -850,7 +950,6 @@
 
     for copy in text_in:
         copy.wait()
-    upto(W_SELF)
     text = work.text[...].reshape(256, 768)
     qkv_s = saved.qkv_s
     project_all(text, W_SELF, qkv_s, (Row(vec96, 0), Row(vec96, 1)))
@@ -868,11 +967,15 @@
             work.mix_s[rows, where] = (mixed[:128] * low + mixed[128:] * high).astype(narrow)
         return carry
 
-    lax.fori_loop(0, 6, self_heads, 0)
+    tick()
+    lax.fori_loop(0, 3, self_heads, 0)
+    tick()
+    lax.fori_loop(3, 6, self_heads, 0)
+    tick()
     save(saved.tab_s)
     flip(text, 96, saved.xt768, 0, 0)
     flip(work.mix_s[...], 96, saved.xt768, 1, 0)
-    upto(W_SELFOUT)
+    need(W_SELFOUT)
     branch(work.mix_s[...], W_SELFOUT, work.text, Row(vec96, 8), saved.sum_s)
     norm_rows(saved.sum_s, vec96[2:3], vec96[5:6], work.one)
     save(saved.sum_s)
@@ -880,13 +983,11 @@
 
     for copy in image_in:
         copy.wait()
-    upto(W_IMAGECO)
     image = work.image[...].reshape(256, 1024)
     qkv_i, qkv_t = saved.qkv_i, saved.qkv_t
     project_all(image, W_IMAGECO, qkv_i, (Row(vec128, 2), Row(vec128, 3)))
     save(saved.qkv_i)
     flip(image, 128, saved.xt1024, 0, 0)
-    upto(W_TEXTCO)
     project_all(work.one[...], W_TEXTCO, qkv_t, (Row(vec128, 0), Row(vec128, 1)))
     save(saved.qkv_t)
 
@@ -905,18 +1006,21 @@
             work.mix_i[rows, where] = mm(table, tv).astype(narrow)
         return carry
 
-    lax.fori_loop(0, 8, co_heads, 0)
+    swaps += swap(2, cots[0]) + swap(3, cots[1])
+    for head in (0, 2, 4, 6):
+        tick()
+        lax.fori_loop(head, head + 2, co_heads, 0)
     save(saved.tab_t)
     save(saved.tab_i)
     flip(work.mix_t[...], 128, saved.xt1024, 1, 0)
     flip(work.mix_i[...], 128, saved.xt1024, 2, 0)
-    upto(W_TEXTOUT)
+    need(W_TEXTOUT)
     branch(work.mix_t[...], W_TEXTOUT, work.one, Row(vec96, 9), saved.sum_t)
     norm_rows(saved.sum_t, vec96[3:4], vec96[6:7], work.two_t)
     save(saved.sum_t)
     flip(work.two_t[...], 96, saved.xt768, 3, 0)
     save(saved.xt768)
-    upto(W_IMAGEOUT)
+    need(W_IMAGEOUT)
     branch(work.mix_i[...], W_IMAGEOUT, work.image, Row(vec128, 9), saved.sum_i)
     norm_rows(saved.sum_i, vec128[5:6], vec128[7:8], work.two_i)
     save(saved.sum_i)
@@ -927,29 +1031,32 @@
         slope = share + inner * (ROOT_TURN * jnp.exp(-0.5 * inner * inner))
         return ((inner * share).astype(narrow), slope.astype(narrow))
 
-    upto(W_TIN)
-    upto(W_TOUT)
     two_t = work.two_t
     tot_t = saved.tot_t
-    tot_t[...] = two_t[...].astype(wide) + vec96[10:11]
 
     def text_inner(owner, carry):
         where = lanes(owner, 384)
         inner = mm(two_t[...], wholes[W_TIN][0, :, where]) + bias_in[0:1, where]
         active, slope = activate(inner)
         saved.slope_t[:, where] = slope
-        saved.xt3072[0, lax.rem(owner, 2), pl.ds(pl.multiple_of(lax.div(owner, 2) * 384, 384), 384), :] = active.T
-        tot_t[...] += mm(active, wholes[W_TOUT][0, where, :])
+        work.active[:, where] = active
+        place_ = pl.ds(pl.multiple_of(lax.div(owner, 2) * 384, 384), 384)
+        saved.xt3072[0, lax.rem(owner, 2), place_, :] = active.T
         return carry
 
-    lax.fori_loop(0, 8, text_inner, 0)
+    need(W_TIN)
+    for owner in (0, 2, 4, 6):
+        lax.fori_loop(owner, owner + 2, text_inner, 0)
+        tick()
     save(saved.slope_t)
     save(saved.xt3072)
+    need(W_TOUT)
+    branch(work.active[...], W_TOUT, two_t, Row(vec96, 10), tot_t)
     save(saved.tot_t)
     norm_rows(tot_t, vec96[4:5], vec96[7:8], saved.out_t)
     save(saved.out_t)
 
-    upto(W_IIN)
+    need(W_IIN)
     two_i = work.two_i
     tot_i = saved.tot_i
     for part in range(4):
@@ -961,14 +1068,21 @@
         work.mix_i[:, where] = active
     save(saved.slope_i)
     save(saved.xt1024)
-    upto(W_IOUT)
+    need(W_IOUT)
     branch(work.mix_i[...], W_IOUT, two_i, Row(vec128, 10), tot_i)
     save(saved.tot_i)
     norm_rows(tot_i, vec128[6:7], vec128[8:9], saved.out_i)
     save(saved.out_i)
 
-    for copy in sent.values():
+    for copy in always:
         copy.wait_send()
+    for planes in (0, 1):
+
+        @pl.when(lax.rem(z, 2) == planes)
+        def _(planes=planes):
+            for copy in fetching[planes]:
+                copy.wait_send()
+
     for copy in swaps:
         copy.wait()
     for copy in outs:
@@ -987,8 +1101,8 @@
     scratch += [pltpu.VMEM((1, 8 * SMALL_ROWS, 128), jnp.float32)]
     scratch += [pltpu.VMEM(dims, kind) for dims, kind in (*SAVED.values(), *WORK.values())]
     scratch += [
-        dma((count + 1, 7)),
-        dma((count + 1, 7)),
+        dma((len(PIECES), 11)),
+        dma((len(PIECES), 7)),
         dma((4, 3)),
         dma((4, 3)),
         dma((count + 5,)),
@@ -1690,11 +1804,9 @@
     states = refs[2:6]
     weights = refs[6:16]
     smalls = refs[16 : 16 + SMALL_COUNT]
-    targets = refs[16 + SMALL_COUNT : 20 + SMALL_COUNT]
-    sem = refs[-1]
-    copies = [pltpu.make_async_copy(states[i], targets[i], sem.at[i]) for i in range(4)]
-    for copy in copies:
-        copy.start()
+    targets = refs[16 + SMALL_COUNT :]
+    for state, target in zip(states, targets):
+        target[...] = state[...]
     places = [{}, {}, {}]
     turn = 0
     for kind, start, count in ORDER:
@@ -1713,8 +1825,6 @@
                 tile += 1
     for (first, rows, width), ref in zip(SMALL_PLACES, smalls):
         ref[...] = small[first : first + rows, :width]
-    for copy in copies:
-        copy.wait()
 
 
 def unpack(summed, small, states):
@@ -1725,10 +1835,9 @@
     results = pl.pallas_call(
         unpack_kernel,
         out_shape=out_shape,
-        in_specs=[VMEM] * 2 + [ANY] * 4,
-        out_specs=[VMEM] * (10 + SMALL_COUNT) + [ANY] * 4,
-        scratch_shapes=[pltpu.SemaphoreType.DMA((4,))],
-        compiler_params=pltpu.CompilerParams(vmem_limit_bytes=40 * 2**20),
+        in_specs=[VMEM] * 6,
+        out_specs=[VMEM] * (14 + SMALL_COUNT),
+        compiler_params=pltpu.CompilerParams(vmem_limit_bytes=61 * 2**20),
         name="unpack",
     )(summed, small, *states)
     return (results[:10], results[10 : 10 + SMALL_COUNT], results[10 + SMALL_COUNT :])

time: 351 us -> 328 us (0.934)
  Pallas kernels: 343 us -> 327 us
  local copies, waits for them, and re-layouts: 6.95 us -> 0 us
    pallas_call x1, Pallas kernels: 161 us -> 140 us  [forward_all(): pl.pallas_call(forward_kernel, out_shape=out_shape, in_specs=[ANY] * coun...]
    unnamed x12 -> x0, local copies, waits for them, and re-layouts: 6.95 us -> none
    pallas_call x1, Pallas kernels: 177 us -> 181 us  [backward_all(): pl.pallas_call(backward_kernel, out_shape=[shape((STEPS,) + block, narrow...]
where the time goes in v3:
time: 328 us
  Pallas kernels  327 us (100%)
    pallas_call x1, Pallas kernels, backward_all(): pl.pallas_call(backward_kernel, out_shape=[shape((STEPS,) + block, narrow...  181 us
    pallas_call x1, Pallas kernels, forward_all(): pl.pallas_call(forward_kernel, out_shape=out_shape, in_specs=[ANY] * coun...  140 us
    pallas_call x1, Pallas kernels, unpack(): pl.pallas_call(unpack_kernel, out_shape=out_shape, in_specs=[VMEM] * 6, o...  6.67 us

profile of v3, /device:TPU:0, one launch (start us, length us, event | category | flops | bytes accessed | tf_op | source)
XLA Modules:
  0.0 327.9 jit_solution(15343184592676484509)
XLA Ops:
  0.7 139.8 %forward_all.1 = (bf16[3,768,768]{2,1,0:T(8,128)(2,1)}, bf16[1,768,768]{2,1,0:T(8,128)(2,1)}, bf16[3,1024,1024]{2,1,0:T(8,128)(2,1)}, bf16[3,768,1024]{2,1,0:T(8...) custom-call(bf16[3,96,768]{2,1,0:T(8,128)(2,1)} %bitcast.28, ...), custom_call_target="tpu_custom_call" | custom-call | tf_op jit(solution)/shard_map/forward_all/pallas_call | solution.py:1112
  140.4 180.7 %backward_all.1 = (bf16[21,768,128]{2,1,0:T(8,128)(2,1)}, f32[32,128]{1,0:T(8,128)}, bf16[8,32,768]{2,1,0:T(8,128)(2,1)}, bf16[8,32,1024]{2,1,0:T(8,128)(2,1)}, ...) custom-call(bf16[3,768,768]{2,1,0:T(8,128)(2,1)} %get-tuple-element.88.refs_0_, ...), custom_call_target="tpu_custom_call" | custom-call | tf_op jit(solution)/shard_map/backward_all/pallas_call | solution.py:1730
  321.1 6.7 %unpack.1 = (f32[3,96,768]{2,1,0:T(8,128)}, f32[1,96,768]{2,1,0:T(8,128)}, f32[3,128,1024]{2,1,0:T(8,128)}, f32[3,96,1024]{2,1,0:T(8,128)}, f32[1,128,768]{2,1,0...) custom-call(bf16[21,768,128]{2,1,0:T(8,128)(2,1)} %get-tuple-element, ...), custom_call_target="tpu_custom_call" | custom-call | tf_op jit(solution)/shard_map/unpack/pallas_call | solution.py:1835

commit v4 on v3

--- a/solution.py
+++ b/solution.py
@@ -564,18 +564,20 @@
 W_SELF, W_SELFOUT, W_IMAGECO, W_TEXTCO, W_TEXTOUT, W_IMAGEOUT, W_TIN, W_TOUT, W_IIN, W_IOUT, W_SMALL = range(11)
 PIECES = (
     (W_SMALL, 0, 0, 32, 0, 128, 2),
-    *((W_SELF, k, 0, 96, 0, 768, k) for k in range(3)),
-    (W_SELFOUT, 0, 0, 96, 0, 768, 2),
-    *((W_IMAGECO, k, 0, 128, 0, 1024, k) for k in range(3)),
-    *((W_TEXTCO, k, 0, 96, 0, 1024, k) for k in range(3)),
-    (W_TEXTOUT, 0, 0, 128, 0, 768, 2),
-    (W_IMAGEOUT, 0, 0, 128, 0, 1024, 2),
-    *((W_TIN, 0, 0, 96, k * 1024, 1024, k) for k in range(3)),
-    *((W_TOUT, 0, k * 128, 128, 0, 768, k) for k in range(3)),
+    *((W_SELF, k, 0, 96, 0, 768, 2) for k in range(3)),
+    (W_SELFOUT, 0, 0, 96, 0, 768, 0),
+    *((W_IMAGECO, k, 0, 128, 0, 1024, (0, 1, 2)[k]) for k in range(3)),
+    *((W_TEXTCO, k, 0, 96, 0, 1024, (0, 1, 2)[k]) for k in range(3)),
+    (W_TEXTOUT, 0, 0, 128, 0, 768, 0),
+    (W_IMAGEOUT, 0, 0, 128, 0, 1024, 1),
+    (W_TIN, 0, 0, 96, 0, 1152, 0),
+    (W_TIN, 0, 0, 96, 1152, 1152, 1),
+    (W_TIN, 0, 0, 96, 2304, 768, 2),
+    *((W_TOUT, 0, k * 128, 128, 0, 768, 2) for k in range(3)),
     (W_IIN, 0, 0, 128, 0, 1024, 2),
     (W_IOUT, 0, 0, 128, 0, 1024, 2),
 )
-LAG_ACROSS = 5
+LAG_ACROSS = 4
 AHEAD = 3
 SAVED = dict(
     qkv_s=((3, 256, 768), jnp.bfloat16),
@@ -825,8 +827,9 @@
                 ready(piece)
         progress[1] += 1
 
-    def need(array, k=None):
-        last = max(i + lag_of(i) for i, piece in enumerate(PIECES) if piece[0] == array and k in (None, piece[1]))
+    def need(array, count=3):
+        places = [i for i, piece in enumerate(PIECES) if piece[0] == array][:count]
+        last = max(i + lag_of(i) for i in places)
         while progress[1] <= last:
             tick()
 
@@ -900,7 +903,7 @@
     def project_all(inputs, array, target, biases):
         width = target.shape[2]
         for k in range(3):
-            need(array, k)
+            need(array, k + 1)
 
             def body(tile, carry, k=k):
                 where = lanes(tile, 256)
@@ -1006,7 +1009,6 @@
             work.mix_i[rows, where] = mm(table, tv).astype(narrow)
         return carry
 
-    swaps += swap(2, cots[0]) + swap(3, cots[1])
     for head in (0, 2, 4, 6):
         tick()
         lax.fori_loop(head, head + 2, co_heads, 0)
@@ -1044,9 +1046,11 @@
         saved.xt3072[0, lax.rem(owner, 2), place_, :] = active.T
         return carry
 
-    need(W_TIN)
-    for owner in (0, 2, 4, 6):
-        lax.fori_loop(owner, owner + 2, text_inner, 0)
+    for part in range(3):
+        need(W_TIN, part + 1)
+        if part == 1:
+            swaps += swap(2, cots[0]) + swap(3, cots[1])
+        lax.fori_loop(part * 3, min(part * 3 + 3, 8), text_inner, 0)
         tick()
     save(saved.slope_t)
     save(saved.xt3072)
@@ -1134,7 +1138,7 @@
 STARTS = ((9, 12, 24), (12, 15, 19, 23), ())
 ORDER = ((2, 0, 3), (0, 6, 3), (1, 4, 5), (0, 3, 3), (1, 0, 4), (0, 0, 3))
 STEPS = 21
-LAG_NEAR, LAG_FAR, LAG_SUM, LAG_MID, LAG_END, LAG_WRITE = 1, 3, 5, 7, 9, 11
+LAG_NEAR, LAG_FAR, LAG_SUM, LAG_MID, LAG_END, LAG_WRITE = 1, 4, 5, 6, 7, 8
 SMALL_TURN = 18
 CHIP_SLOTS, NEAR_SLOTS, PLANE_SLOTS = 7, 9, 9
 AT_BSELF, AT_TEXTCO, AT_TIN = 2304, 3072, 6144

time: 328 us -> 315 us (0.960)
  Pallas kernels: 327 us -> 314 us
    pallas_call x1, Pallas kernels: 181 us -> 169 us  [backward_all(): pl.pallas_call(backward_kernel, out_shape=[shape((STEPS,) + block, narrow...]
where the time goes in v4:
time: 315 us
  Pallas kernels  314 us (100%)
    pallas_call x1, Pallas kernels, backward_all(): pl.pallas_call(backward_kernel, out_shape=[shape((STEPS,) + block, narrow...  169 us
    pallas_call x1, Pallas kernels, forward_all(): pl.pallas_call(forward_kernel, out_shape=out_shape, in_specs=[ANY] * coun...  138 us
    pallas_call x1, Pallas kernels, unpack(): pl.pallas_call(unpack_kernel, out_shape=out_shape, in_specs=[VMEM] * 6, o...  6.67 us

profile of v4, /device:TPU:0, one launch (start us, length us, event | category | flops | bytes accessed | tf_op | source)
XLA Modules:
  0.0 314.6 jit_solution(18041041424098651032)
XLA Ops:
  0.7 138.3 %forward_all.1 = (bf16[3,768,768]{2,1,0:T(8,128)(2,1)}, bf16[1,768,768]{2,1,0:T(8,128)(2,1)}, bf16[3,1024,1024]{2,1,0:T(8,128)(2,1)}, bf16[3,768,1024]{2,1,0:T(8...) custom-call(bf16[3,96,768]{2,1,0:T(8,128)(2,1)} %bitcast.28, ...), custom_call_target="tpu_custom_call" | custom-call | tf_op jit(solution)/shard_map/forward_all/pallas_call | solution.py:1116
  139.0 168.7 %backward_all.1 = (bf16[21,768,128]{2,1,0:T(8,128)(2,1)}, f32[32,128]{1,0:T(8,128)}, bf16[8,32,768]{2,1,0:T(8,128)(2,1)}, bf16[8,32,1024]{2,1,0:T(8,128)(2,1)}, ...) custom-call(bf16[3,768,768]{2,1,0:T(8,128)(2,1)} %get-tuple-element.88.refs_0_, ...), custom_call_target="tpu_custom_call" | custom-call | tf_op jit(solution)/shard_map/backward_all/pallas_call | solution.py:1734
  307.7 6.7 %unpack.1 = (f32[3,96,768]{2,1,0:T(8,128)}, f32[1,96,768]{2,1,0:T(8,128)}, f32[3,128,1024]{2,1,0:T(8,128)}, f32[3,96,1024]{2,1,0:T(8,128)}, f32[1,128,768]{2,1,0...) custom-call(bf16[21,768,128]{2,1,0:T(8,128)(2,1)} %get-tuple-element, ...), custom_call_target="tpu_custom_call" | custom-call | tf_op jit(solution)/shard_map/unpack/pallas_call | solution.py:1839

commit v5 on v4

--- a/solution.py
+++ b/solution.py
@@ -816,10 +816,12 @@
         turn = progress[1]
         if turn >= len(PIECES) + LAG_ACROSS:
             return
+        if turn < len(PIECES):
+            relay(turn)
         while progress[0] < min(turn + AHEAD, len(PIECES)):
             start(progress[0])
             progress[0] += 1
-        for step, lag in ((relay, 0), (pass_on, 1), (receive, LAG_ACROSS - 2), (receive_last, LAG_ACROSS - 1)):
+        for step, lag in ((pass_on, 1), (receive, LAG_ACROSS - 2), (receive_last, LAG_ACROSS - 1)):
             if 0 <= turn - lag < len(PIECES):
                 step(turn - lag)
         for piece in (turn - LAG_ACROSS, turn - 2):
@@ -875,6 +877,9 @@
         start(piece)
     image_in = swap(1, work.image)
     progress[0] = 2
+    while progress[0] < AHEAD:
+        start(progress[0])
+        progress[0] += 1
     for keep in kept.values():
         keep.start()
 
@@ -1138,9 +1143,9 @@
 STARTS = ((9, 12, 24), (12, 15, 19, 23), ())
 ORDER = ((2, 0, 3), (0, 6, 3), (1, 4, 5), (0, 3, 3), (1, 0, 4), (0, 0, 3))
 STEPS = 21
-LAG_NEAR, LAG_FAR, LAG_SUM, LAG_MID, LAG_END, LAG_WRITE = 1, 4, 5, 6, 7, 8
+LAG_NEAR, LAG_FAR, LAG_SUM, LAG_MID, LAG_END, LAG_WRITE = 1, 5, 6, 7, 8, 9
 SMALL_TURN = 18
-CHIP_SLOTS, NEAR_SLOTS, PLANE_SLOTS = 7, 9, 9
+CHIP_SLOTS, NEAR_SLOTS, PLANE_SLOTS = 8, 11, 9
 AT_BSELF, AT_TEXTCO, AT_TIN = 2304, 3072, 6144
 AT_BTEXT, AT_BIMAGE, AT_IIN, AT_BIFF = 3072, 3840, 4864, 5888
 
@@ -1212,10 +1217,10 @@
         (saved.tot_t, tot_t),
         (cot_t.reshape(256, 768), span(dz768, AT_BSELF, 768)),
         (saved.vec96, vec96),
+        (saved.xt3072, xt[2]),
+    )
+    get_text_in = load(
         *((weights[W_TOUT].at[0, pl.ds(i * 768, 768), :], w_q.at[i]) for i in range(4)),
-    )
-    get_text_in = load(
-        (saved.xt3072, xt[2]),
         (saved.xt768, xt[0]),
         (saved.slope_t, span(dz768, AT_TIN, 3072)),
         *((weights[W_TIN].at[0, :, pl.ds(i * 1024, 1024)], w_p.at[i]) for i in range(3)),
@@ -1249,8 +1254,8 @@
     get_textco = load((weights[W_TEXTCO], w_p))
     get_selfs = load((weights[W_SELF], w_q.at[pl.ds(0, 3)]), (weights[W_SELFOUT].at[0], w_q.at[3]))
     get_imageco = load((weights[W_IMAGECO], w_i))
-    for group in (get_text3, get_text_in, get_image, get_co, get_heads, get_self):
-        begin(group)
+    begin(get_text3)
+    begin(get_text_in)
     sums96[...] = jnp.zeros((16, 768), wide)
     sums128[...] = jnp.zeros((16, 1024), wide)
     s_own[...] = jnp.zeros((2, 4, SMALL_ROWS, 128), wide)
@@ -1650,7 +1655,8 @@
         small_start()
 
     text_three()
-    finish(get_text_in)
+    for group in (get_image, get_co, get_heads, get_self):
+        begin(group)
 
     def turn_body(turn, carry):
         for stage, lag in stages:
@@ -1660,6 +1666,7 @@
             def _(stage=stage, index=index):
                 stage(index)
 
+        pl.when(turn == 0)(lambda: finish(get_text_in))
         pl.when(turn < 3)(lambda: text_inner(turn))
         pl.when(turn == 3)(image_three)
         pl.when(turn == 4)(text_second)

time: 315 us -> 311 us (0.987)
  Pallas kernels: 314 us -> 310 us
    pallas_call x1, Pallas kernels: 138 us -> 135 us  [forward_all(): pl.pallas_call(forward_kernel, out_shape=out_shape, in_specs=[ANY] * coun...]
where the time goes in v5:
time: 311 us
  Pallas kernels  310 us (100%)
    pallas_call x1, Pallas kernels, backward_all(): pl.pallas_call(backward_kernel, out_shape=[shape((STEPS,) + block, narrow...  168 us
    pallas_call x1, Pallas kernels, forward_all(): pl.pallas_call(forward_kernel, out_shape=out_shape, in_specs=[ANY] * coun...  135 us
    pallas_call x1, Pallas kernels, unpack(): pl.pallas_call(unpack_kernel, out_shape=out_shape, in_specs=[VMEM] * 6, o...  6.67 us

profile of v5, /device:TPU:0, one launch (start us, length us, event | category | flops | bytes accessed | tf_op | source)
XLA Modules:
  0.0 310.7 jit_solution(4007881253632811299)
XLA Ops:
  0.7 135.1 %forward_all.1 = (bf16[3,768,768]{2,1,0:T(8,128)(2,1)}, bf16[1,768,768]{2,1,0:T(8,128)(2,1)}, bf16[3,1024,1024]{2,1,0:T(8,128)(2,1)}, bf16[3,768,1024]{2,1,0:T(8...) custom-call(bf16[3,96,768]{2,1,0:T(8,128)(2,1)} %bitcast.28, ...), custom_call_target="tpu_custom_call" | custom-call | tf_op jit(solution)/shard_map/forward_all/pallas_call | solution.py:1121
  135.8 168.1 %backward_all.1 = (bf16[21,768,128]{2,1,0:T(8,128)(2,1)}, f32[32,128]{1,0:T(8,128)}, bf16[8,32,768]{2,1,0:T(8,128)(2,1)}, bf16[8,32,1024]{2,1,0:T(8,128)(2,1)}, ...) custom-call(bf16[3,768,768]{2,1,0:T(8,128)(2,1)} %get-tuple-element.88.refs_0_, ...), custom_call_target="tpu_custom_call" | custom-call | tf_op jit(solution)/shard_map/backward_all/pallas_call | solution.py:1741
  303.9 6.7 %unpack.1 = (f32[3,96,768]{2,1,0:T(8,128)}, f32[1,96,768]{2,1,0:T(8,128)}, f32[3,128,1024]{2,1,0:T(8,128)}, f32[3,96,1024]{2,1,0:T(8,128)}, f32[1,128,768]{2,1,0...) custom-call(bf16[21,768,128]{2,1,0:T(8,128)(2,1)} %get-tuple-element, ...), custom_call_target="tpu_custom_call" | custom-call | tf_op jit(solution)/shard_map/unpack/pallas_call | solution.py:1846

commit v6 on v5

--- a/solution.py
+++ b/solution.py
@@ -577,7 +577,7 @@
     (W_IIN, 0, 0, 128, 0, 1024, 2),
     (W_IOUT, 0, 0, 128, 0, 1024, 2),
 )
-LAG_ACROSS = 4
+LAG_ACROSS = 5
 AHEAD = 3
 SAVED = dict(
     qkv_s=((3, 256, 768), jnp.bfloat16),

time: 311 us -> 310 us (level)
    pallas_call x1, Pallas kernels: 135 us -> 131 us  [forward_all(): pl.pallas_call(forward_kernel, out_shape=out_shape, in_specs=[ANY] * coun...]
where the time goes in v6:
time: 310 us; the launch traced here: 309 us
  Pallas kernels  309 us (100%)
    pallas_call x1, Pallas kernels, backward_all(): pl.pallas_call(backward_kernel, out_shape=[shape((STEPS,) + block, narrow...  171 us
    pallas_call x1, Pallas kernels, forward_all(): pl.pallas_call(forward_kernel, out_shape=out_shape, in_specs=[ANY] * coun...  131 us
    pallas_call x1, Pallas kernels, unpack(): pl.pallas_call(unpack_kernel, out_shape=out_shape, in_specs=[VMEM] * 6, o...  6.67 us

profile of v6, /device:TPU:0, one launch (start us, length us, event | category | flops | bytes accessed | tf_op | source)
XLA Modules:
  0.0 309.4 jit_solution(11904042396168409434)
XLA Ops:
  0.7 130.8 %forward_all.1 = (bf16[3,768,768]{2,1,0:T(8,128)(2,1)}, bf16[1,768,768]{2,1,0:T(8,128)(2,1)}, bf16[3,1024,1024]{2,1,0:T(8,128)(2,1)}, bf16[3,768,1024]{2,1,0:T(8...) custom-call(bf16[3,96,768]{2,1,0:T(8,128)(2,1)} %bitcast.28, ...), custom_call_target="tpu_custom_call" | custom-call | tf_op jit(solution)/shard_map/forward_all/pallas_call | solution.py:1121
  131.5 171.1 %backward_all.1 = (bf16[21,768,128]{2,1,0:T(8,128)(2,1)}, f32[32,128]{1,0:T(8,128)}, bf16[8,32,768]{2,1,0:T(8,128)(2,1)}, bf16[8,32,1024]{2,1,0:T(8,128)(2,1)}, ...) custom-call(bf16[3,768,768]{2,1,0:T(8,128)(2,1)} %get-tuple-element.88.refs_0_, ...), custom_call_target="tpu_custom_call" | custom-call | tf_op jit(solution)/shard_map/backward_all/pallas_call | solution.py:1741
  302.6 6.7 %unpack.1 = (f32[3,96,768]{2,1,0:T(8,128)}, f32[1,96,768]{2,1,0:T(8,128)}, f32[3,128,1024]{2,1,0:T(8,128)}, f32[3,96,1024]{2,1,0:T(8,128)}, f32[1,128,768]{2,1,0...) custom-call(bf16[21,768,128]{2,1,0:T(8,128)(2,1)} %get-tuple-element, ...), custom_call_target="tpu_custom_call" | custom-call | tf_op jit(solution)/shard_map/unpack/pallas_call | solution.py:1846
